TPU v7x, 32 devices: a whole 2x2x4 slice. The times are simulated.
32 devices in a mesh: head: 2 (over x), blk: 16 (over z, y, core).
Axes of the slice: x: 2, y: 2, z: 4, core: 2. Of those that a mesh axis runs over, the one named last changes fastest.
Arguments:
- inputs: bfloat16 [4096, 2048], P(('head', 'blk')), may hold values from -6 to 6
- attn_norm_gain: bfloat16 [2048], P(('head', 'blk')), may hold values from 0.5 to 1.5
- attn_norm_bias: bfloat16 [2048], P(('head', 'blk')), may hold values from -1.25 to 1.25
- mlp_norm_gain: bfloat16 [2048], P(('head', 'blk')), may hold values from 0.5 to 1.5
- mlp_norm_bias: bfloat16 [2048], P(('head', 'blk')), may hold values from -1.25 to 1.25
- qkv_weight: bfloat16 [2048, 6144], P(('head', 'blk')), may hold values from -0.125 to 0.125
- qkv_bias: bfloat16 [6144], P(('head', 'blk')), may hold values from -1.25 to 1.25
- dense_weight: bfloat16 [2048, 2048], P(('head', 'blk')), may hold values from -2 to 2
- dense_bias: bfloat16 [2048], P(('head', 'blk')), may hold values from -1.25 to 1.25
- expand_weight: bfloat16 [2048, 8192], P(('head', 'blk')), may hold values from -0.125 to 0.125
- expand_bias: bfloat16 [8192], P(('head', 'blk')), may hold values from -1.25 to 1.25
- shrink_weight: bfloat16 [2048, 8192], P(('head', 'blk')), may hold values from -0.0625 to 0.0625
- shrink_bias: bfloat16 [2048], P(('head', 'blk')), may hold values from -1.25 to 1.25
- token_of_row: int32 [4096], replicated, may hold values from 0 to 4095, as said below
- cont_parent: int32 [8], replicated, may hold values from 0 to 0, as said below
- position_ids: int32 [4096], P(('head', 'blk')), may hold values from 0 to 2815, as said below
- cotangent: bfloat16 [4096, 2048], P(('head', 'blk')), may hold values from -12 to 12
Outputs:
- output: bfloat16 [4096, 2048], P(('head', 'blk'))
- input_grad: bfloat16 [4096, 2048], P(('head', 'blk'))
- attn_norm_gain_grad: float32 [2048], P(('head', 'blk'))
- attn_norm_bias_grad: float32 [2048], P(('head', 'blk'))
- mlp_norm_gain_grad: float32 [2048], P(('head', 'blk'))
- mlp_norm_bias_grad: float32 [2048], P(('head', 'blk'))
- qkv_weight_grad: float32 [2048, 6144], P(('head', 'blk'))
- qkv_bias_grad: float32 [4096], P(('head', 'blk'))
- value_bias_grad: float32 [2048], P(('head', 'blk'))
- dense_weight_grad: float32 [2048, 2048], P(('head', 'blk'))
- dense_bias_grad: float32 [2048], P(('head', 'blk'))
- expand_weight_grad: float32 [2048, 8192], P(('head', 'blk'))
- expand_bias_grad: float32 [8192], P(('head', 'blk'))
- shrink_weight_grad: float32 [2048, 8192], P(('head', 'blk'))
- shrink_bias_grad: float32 [2048], P(('head', 'blk'))
Inputs may be any that keep to these rules, and one draw needn't show every extreme that they name: `token_of_row`: a permutation of the logical tokens; each aligned stripe of 16 logical tokens lies whole on one device, and each aligned run of 32 stripes puts one stripe on every device. `cont_parent`: each prompt is named by exactly 8 continuations. `position_ids`: a prompt token's position is its place in the prompt; the tokens of a continuation take 2048 + its gap + their place, with one gap of 0 to 512 for each continuation.
All inputs are finite; a program needn't handle non-finite values.
Results may differ from a plain program's by a relative error of at most 0.013.
Values may be sent and summed in bfloat16 or wider, within the bound.
A program may use at most 704 MiB of HBM per device.

v0:
```python
import math

import jax
import jax.numpy as jnp
from jax import lax
from jax.sharding import PartitionSpec as P

D = 2048
HEADS = 8
HEAD_DIM = 256
ROT = 64
PROMPT = 2048
CONT = 256


def layer_norm(values, gain, shift):
    average = jnp.mean(values, -1, keepdims=True)
    centered = values - average
    spread = jnp.mean(centered * centered, -1, keepdims=True)
    return centered * lax.rsqrt(spread + 1e-05) * gain + shift


def exact_gelu(values):
    return jax.nn.gelu(values, approximate=False)


def angles_of(positions):
    frequency = 10000.0 ** (-jnp.arange(0, ROT, 2, dtype=jnp.float32) / ROT)
    return positions.astype(jnp.float32)[:, None] * frequency[None, :]


def rotate(values, angles):
    half_rot = ROT // 2
    cosine = jnp.cos(angles)[:, None, :]
    sine_part = jnp.sin(angles)[:, None, :]
    leading = values[..., :half_rot]
    behind = values[..., half_rot:ROT]
    return jnp.concatenate(
        [
            leading * cosine - behind * sine_part,
            behind * cosine + leading * sine_part,
            values[..., ROT:],
        ],
        -1,
    )


def token_meta(token_ids, cont_parent, prompt_total):
    is_prompt = token_ids < prompt_total
    offset = token_ids - prompt_total
    cont_id = jnp.where(is_prompt, -1, offset // CONT)
    position = jnp.where(is_prompt, token_ids % PROMPT, offset % CONT)
    matches = cont_id[:, None] == jnp.arange(cont_parent.shape[0], dtype=jnp.int32)[None, :]
    prompt_id = jnp.where(
        is_prompt, token_ids // PROMPT, jnp.sum(jnp.where(matches, cont_parent[None, :], 0), 1)
    )
    return (prompt_id, cont_id, position, is_prompt)


def allowed_pairs(query_meta, key_meta):
    same_prompt = query_meta[0][:, None] == key_meta[0][None, :]
    same_cont = query_meta[1][:, None] == key_meta[1][None, :]
    earlier = key_meta[2][None, :] <= query_meta[2][:, None]
    from_prompt = key_meta[3][None, :] & (jnp.logical_not(query_meta[3])[:, None] | earlier)
    return same_prompt & (from_prompt | same_cont & earlier)


def gathered_rows(first_row, row_count, tok_dev, head_count, block_count):
    gathered = first_row + jnp.arange(row_count, dtype=jnp.int32)
    pair_size = head_count * tok_dev
    block_index = gathered // pair_size
    within = gathered % pair_size
    head_index = within // tok_dev
    return (head_index * block_count + block_index) * tok_dev + within % tok_dev


def block_width():
    return 512


def per_device(
    inputs,
    attn_norm_gain,
    attn_norm_bias,
    mlp_norm_gain,
    mlp_norm_bias,
    qkv_weight,
    qkv_bias,
    dense_weight,
    dense_bias,
    expand_weight,
    expand_bias,
    shrink_weight,
    shrink_bias,
    token_of_row,
    cont_parent,
    position_ids,
    cotangent,
):
    head_count = lax.axis_size("head")
    block_count = lax.axis_size("blk")
    tok_dev = inputs.shape[0]
    pair_rows = head_count * tok_dev
    local_heads = HEADS // head_count
    score_scale = 1.0 / math.sqrt(HEAD_DIM)
    prompt_total = token_of_row.shape[0] - cont_parent.shape[0] * CONT
    contract_rows = (((1,), (1,)), ((), ()))
    contract_tokens = (((0,), (0,)), ((), ()))
    gathered = (
        lax.all_gather(qkv_weight, ("head", "blk"), axis=0, tiled=True),
        lax.all_gather(expand_weight, ("head", "blk"), axis=0, tiled=True),
        lax.all_gather(dense_weight, ("head", "blk"), axis=0, tiled=True),
        lax.all_gather(shrink_weight, ("head", "blk"), axis=0, tiled=True),
        lax.all_gather(attn_norm_gain, ("head", "blk"), axis=0, tiled=True),
        lax.all_gather(attn_norm_bias, ("head", "blk"), axis=0, tiled=True),
        lax.all_gather(mlp_norm_gain, ("head", "blk"), axis=0, tiled=True),
        lax.all_gather(mlp_norm_bias, ("head", "blk"), axis=0, tiled=True),
        lax.all_gather(qkv_bias, ("head", "blk"), axis=0, tiled=True),
        lax.all_gather(dense_bias, ("head", "blk"), axis=0, tiled=True),
        lax.all_gather(expand_bias, ("head", "blk"), axis=0, tiled=True),
        lax.all_gather(shrink_bias, ("head", "blk"), axis=0, tiled=True),
    )
    whole_qkv, whole_expand, whole_dense, whole_shrink = (
        gathered[0],
        gathered[1],
        gathered[2],
        gathered[3],
    )
    small_params = [param_item.astype(jnp.float32) for param_item in gathered[4:]]
    gain_one, shift_one, gain_two, shift_two, bias_qkv, bias_dense, bias_expand, bias_shrink = (
        small_params
    )
    states = inputs.astype(jnp.float32)
    norm_one, norm_one_back = jax.vjp(layer_norm, states, gain_one, shift_one)
    norm_two, norm_two_back = jax.vjp(layer_norm, states, gain_two, shift_two)
    norm_one_low = norm_one.astype(jnp.bfloat16)
    norm_two_low = norm_two.astype(jnp.bfloat16)
    mixed = jnp.dot(norm_one_low, whole_qkv, preferred_element_type=jnp.float32) + bias_qkv
    split_heads = mixed.reshape(tok_dev, 3, HEADS, HEAD_DIM)
    angles = angles_of(position_ids)
    rotated = jnp.stack(
        [rotate(split_heads[:, 0], angles), rotate(split_heads[:, 1], angles), split_heads[:, 2]], 1
    )
    outgoing = rotated.astype(jnp.bfloat16).reshape(tok_dev, 3, head_count, local_heads * HEAD_DIM)
    incoming = lax.all_to_all(outgoing, "head", split_axis=2, concat_axis=0, tiled=True)
    shaped = incoming.reshape(pair_rows, 3, local_heads, HEAD_DIM)
    queries = shaped[:, 0]
    keys_own = shaped[:, 1]
    values_own = shaped[:, 2]
    expanded = jnp.dot(norm_two_low, whole_expand, preferred_element_type=jnp.float32) + bias_expand
    activated, gelu_back = jax.vjp(exact_gelu, expanded)
    activated_low = activated.astype(jnp.bfloat16)
    own_block = lax.axis_index("blk")
    query_meta = token_meta(
        jnp.take(
            token_of_row,
            gathered_rows(own_block * pair_rows, pair_rows, tok_dev, head_count, block_count),
        ),
        cont_parent,
        prompt_total,
    )

    def meta_blocks(first_row, row_count, key_width):
        meta = token_meta(
            jnp.take(
                token_of_row, gathered_rows(first_row, row_count, tok_dev, head_count, block_count)
            ),
            cont_parent,
            prompt_total,
        )
        return tuple((meta_item.reshape(row_count // key_width, key_width) for meta_item in meta))

    def absorb(running, block_in):
        row_peak, row_total, weighted = running
        keys_now, values_now, key_meta = block_in
        allowed = allowed_pairs(query_meta, key_meta)[None]
        scores = (
            jnp.einsum("qhd,khd->hqk", queries, keys_now, preferred_element_type=jnp.float32)
            * score_scale
        )
        scores = jnp.where(allowed, scores, -1e30)
        new_peak = jnp.maximum(row_peak, jnp.max(scores, -1))
        weights = jnp.where(allowed, jnp.exp(scores - new_peak[..., None]), 0.0)
        factor = jnp.exp(row_peak - new_peak)
        row_total = row_total * factor + jnp.sum(weights, -1)
        weighted = weighted * factor.T[:, :, None] + jnp.einsum(
            "hqk,khd->qhd",
            weights.astype(jnp.bfloat16),
            values_now,
            preferred_element_type=jnp.float32,
        )
        return ((new_peak, row_total, weighted), None)

    start_state = (
        jnp.full((local_heads, pair_rows), -1e30, jnp.float32),
        jnp.zeros((local_heads, pair_rows), jnp.float32),
        jnp.zeros((pair_rows, local_heads, HEAD_DIM), jnp.float32),
    )
    running = start_state
    pieces = (
        lax.all_gather(keys_own, "blk", axis=0, tiled=True),
        lax.all_gather(values_own, "blk", axis=0, tiled=True),
    )
    row_count = pieces[0].shape[0]
    key_width = block_width()
    rounds = row_count // key_width
    blocks = (
        pieces[0].reshape(rounds, key_width, local_heads, HEAD_DIM),
        pieces[1].reshape(rounds, key_width, local_heads, HEAD_DIM),
        meta_blocks(jnp.int32(0), row_count, key_width),
    )
    running, unused = lax.scan(absorb, running, blocks)
    row_peak, row_total, weighted = running
    attention = weighted / row_total.T[:, :, None]
    log_total = row_peak + jnp.log(row_total)
    sent_out = attention.astype(jnp.bfloat16).reshape(pair_rows, 1, local_heads * HEAD_DIM)
    attended = lax.all_to_all(sent_out, "head", split_axis=0, concat_axis=1, tiled=True).reshape(
        tok_dev, D
    )
    branch_one = lax.dot_general(
        attended, whole_dense, contract_rows, preferred_element_type=jnp.float32
    )
    branch_two = lax.dot_general(
        activated_low, whole_shrink, contract_rows, preferred_element_type=jnp.float32
    )
    output = (states + branch_one + bias_dense + branch_two + bias_shrink).astype(jnp.bfloat16)
    back_qkv, back_expand, back_dense, back_shrink = (
        lax.all_gather(qkv_weight, ("head", "blk"), axis=0, tiled=True),
        lax.all_gather(expand_weight, ("head", "blk"), axis=0, tiled=True),
        lax.all_gather(dense_weight, ("head", "blk"), axis=0, tiled=True),
        lax.all_gather(shrink_weight, ("head", "blk"), axis=0, tiled=True),
    )
    grad_out = cotangent.astype(jnp.float32)
    d_attended = jnp.dot(cotangent, back_dense, preferred_element_type=jnp.float32).astype(
        jnp.bfloat16
    )
    d_activated = jnp.dot(cotangent, back_shrink, preferred_element_type=jnp.float32)
    d_expanded = gelu_back(d_activated)[0].astype(jnp.bfloat16)
    part_dense = lax.dot_general(
        cotangent, attended, contract_tokens, preferred_element_type=jnp.float32
    )
    part_shrink = lax.dot_general(
        cotangent, activated_low, contract_tokens, preferred_element_type=jnp.float32
    )
    out_grads = lax.psum_scatter(
        jnp.concatenate([part_dense, part_shrink], 1),
        ("head", "blk"),
        scatter_dimension=0,
        tiled=True,
    )
    grad_heads = lax.all_to_all(
        d_attended.reshape(tok_dev, head_count, local_heads * HEAD_DIM),
        "head",
        split_axis=1,
        concat_axis=0,
        tiled=True,
    ).reshape(pair_rows, local_heads, HEAD_DIM)
    row_delta = jnp.sum(grad_heads.astype(jnp.float32) * attention, -1).T
    all_log_total, all_delta = (
        lax.all_gather(log_total, "blk", axis=1, tiled=True),
        lax.all_gather(row_delta, "blk", axis=1, tiled=True),
    )

    def query_step(running, block_in):
        keys_now, values_now, key_meta = block_in
        allowed = allowed_pairs(query_meta, key_meta)[None]
        scores = (
            jnp.einsum("qhd,khd->hqk", queries, keys_now, preferred_element_type=jnp.float32)
            * score_scale
        )
        probability = jnp.where(allowed, jnp.exp(scores - log_total[..., None]), 0.0)
        dprobs = jnp.einsum(
            "qhd,khd->hqk", grad_heads, values_now, preferred_element_type=jnp.float32
        )
        dscores = (probability * (dprobs - row_delta[..., None])).astype(jnp.bfloat16)
        return (
            running
            + jnp.einsum("hqk,khd->qhd", dscores, keys_now, preferred_element_type=jnp.float32)
            * score_scale,
            None,
        )

    zero_grads = jnp.zeros((pair_rows, local_heads, HEAD_DIM), jnp.float32)
    running = zero_grads
    pieces = (
        lax.all_gather(keys_own, "blk", axis=0, tiled=True),
        lax.all_gather(values_own, "blk", axis=0, tiled=True),
    )
    row_count = pieces[0].shape[0]
    key_width = block_width()
    rounds = row_count // key_width
    blocks = (
        pieces[0].reshape(rounds, key_width, local_heads, HEAD_DIM),
        pieces[1].reshape(rounds, key_width, local_heads, HEAD_DIM),
        meta_blocks(jnp.int32(0), row_count, key_width),
    )
    running, unused = lax.scan(query_step, running, blocks)
    grad_queries = running

    def key_step(running, block_in):
        grad_keys, grad_values = running
        queries_now, grads_now, stat_total, stat_delta, remote_meta = block_in
        allowed = allowed_pairs(remote_meta, query_meta)[None]
        scores = (
            jnp.einsum("qhd,khd->hqk", queries_now, keys_own, preferred_element_type=jnp.float32)
            * score_scale
        )
        probability = jnp.where(allowed, jnp.exp(scores - stat_total[..., None]), 0.0)
        dprobs = jnp.einsum(
            "qhd,khd->hqk", grads_now, values_own, preferred_element_type=jnp.float32
        )
        dscores = (probability * (dprobs - stat_delta[..., None])).astype(jnp.bfloat16)
        grad_keys = (
            grad_keys
            + jnp.einsum("hqk,qhd->khd", dscores, queries_now, preferred_element_type=jnp.float32)
            * score_scale
        )
        grad_values = grad_values + jnp.einsum(
            "hqk,qhd->khd",
            probability.astype(jnp.bfloat16),
            grads_now,
            preferred_element_type=jnp.float32,
        )
        return ((grad_keys, grad_values), None)

    running = (zero_grads, zero_grads)
    pieces = (
        lax.all_gather(queries, "blk", axis=0, tiled=True),
        lax.all_gather(grad_heads, "blk", axis=0, tiled=True),
    )
    row_count = pieces[0].shape[0]
    key_width = block_width()
    rounds = row_count // key_width
    stat_total = all_log_total
    stat_delta = all_delta
    blocks = (
        pieces[0].reshape(rounds, key_width, local_heads, HEAD_DIM),
        pieces[1].reshape(rounds, key_width, local_heads, HEAD_DIM),
        stat_total.reshape(local_heads, rounds, key_width).transpose(1, 0, 2),
        stat_delta.reshape(local_heads, rounds, key_width).transpose(1, 0, 2),
        meta_blocks(jnp.int32(0), row_count, key_width),
    )
    running, unused = lax.scan(key_step, running, blocks)
    grad_keys, grad_values = running
    sent_grads = (
        jnp.stack([grad_queries, grad_keys, grad_values], 1)
        .astype(jnp.bfloat16)
        .reshape(pair_rows, 3, 1, local_heads * HEAD_DIM)
    )
    back_mixed = (
        lax.all_to_all(sent_grads, "head", split_axis=0, concat_axis=2, tiled=True)
        .reshape(tok_dev, 3, HEADS, HEAD_DIM)
        .astype(jnp.float32)
    )
    d_mixed = jnp.stack(
        [rotate(back_mixed[:, 0], -angles), rotate(back_mixed[:, 1], -angles), back_mixed[:, 2]], 1
    )
    d_mixed = d_mixed.reshape(tok_dev, 3 * D).astype(jnp.bfloat16)
    part_qkv = lax.dot_general(
        norm_one_low, d_mixed, contract_tokens, preferred_element_type=jnp.float32
    )
    part_expand = lax.dot_general(
        norm_two_low, d_expanded, contract_tokens, preferred_element_type=jnp.float32
    )
    in_grads = lax.psum_scatter(
        jnp.concatenate([part_qkv, part_expand], 1),
        ("head", "blk"),
        scatter_dimension=0,
        tiled=True,
    )
    qkv_grad = in_grads[:, : 3 * D]
    expand_grad = in_grads[:, 3 * D :]
    dense_grad = out_grads[:, :D]
    shrink_grad = out_grads[:, D:]
    d_norm_one = lax.dot_general(
        d_mixed, back_qkv, contract_rows, preferred_element_type=jnp.float32
    )
    d_norm_two = lax.dot_general(
        d_expanded, back_expand, contract_rows, preferred_element_type=jnp.float32
    )
    input_one, gain_one_grad, shift_one_grad = norm_one_back(d_norm_one)
    input_two, gain_two_grad, shift_two_grad = norm_two_back(d_norm_two)
    input_grad = (grad_out + input_one + input_two).astype(jnp.bfloat16)
    out_sum = jnp.sum(grad_out, 0)
    qkv_sum = jnp.sum(d_mixed, 0, dtype=jnp.float32)
    query_key_sum = qkv_sum[: 2 * D]
    value_sum = qkv_sum[2 * D :]
    expand_sum = jnp.sum(d_expanded, 0, dtype=jnp.float32)
    small_grads = (
        lax.psum_scatter(gain_one_grad, ("head", "blk"), scatter_dimension=0, tiled=True),
        lax.psum_scatter(shift_one_grad, ("head", "blk"), scatter_dimension=0, tiled=True),
        lax.psum_scatter(gain_two_grad, ("head", "blk"), scatter_dimension=0, tiled=True),
        lax.psum_scatter(shift_two_grad, ("head", "blk"), scatter_dimension=0, tiled=True),
        lax.psum_scatter(query_key_sum, ("head", "blk"), scatter_dimension=0, tiled=True),
        lax.psum_scatter(value_sum, ("head", "blk"), scatter_dimension=0, tiled=True),
        lax.psum_scatter(out_sum, ("head", "blk"), scatter_dimension=0, tiled=True),
        lax.psum_scatter(expand_sum, ("head", "blk"), scatter_dimension=0, tiled=True),
        lax.psum_scatter(out_sum, ("head", "blk"), scatter_dimension=0, tiled=True),
    )
    return (
        output,
        input_grad,
        small_grads[0],
        small_grads[1],
        small_grads[2],
        small_grads[3],
        qkv_grad,
        small_grads[4],
        small_grads[5],
        dense_grad,
        small_grads[6],
        expand_grad,
        small_grads[7],
        shrink_grad,
        small_grads[8],
    )


def solution(mesh):
    placed = (
        P(("head", "blk"), None),
        P(("head", "blk")),
        P(("head", "blk")),
        P(("head", "blk")),
        P(("head", "blk")),
        P(("head", "blk"), None),
        P(("head", "blk")),
        P(("head", "blk"), None),
        P(("head", "blk")),
        P(("head", "blk"), None),
        P(("head", "blk")),
        P(("head", "blk"), None),
        P(("head", "blk")),
        P(),
        P(),
        P(("head", "blk")),
        P(("head", "blk"), None),
    )
    return jax.shard_map(
        per_device,
        mesh=mesh,
        in_specs=placed,
        out_specs=(
            P(("head", "blk"), None),
            P(("head", "blk"), None),
            P(("head", "blk")),
            P(("head", "blk")),
            P(("head", "blk")),
            P(("head", "blk")),
            P(("head", "blk"), None),
            P(("head", "blk")),
            P(("head", "blk")),
            P(("head", "blk"), None),
            P(("head", "blk")),
            P(("head", "blk"), None),
            P(("head", "blk")),
            P(("head", "blk"), None),
            P(("head", "blk")),
        ),
        check_vma=False,
    )
```

profile of v0, /device:TPU:8, one launch (start us, length us, event | category | flops | bytes accessed | tf_op | source)
XLA Modules:
  0.0 3801.1 jit_solution(11751306690166565049)
XLA Ops:
  16.6 42.4 %all-reduce.17 = (bf16[6144]{0:T(1024)(128)(2,1)S(1)}, bf16[2048]{0:T(1024)(128)(2,1)S(1)}, bf16[2048]{0:T(1024)(128)(2,1)S(1)}, bf16[2048]{0:T(1024)(128)(2,1)}...) all-reduce(bf16[6144]{0:T(1024)(128)(2,1)S(1)} %dynamic-update-slic, ...), channel_id=1, replica_groups=mesh['head'=2,'blk'=16] {'head','blk'}, use_global_device_ids=true, to_apply=%add.2 | all-reduce | flops 18432 | bytes 73728
  61.3 104.9 %all-gather.13.cloned.1.call-done = bf16[2048,6144]{1,0:T(8,128)(2,1)} async-done(((bf16[64,6144]{1,0:T(8,128)(2,1)}), bf16[2048,6144]{1,0:T(8,128)(2,1)}) %all-gather.13.cloned.1.call-update) | async-done | bytes 25165840 | tf_op jit(solution)/shard_map/all_gather | solution.py:110
  166.2 13.3 convolution_add_fusion.1
  186.8 29.9 all_to_all.54
  223.7 30.6 all-gather.15.cloned.1.call-done
  259.0 14.4 all_to_all.55
  277.1 23.0 gather_fusion.1
  300.4 34.6 all-gather.3
  339.9 108.9 %all-gather.17.cloned.1.call-done = bf16[2048,8192]{1,0:T(8,128)(2,1)} async-done(((bf16[64,8192]{1,0:T(8,128)(2,1)}), bf16[2048,8192]{1,0:T(8,128)(2,1)}) %all-gather.17.cloned.1.call-update) | async-done | bytes 33554448 | tf_op jit(solution)/shard_map/all_gather | solution.py:111
  448.8 17.1 convolution_add_fusion
  465.9 178.6 %all-gather.19.cloned.1.call-done = bf16[2048,8192]{1,0:T(8,128)(2,1)} async-done(((bf16[64,8192]{1,0:T(8,128)(2,1)}), bf16[2048,8192]{1,0:T(8,128)(2,1)}) %all-gather.19.cloned.1.call-update) | async-done | bytes 33554448 | tf_op jit(solution)/shard_map/all_gather | solution.py:113
  644.5 23.3 convert_reduce_fusion
  669.1 24.4 fusion.118
  693.5 27.4 all-gather.23.cloned.1.call-done
  720.9 8.3 copy.214
  729.2 67.0 %all-gather.25.cloned.1.call-done = bf16[4096,1,4,256]{3,2,1,0:T(4,128)(2,1)} async-done(((bf16[256,1,4,256]{3,2,1,0:T(4,128)(2,1)}), bf16[4096,1,4,256]{3,2,1,0:T(4,128)(2,1)}) %all-gather.25.cloned.1.call-update) | async-done | bytes 8388624 | tf_op jit(solution)/shard_map/all_gather | solution.py:202
  796.2 67.0 %while.43 = (s32[]{:T(128)}, f32[4,256]{1,0:T(4,128)S(1)}, f32[4,256]{1,0:T(4,128)S(1)}, f32[256,4,256]{0,2,1:T(8,128)}, s32[256]{0:T(256)S(1)}, /*index=5*/s32[...) while((s32[]{:T(128)}, f32[4,256]{1,0:T(4,128)S(1)}, ...), condition=%wide.region_7.9_spmd.clone, body=%wide.region_4.8_spmd.clone.sunk | while | flops 545527808 | bytes 15818190 | solution.py:212
  865.4 61.6 %while.44 = (s32[]{:T(128)}, f32[256,4,256]{0,2,1:T(8,128)}, bf16[8,512,4,256]{3,1,2,0:T(8,128)(2,1)}, s32[256]{0:T(256)S(1)}, s32[8,512]{1,0:T(8,128)S(1)}, /*i...) while((s32[]{:T(128)}, f32[256,4,256]{0,2,1:T(8,128)}, ...), condition=%wide.region_10.12_spmd.clone, body=%wide.region_9.11_spmd.clone.sunk | while | flops 810287104 | bytes 12877272 | solution.py:297
  929.1 17.3 all_gather.75
  946.4 17.6 all_gather.77
  964.1 86.0 %while.45 = (s32[]{:T(128)}, f32[256,4,256]{0,2,1:T(8,128)}, f32[256,4,256]{0,2,1:T(8,128)}, bf16[8,512,4,256]{3,2,1,0:T(4,128)(2,1)}, s32[8,512]{1,0:T(8,128)S(...) while((s32[]{:T(128)}, f32[256,4,256]{0,2,1:T(8,128)}, ...), condition=%wide.region_12.14_spmd.clone, body=%wide.region_11.13_spmd.clone.sunk | while | flops 1079771648 | bytes 26549260 | solution.py:343
  1064.4 16.4 fusion.129
  1080.7 9.3 all-to-all-done.3
  1103.0 19.6 fusion.121
  1122.6 15.3 fusion.127
  1144.3 76.0 %pad_maximum_fusion = f32[2048,14336]{1,0:T(8,128)} fusion(f32[2048,8192]{1,0:T(8,128)} %fusion.118, f32[2048,6144]{1,0:T(8,128)} %fusion.121), kind=kLoop, calls=%fused_computation.94 | loop fusion | flops 29360128 | bytes 234881024 | tf_op jit(solution)/shard_map/concatenate | solution.py:366
  1233.5 23.4 convolution_bitcast_fusion.2
  1269.7 57.7 %pad_maximum_fusion.1 = f32[2048,10240]{0,1:T(8,128)} fusion(f32[2048,8192]{0,1:T(8,128)} %convolution_bitcast_fusion.2, f32[2048,2048]{0,1:T(8,128)} %convolution_bitcast_fusion.3), kind=kLoop, calls=%fused_computation.95 | loop fusion | flops 20971520 | bytes 167772160 | tf_op jit(solution)/shard_map/concatenate | solution.py:246
  1327.4 77.1 %copy.246 = f32[2048,10240]{1,0:T(8,128)} copy(f32[2048,10240]{0,1:T(8,128)} %pad_maximum_fusion.1) | data formatting | bytes 167772160
  1412.0 18.3 fusion.61
  1440.0 1472.3 %all-reduce.21.cloned.1.call-done = f32[2048,14336]{1,0:T(8,128)} async-done(((f32[2048,14336]{1,0:T(8,128)}), f32[2048,14336]{1,0:T(8,128)}) %all-reduce.21.cloned.1.call-update) | async-done | bytes 117440528
  2918.5 870.4 %reduce-scatter.4.cloned.1.call-done = f32[64,10240]{1,0:T(8,128)} async-done(((f32[2048,10240]{1,0:T(8,128)}), f32[64,10240]{1,0:T(8,128)}) %reduce-scatter.4.cloned.1.call-update) | async-done | bytes 2621456
  (476 shorter events, 346.0 us)
Async XLA Ops:
  7.2 268.1 %copy-start = (s32[4096]{0:T(1024)S(1)}, s32[4096]{0:T(1024)}, u32[]{:S(2)}) copy-start(s32[4096]{0:T(1024)} %param.38) | copy-start | bytes 49156
  7.2 53.0 %copy-start.3 = (bf16[128,2048]{1,0:T(8,128)(2,1)S(1)}, bf16[128,2048]{1,0:T(8,128)(2,1)}, u32[]{:S(2)}) copy-start(bf16[128,2048]{1,0:T(8,128)(2,1)} %param.25) | copy-start | bytes 1572868
  7.2 159.0 %all-gather.13.cloned.1.call-start = ((), (), s32[]{:S(2)}) async-start(), calls=%async_computation.5 | async-start | bytes 25952256 | tf_op jit(solution)/shard_map/all_gather | solution.py:110
  7.9 246.4 %all-gather.15.cloned.1.call-start = ((), (), s32[]{:S(2)}) async-start(), calls=%async_computation.6 | async-start | bytes 8650752 | tf_op jit(solution)/shard_map/all_gather | solution.py:112
  8.7 440.1 %all-gather.17.cloned.1.call-start = ((), (), s32[]{:S(2)}) async-start(), calls=%async_computation.7 | async-start | bytes 34603008 | tf_op jit(solution)/shard_map/all_gather | solution.py:111
  9.4 635.1 %all-gather.19.cloned.1.call-start = ((), (), s32[]{:S(2)}) async-start(), calls=%async_computation.8 | async-start | bytes 34603008 | tf_op jit(solution)/shard_map/all_gather | solution.py:113
  10.0 710.9 %all-gather.23.cloned.1.call-start = ((), (), s32[]{:S(2)}) async-start(), calls=%async_computation.10 | async-start | bytes 8912896 | tf_op jit(solution)/shard_map/all_gather | solution.py:201
  59.0 120.6 %copy-start.14 = (f32[2048]{0:T(1024)}, f32[2048]{0:T(1024)S(1)}, u32[]{:S(2)}) copy-start(f32[2048]{0:T(1024)S(1)} %convert_element_type.113) | copy-start | bytes 24580
  59.0 120.6 %copy-start.17 = (f32[2048]{0:T(1024)}, f32[2048]{0:T(1024)S(1)}, u32[]{:S(2)}) copy-start(f32[2048]{0:T(1024)S(1)} %convert_element_type.114) | copy-start | bytes 24580
  60.5 119.1 %copy-start.24 = (f32[128]{0:T(128)}, f32[128]{0:T(128)S(1)}, u32[]{:S(2)}) copy-start(f32[128]{0:T(128)S(1)} %fusion.80) | copy-start | bytes 1540
  218.2 36.1 copy-start.6
  223.1 573.1 %all-gather.25.cloned.1.call-start = ((), (), s32[]{:S(2)}) async-start(), calls=%async_computation.11 | async-start | bytes 8912896 | tf_op jit(solution)/shard_map/all_gather | solution.py:202
  223.7 51.5 %copy-start.26 = (bf16[256]{0:T(256)(128)(2,1)S(1)}, bf16[256]{0:T(256)(128)(2,1)}, u32[]{:S(2)}) copy-start(bf16[256]{0:T(256)(128)(2,1)} %param.35) | copy-start | bytes 1540
  223.7 740.4 %all-gather.21.cloned.1.call-start = ((), (), s32[]{:S(2)}) async-start(), calls=%async_computation.9 | async-start | bytes 8912896 | tf_op jit(solution)/shard_map/all_gather | solution.py:329
  274.6 689.5 %all-gather.27.cloned.1.call-start = ((), (), s32[]{:S(2)}) async-start(), calls=%async_computation.12 | async-start | bytes 8912896 | tf_op jit(solution)/shard_map/all_gather | solution.py:328
  277.0 23.2 copy-start.23
  277.0 58.2 %copy-start.10 = (bf16[256,4,256]{2,1,0:T(4,128)(2,1)S(1)}, bf16[256,4,256]{2,1,0:T(4,128)(2,1)}, u32[]{:S(2)}) copy-start(bf16[256,4,256]{2,1,0:T(4,128)(2,1)} %reshape.930) | copy-start | bytes 1572868
  277.1 60.2 %copy-start.12 = (bf16[256,4,256]{2,1,0:T(4,128)(2,1)S(1)}, bf16[256,4,256]{2,1,0:T(4,128)(2,1)}, u32[]{:S(2)}) copy-start(bf16[256,4,256]{2,1,0:T(4,128)(2,1)} %get-tuple-element.1190) | copy-start | bytes 1572868
  277.1 61.0 %copy-start.11 = (bf16[256,4,256]{2,1,0:T(4,128)(2,1)S(1)}, bf16[256,4,256]{2,1,0:T(4,128)(2,1)}, u32[]{:S(2)}) copy-start(bf16[256,4,256]{2,1,0:T(4,128)(2,1)} %get-tuple-element.1194) | copy-start | bytes 1572868
  796.2 67.0 %copy-start.13 = (bf16[256,4,256]{0,2,1:T(8,128)(2,1)S(1)}, bf16[256,4,256]{0,2,1:T(8,128)(2,1)}, u32[]{:S(2)}) copy-start(bf16[256,4,256]{0,2,1:T(8,128)(2,1)} %copy.220) | copy-start | bytes 1572868
  964.1 3.7 copy-start.16
  995.3 3.7 copy-start.16
  1054.9 9.4 copy-start.9
  1059.5 30.5 all-to-all-start.3
  1064.3 366.1 %all-reduce.23.cloned.1.call-start = ((), (), s32[]{:S(2)}) async-start(), calls=%async_computation.15 | async-start | bytes 196608
  1122.6 15.3 copy-start.25
  1144.2 1768.1 %all-reduce.21.cloned.1.call-start = ((), (), s32[]{:S(2)}) async-start(), calls=%async_computation.14 | async-start | bytes 234881024
  1224.3 9.2 copy-start.7
  1229.9 26.9 all-to-all-start.1
  1233.4 2555.5 %reduce-scatter.4.cloned.1.call-start = ((), (), s32[]{:S(2)}) async-start(), calls=%async_computation.13 | async-start | bytes 86507520
  1432.4 2361.5 %copy-start.27 = (f32[64]{0:T(128)}, f32[64]{0:T(128)S(1)}, u32[]{:S(2)}) copy-start(f32[64]{0:T(128)S(1)} %dynamic-slice.7) | copy-start | bytes 772
  2912.3 882.1 %copy-start.1 = (s32[4096]{0:T(1024)S(1)}, s32[4096]{0:T(1024)}, u32[]{:S(2)}) copy-start(s32[4096]{0:T(1024)} %param.38) | copy-start | bytes 49156
  (23 other events, 46.4 us)
Sparse Core Ops, SparseCore 0:
  10.9 155.2 all-gather.12
  169.1 85.1 all-gather.14
  257.2 191.5 all-gather.16
  451.5 192.9 all-gather.18
  646.5 74.3 all-gather.22
  722.9 73.2 all-gather.24
  798.9 73.1 all-gather.20
  874.2 73.3 all-gather.26
  1144.4 125.8 all-reduce.22
  1277.6 1634.6 all-reduce.20
  2914.7 874.2 reduce-scatter.3
where the time goes:
time: 3820 us; the launch traced here: 3800 us
  waiting for transfers between devices  2870 us (75%)
  matrix products  330 us (9%)
  local copies, waits for them, and re-layouts  242 us (6%)
  other arithmetic  175 us (5%)
  blocking collectives  156 us (4%)
    unnamed x14, waiting for transfers between devices  2350 us
    all_gather x1, waiting for transfers between devices, per_device(): lax.all_gather(shrink_weight, ('head', 'blk'), axis=0, tiled=True)  179 us
    unnamed x89, local copies, waits for them, and re-layouts  114 us
    all_gather x1, waiting for transfers between devices, per_device(): lax.all_gather(expand_weight, ('head', 'blk'), axis=0, tiled=True)  109 us
    all_gather x1, waiting for transfers between devices, per_device(): lax.all_gather(qkv_weight, ('head', 'blk'), axis=0, tiled=True)  105 us
  transfers between devices with their start and end apart: 13, of which 9 were waited for; matrix products, arithmetic and copies ran while one was open for 16% of the time, Pallas kernels for 0%

commit v1 on v0

v1 whole, which is shorter than its diff:
```python
import functools
import math

import jax
import jax.numpy as jnp
from jax import lax
from jax.experimental import pallas as pl
from jax.experimental.pallas import tpu as pltpu
from jax.sharding import PartitionSpec as P

HEADS = 8
HEAD_DIM = 256
ROT = 64
PROMPT = 2048
CONT = 256
STRIPE = 16
MESH = pl.DeviceIdType.MESH
BF = jnp.bfloat16
F32 = jnp.float32
ANY = pl.BlockSpec(memory_space=pl.ANY)
VMEM = pl.BlockSpec(memory_space=pltpu.VMEM)
DMA = pltpu.SemaphoreType.DMA


class Place:
    def __init__(self, ways):
        self.ways = ways
        self.x = lax.axis_index("head")
        b = lax.axis_index("blk")
        self.c = b % 2
        self.h = (b // 2) % HEADS
        self.w = b // (2 * HEADS)
        self.hy = self.h % 2
        self.hz = self.h // 2

    def device(self, x=None, w=None, h=None, c=None):
        x = self.x if x is None else x
        w = self.w if w is None else w
        h = self.h if h is None else h
        c = self.c if c is None else c
        return (x, w * (2 * HEADS) + h * 2 + c)

    def peers_h(self):
        return [self.device(h=(self.h + k) % HEADS) for k in range(1, HEADS)]

    def peers_w(self):
        return [self.device(w=(self.w + k) % self.ways) for k in range(1, self.ways)]

    def peer_x(self):
        return self.device(x=1 - self.x)

    def peer_c(self):
        return self.device(c=1 - self.c)

    def peer_y(self):
        return self.device(h=self.h + 1 - 2 * self.hy)


def greet(devices):
    barrier = pltpu.get_barrier_semaphore()
    for one in devices:
        pl.semaphore_signal(barrier, inc=1, device_id=one, device_id_type=MESH)
    pl.semaphore_wait(barrier, len(devices))


def remote(src, dst, send, recv, device):
    return pltpu.make_async_remote_copy(
        src_ref=src, dst_ref=dst, send_sem=send, recv_sem=recv, device_id=device, device_id_type=MESH
    )


def call(body, out_shape, ins, scratch, ident, out_spec=ANY, in_spec=ANY):
    return pl.pallas_call(
        body,
        out_shape=out_shape,
        in_specs=[in_spec] * len(ins),
        out_specs=jax.tree.map(lambda _: out_spec, out_shape),
        scratch_shapes=scratch,
        compiler_params=pltpu.CompilerParams(
            collective_id=ident, has_side_effects=True, vmem_limit_bytes=60 * 2**20
        ),
    )(*ins)


LINE = HEADS // 2


def spread_rows(place, own, full, up, down, side, recv):
    hz, hy = place.hz, place.hy

    def piece(src, z, target, send):
        idx = z * 2 + hy
        return remote(src, full.at[:, idx], send, recv.at[idx], target)

    def up_to():
        return place.device(h=place.h + 2)

    def down_to():
        return place.device(h=place.h - 2)

    def first():
        @pl.when(hz < LINE - 1)
        def _():
            piece(own, hz, up_to(), up.at[0]).start()

        @pl.when(hz > 0)
        def _():
            piece(own, hz, down_to(), down.at[0]).start()

        piece(own, hz, place.peer_y(), side.at[0]).start()

    def arrived(idx):
        remote(full.at[:, idx], full.at[:, idx], side.at[0], recv.at[idx], place.peer_y()).wait_recv()

    def step(s):
        low, high = hz - s - 1, hz + s + 1

        @pl.when(low >= 0)
        def _():
            arrived(low * 2 + hy)
            src = full.at[:, low * 2 + hy]

            @pl.when(hz < LINE - 1)
            def _():
                piece(src, low, up_to(), up.at[s + 1]).start()

            piece(src, low, place.peer_y(), side.at[low + 1]).start()

        @pl.when(high < LINE)
        def _():
            arrived(high * 2 + hy)
            src = full.at[:, high * 2 + hy]

            @pl.when(hz > 0)
            def _():
                piece(src, high, down_to(), down.at[s + 1]).start()

            piece(src, high, place.peer_y(), side.at[high + 1]).start()

    def finish():
        for z in range(LINE):
            arrived(z * 2 + 1 - hy)

    def sent():
        piece(own, hz, place.peer_y(), side.at[0]).wait_send()
        for z in range(LINE):
            @pl.when(z != hz)
            def _():
                piece(own, z, place.peer_y(), side.at[z + 1]).wait_send()
        for s in range(LINE - 1):
            @pl.when((hz < LINE - 1) & (hz - s >= 0))
            def _():
                piece(own, hz, up_to(), up.at[s]).wait_send()

            @pl.when((hz > 0) & (hz + s < LINE))
            def _():
                piece(own, hz, down_to(), down.at[s]).wait_send()

    return first, step, finish, sent


def gather_kernel(ways, n_in, g_in, w_in, m_in, n_all, g_all, w_all, m_all,
                  local, nu, nd, ns, nr, gu, gd, gs, gr, wa, wx, wc, wr, ma, mx, mc, mr):
    place = Place(ways)
    x, w, h, c = place.x, place.w, place.h, place.c
    stage_a = [(dw, dh) for dw in range(ways) for dh in range(HEADS) if (dw, dh) != (0, 0)]
    greet(
        [place.device(w=(w + dw) % ways, h=(h + dh) % HEADS) for dw, dh in stage_a]
        + [place.peer_x(), place.peer_c()]
    )
    n_first, n_step, n_finish, n_sent = spread_rows(place, n_in, n_all, nu, nd, ns, nr)
    g_first, g_step, g_finish, g_sent = spread_rows(place, g_in, g_all, gu, gd, gs, gr)
    copies = [
        pltpu.make_async_copy(n_in, n_all.at[:, h], local.at[0]),
        pltpu.make_async_copy(g_in, g_all.at[:, h], local.at[1]),
        pltpu.make_async_copy(w_in.at[h], w_all.at[x, w, h, c], local.at[2]),
        pltpu.make_async_copy(m_in.at[h], m_all.at[x, w, h, c], local.at[3]),
    ]
    n_first()
    sends = []

    def send(src, dst, s, r, device):
        copy = remote(src, dst, s, r, device)
        copy.start()
        sends.append(copy)

    pairs = ((w_all, wa, wx, wc, wr), (m_all, ma, mx, mc, mr))
    for k, (dw, dh) in enumerate(stage_a):
        h2 = (h + dh) % HEADS
        target = place.device(w=(w + dw) % ways, h=h2)
        send(w_in.at[h2], w_all.at[x, w, h, c], wa.at[k], wr.at[x, w, h, c], target)
        send(m_in.at[h2], m_all.at[x, w, h, c], ma.at[k], mr.at[x, w, h, c], target)
    send(w_in.at[h], w_all.at[x, w, h, c], wx.at[w, h], wr.at[x, w, h, c], place.peer_x())
    send(m_in.at[h], m_all.at[x, w, h, c], mx.at[w, h], mr.at[x, w, h, c], place.peer_x())
    send(w_in.at[h], w_all.at[x, w, h, c], wc.at[x, w, h], wr.at[x, w, h, c], place.peer_c())
    send(m_in.at[h], m_all.at[x, w, h, c], mc.at[x, w, h], mr.at[x, w, h, c], place.peer_c())
    g_first()
    for copy in copies:
        copy.start()

    def arrived(full, recv, xs, ws, hs, cs):
        place_ref = full.at[xs, ws, hs, cs]
        remote(place_ref, place_ref, local.at[0], recv.at[xs, ws, hs, cs], place.peer_x()).wait_recv()

    for s in range(LINE - 1):
        n_step(s)
    for dw, dh in stage_a:
        ws, hs = (w - dw) % ways, (h - dh) % HEADS
        for full, _, to_x, to_c, recv in pairs:
            arrived(full, recv, x, ws, hs, c)
            block = full.at[x, ws, hs, c]
            send(block, block, to_x.at[ws, hs], recv.at[x, ws, hs, c], place.peer_x())
            send(block, block, to_c.at[x, ws, hs], recv.at[x, ws, hs, c], place.peer_c())
    for s in range(LINE - 1):
        g_step(s)
    for dw, dh in [(0, 0)] + stage_a:
        ws, hs = (w - dw) % ways, (h - dh) % HEADS
        for full, _, _, to_c, recv in pairs:
            arrived(full, recv, 1 - x, ws, hs, c)
            block = full.at[1 - x, ws, hs, c]
            send(block, block, to_c.at[1 - x, ws, hs], recv.at[1 - x, ws, hs, c], place.peer_c())
    n_finish()
    g_finish()
    for dw, dh in [(0, 0)] + stage_a:
        ws, hs = (w - dw) % ways, (h - dh) % HEADS
        for full, _, _, _, recv in pairs:
            for xs in (x, 1 - x):
                arrived(full, recv, xs, ws, hs, 1 - c)
    for copy in copies:
        copy.wait()
    for copy in sends:
        copy.wait_send()
    n_sent()
    g_sent()


def gather_all(ways, normed, grads, weights, notes):
    runs, _, width = normed.shape
    _, rows, columns = weights.shape
    blocks = (2, ways, HEADS, 2)
    shapes = (
        jax.ShapeDtypeStruct((runs, HEADS, STRIPE, width), BF),
        jax.ShapeDtypeStruct((runs, HEADS, STRIPE, width), BF),
        jax.ShapeDtypeStruct(blocks + (rows, columns), BF),
        jax.ShapeDtypeStruct(blocks + notes.shape[1:], F32),
    )
    row_sems = [DMA((LINE,)), DMA((LINE,)), DMA((LINE + 1,)), DMA((HEADS,))]
    block_sems = [DMA((ways * HEADS,)), DMA((ways, HEADS)), DMA((2, ways, HEADS)), DMA(blocks)]
    return call(
        functools.partial(gather_kernel, ways),
        shapes,
        (normed, grads, weights, notes),
        [DMA((4,))] + row_sems + row_sems + block_sems + block_sems,
        0,
    )


def exchange_kernel(ways, own, full, local, to_w, to_x, to_c, recv):
    place = Place(ways)
    x, w, c = place.x, place.w, place.c
    runs = own.shape[0]
    parts = 4
    span = runs // parts
    greet(place.peers_w() + [place.peer_x(), place.peer_c()])

    def spot(ws, xs, cs, p):
        return full.at[pl.ds(p * span, span), ws * 4 + xs * 2 + cs]

    sends = []

    def send(src, ws, xs, cs, p, sem, device):
        copy = remote(src, spot(ws, xs, cs, p), sem, recv.at[ws, xs, cs, p], device)
        copy.start()
        sends.append(copy)

    def arrived(ws, xs, cs, p):
        remote(spot(ws, xs, cs, p), spot(ws, xs, cs, p), local.at[0], recv.at[ws, xs, cs, p], place.peer_x()).wait_recv()

    keep = pltpu.make_async_copy(own, full.at[:, w * 4 + x * 2 + c], local.at[0])
    for p in range(parts):
        src = own.at[pl.ds(p * span, span)]
        for k, device in enumerate(place.peers_w()):
            send(src, w, x, c, p, to_w.at[k, p], device)
        send(src, w, x, c, p, to_x.at[w, p], place.peer_x())
    for p in range(parts):
        send(own.at[pl.ds(p * span, span)], w, x, c, p, to_c.at[w, x, p], place.peer_c())
    keep.start()
    for k in range(1, ways):
        ws = (w - k) % ways
        for p in range(parts):
            arrived(ws, x, c, p)
            send(spot(ws, x, c, p), ws, x, c, p, to_x.at[ws, p], place.peer_x())
            send(spot(ws, x, c, p), ws, x, c, p, to_c.at[ws, x, p], place.peer_c())
    for k in range(ways):
        ws = (w - k) % ways
        for p in range(parts):
            arrived(ws, 1 - x, c, p)
            send(spot(ws, 1 - x, c, p), ws, 1 - x, c, p, to_c.at[ws, 1 - x, p], place.peer_c())
    for k in range(ways):
        ws = (w - k) % ways
        for p in range(parts):
            arrived(ws, x, 1 - c, p)
            arrived(ws, 1 - x, 1 - c, p)
    keep.wait()
    for copy in sends:
        copy.wait_send()


def exchange(ways, own):
    runs, rows, columns = own.shape
    return call(
        functools.partial(exchange_kernel, ways),
        jax.ShapeDtypeStruct((runs, 4 * ways, rows, columns), BF),
        (own,),
        [DMA((1,)), DMA((ways, 4)), DMA((ways, 4)), DMA((ways, 2, 4)), DMA((ways, 2, 2, 4))],
        1,
    )


def fold_kernel(ways, part, total, from_c, from_x, from_w, s_c, r_c, s_x, r_x, s_w, r_w):
    place = Place(ways)
    x, w, c = place.x, place.w, place.c
    runs = part.shape[0]
    greet(place.peers_w() + [place.peer_x(), place.peer_c()])

    def slot(ws, xs, cs):
        return ws * 4 + xs * 2 + cs

    sends = []

    def send(src, dst, s, r, device):
        copy = remote(src, dst, s, r, device)
        copy.start()
        sends.append(copy)
        return copy

    order = [(w + k) % ways for k in range(1, ways)] + [w]
    first = []
    for i, ws in enumerate(order):
        for xs, k in ((1 - x, 0), (x, 1)):
            first.append(
                send(part.at[:, slot(ws, xs, 1 - c)], from_c.at[:, i, k], s_c.at[i, k], r_c.at[i, k], place.peer_c())
            )

    def add(i, k, ws, xs, extra):
        @pl.loop(0, runs)
        def _(run):
            value = part[run, slot(ws, xs, c)].astype(F32) + from_c[run, i, k].astype(F32)
            if extra:
                value = value + from_x[run, i].astype(F32)
            if extra and i == ways - 1:
                for q in range(ways - 1):
                    value = value + from_w[run, q].astype(F32)
                total[run] = value
            else:
                from_c[run, i, k] = value.astype(BF)

    for i, ws in enumerate(order):
        first[2 * i].wait_recv()
        add(i, 0, ws, 1 - x, False)
        send(from_c.at[:, i, 0], from_x.at[:, i], s_x.at[i], r_x.at[i], place.peer_x())
    for i, ws in enumerate(order):
        first[2 * i + 1].wait_recv()
        remote(from_x.at[:, i], from_x.at[:, i], s_x.at[i], r_x.at[i], place.peer_x()).wait_recv()
        if i == ways - 1:
            for q in range(ways - 1):
                remote(from_w.at[:, q], from_w.at[:, q], s_w.at[q], r_w.at[q], place.peer_x()).wait_recv()
        add(i, 1, ws, x, True)
        if i < ways - 1:
            send(from_c.at[:, i, 1], from_w.at[:, i], s_w.at[i], r_w.at[i], place.device(w=ws))
    for copy in sends:
        copy.wait_send()


def fold(ways, part):
    runs, _, rows, columns = part.shape
    extra = max(ways - 1, 1)
    return call(
        functools.partial(fold_kernel, ways),
        jax.ShapeDtypeStruct((runs, rows, columns), F32),
        (part,),
        [
            pltpu.VMEM((runs, ways, 2, rows, columns), BF),
            pltpu.VMEM((runs, ways, rows, columns), BF),
            pltpu.VMEM((runs, extra, rows, columns), BF),
            DMA((ways, 2)), DMA((ways, 2)), DMA((ways,)), DMA((ways,)), DMA((extra,)), DMA((extra,)),
        ],
        2,
        VMEM,
        VMEM,
    )


def collect_kernel(ways, part, total, from_y, from_z, s_y, r_y, s_z, r_z):
    place = Place(ways)
    hz, hy = place.hz, place.hy
    runs = part.shape[0]
    others = [(hz + k) % LINE for k in range(1, LINE)]
    greet([place.peer_y()] + [place.device(h=z * 2 + hy) for z in others])
    order = others + [hz]
    sends, first = [], []
    for i, z in enumerate(order):
        copy = remote(part.at[:, z * 2 + 1 - hy], from_y.at[:, i], s_y.at[i], r_y.at[i], place.peer_y())
        copy.start()
        sends.append(copy)
    for i, z in enumerate(order):
        sends[i].wait_recv()
        if i < LINE - 1:
            @pl.loop(0, runs)
            def _(run):
                value = part[run, z * 2 + hy].astype(F32) + from_y[run, i].astype(F32)
                from_y[run, i] = value.astype(BF)

            copy = remote(from_y.at[:, i], from_z.at[:, i], s_z.at[i], r_z.at[i], place.device(h=z * 2 + hy))
            copy.start()
            first.append(copy)
    for copy in first:
        copy.wait_recv()

    @pl.loop(0, runs)
    def _(run):
        value = part[run, hz * 2 + hy].astype(F32) + from_y[run, LINE - 1].astype(F32)
        for i in range(LINE - 1):
            value = value + from_z[run, i].astype(F32)
        total[run] = value

    for copy in sends + first:
        copy.wait_send()


def collect(ways, part, ident):
    runs, _, rows, width = part.shape
    return call(
        functools.partial(collect_kernel, ways),
        jax.ShapeDtypeStruct((runs, rows, width), F32),
        (part,),
        [
            pltpu.VMEM((runs, LINE, rows, width), BF),
            pltpu.VMEM((runs, LINE - 1, rows, width), BF),
            DMA((LINE,)), DMA((LINE,)), DMA((LINE - 1,)), DMA((LINE - 1,)),
        ],
        ident,
        VMEM,
        VMEM,
    )


def owners_kernel(ways, part, note, out, note_out, from_c, from_x, from_w, note_c, note_x, note_w,
                  local, s_c, r_c, s_x, r_x, s_w, r_w, s_h, r_h, ns_c, nr_c, ns_x, nr_x, ns_w, nr_w, ns_h, nr_h):
    place = Place(ways)
    x, w, h, c = place.x, place.w, place.h, place.c
    rows = part.shape[4]
    piece = min(rows, 16)
    greet(place.peers_h() + place.peers_w() + [place.peer_x(), place.peer_c()])
    order = [(dw, dh) for dh in list(range(1, HEADS)) + [0] for dw in list(range(1, ways)) + [0]]
    sends = []

    def send(src, dst, s, r, device):
        copy = remote(src, dst, s, r, device)
        copy.start()
        sends.append(copy)
        return copy

    def both(src, nsrc, dst, ndst, s, ns, r, nr, device):
        return send(src, dst, s, r, device), send(nsrc, ndst, ns, nr, device)

    first = {}
    for k, xs in ((0, 1 - x), (1, x)):
        for dw, dh in order:
            ws, hs = (w + dw) % ways, (h + dh) % HEADS
            first[k, dw, dh] = both(
                part.at[xs, ws, hs, 1 - c], note.at[xs, ws, hs, 1 - c],
                from_c.at[k, dw, dh], note_c.at[k, dw, dh],
                s_c.at[k, dw, dh], ns_c.at[k, dw, dh], r_c.at[k, dw, dh], nr_c.at[k, dw, dh], place.peer_c(),
            )

    def add(k, dw, dh, xs, more):
        ws, hs = (w + dw) % ways, (h + dh) % HEADS

        @pl.loop(0, rows // piece)
        def _(q):
            at = pl.ds(pl.multiple_of(q * piece, piece), piece)
            value = part[xs, ws, hs, c, at].astype(F32) + from_c[k, dw, dh, at].astype(F32)
            for ref in more:
                value = value + ref[at].astype(F32)
            from_c[k, dw, dh, at] = value.astype(BF)

    second = {}
    for dw, dh in order:
        ws, hs = (w + dw) % ways, (h + dh) % HEADS
        for copy in first[0, dw, dh]:
            copy.wait_recv()
        add(0, dw, dh, 1 - x, [])
        note_c[0, dw, dh] = note_c[0, dw, dh] + note[1 - x, ws, hs, c]
        second[dw, dh] = both(
            from_c.at[0, dw, dh], note_c.at[0, dw, dh], from_x.at[dw, dh], note_x.at[dw, dh],
            s_x.at[dw, dh], ns_x.at[dw, dh], r_x.at[dw, dh], nr_x.at[dw, dh], place.peer_x(),
        )
    third = {}
    last = []
    for dw, dh in order:
        ws, hs = (w + dw) % ways, (h + dh) % HEADS
        for copy in first[1, dw, dh] + second[dw, dh]:
            copy.wait_recv()
        more = [from_x.at[dw, dh]]
        summed = note_c[1, dw, dh] + note[x, ws, hs, c] + note_x[dw, dh]
        if dw == 0:
            for dv in range(1, ways):
                for copy in third[dv, dh]:
                    copy.wait_recv()
                more.append(from_w.at[dv - 1, dh])
                summed = summed + note_w[dv - 1, dh]
        add(1, dw, dh, x, more)
        note_c[1, dw, dh] = summed
        if dw != 0:
            third[dw, dh] = both(
                from_c.at[1, dw, dh], note_c.at[1, dw, dh], from_w.at[dw - 1, dh], note_w.at[dw - 1, dh],
                s_w.at[dw - 1, dh], ns_w.at[dw - 1, dh], r_w.at[dw - 1, dh], nr_w.at[dw - 1, dh], place.device(w=ws),
            )
        elif dh != 0:
            last.append(both(
                from_c.at[1, 0, dh], note_c.at[1, 0, dh], out.at[h], note_out.at[h],
                s_h.at[dh], ns_h.at[dh], r_h.at[h], nr_h.at[h], place.device(h=hs),
            ))
        else:
            keep = [
                pltpu.make_async_copy(from_c.at[1, 0, 0], out.at[h], local.at[0]),
                pltpu.make_async_copy(note_c.at[1, 0, 0], note_out.at[h], local.at[1]),
            ]
            for copy in keep:
                copy.start()
    for dh in range(1, HEADS):
        hs = (h - dh) % HEADS
        remote(out.at[hs], out.at[hs], s_h.at[0], r_h.at[hs], place.peer_x()).wait_recv()
        remote(note_out.at[hs], note_out.at[hs], ns_h.at[0], nr_h.at[hs], place.peer_x()).wait_recv()
    for copy in keep:
        copy.wait()
    for copy in sends:
        copy.wait_send()


def to_owners(ways, part, note):
    rows, columns = part.shape[4:]
    extra = max(ways - 1, 1)

    def sems():
        return [
            DMA((2, ways, HEADS)), DMA((2, ways, HEADS)), DMA((ways, HEADS)), DMA((ways, HEADS)),
            DMA((extra, HEADS)), DMA((extra, HEADS)), DMA((HEADS,)), DMA((HEADS,)),
        ]

    def slots(shape, kind):
        return [
            pltpu.VMEM((2, ways, HEADS) + shape, kind),
            pltpu.VMEM((ways, HEADS) + shape, kind),
            pltpu.VMEM((extra, HEADS) + shape if ways > 1 else (1, 1) + shape, kind),
        ]

    return call(
        functools.partial(owners_kernel, ways),
        (
            jax.ShapeDtypeStruct((HEADS, rows, columns), BF),
            jax.ShapeDtypeStruct((HEADS,) + note.shape[4:], F32),
        ),
        (part, note),
        slots((rows, columns), BF) + slots(note.shape[4:], F32) + [DMA((2,))] + sems() + sems(),
        5,
        VMEM,
        VMEM,
    )


def attention_kernel(prompt_runs, one_prompt, q_ref, do_ref, k_ref, v_ref, row_ref, col_ref,
                     o_ref, dq_ref, dk_ref, dv_ref, s_ref):
    runs, m, _ = q_ref.shape
    keys = k_ref.shape[1]
    by_rows = (((1,), (1,)), ((), ()))
    by_tokens = (((0,), (0,)), ((), ()))

    def dot(a, b, dims):
        return lax.dot_general(a, b, dims, preferred_element_type=F32)

    def mask(i, k):
        rows, cols = row_ref[i], col_ref[k]
        if isinstance(i, int) and isinstance(k, int) and i == k:
            return (rows[:, 1:2] == cols[1:2, :]) & (cols[0:1, :] <= rows[:, 0:1])
        if one_prompt:
            return None
        return rows[:, 2:3] == cols[2:3, :]

    for i in range(runs):
        pieces = list(range(min(i + 1, prompt_runs))) + ([i] if i >= prompt_runs else [])
        q = q_ref[i]
        peak = None
        for at, k in enumerate(pieces):
            s = dot(q, k_ref[k], by_rows)
            keep = mask(i, k)
            if keep is not None:
                s = jnp.where(keep, s, -1e30)
            s_ref[:, at * keys : (at + 1) * keys] = s
            top = jnp.max(s, -1, keepdims=True)
            peak = top if peak is None else jnp.maximum(peak, top)
        total = jnp.zeros((m, 1), F32)
        out = jnp.zeros((m, HEAD_DIM), F32)
        for at, k in enumerate(pieces):
            s = s_ref[:, at * keys : (at + 1) * keys]
            p = jnp.exp(s - peak)
            keep = mask(i, k)
            if keep is not None:
                p = jnp.where(keep, p, 0.0)
            s_ref[:, at * keys : (at + 1) * keys] = p
            total = total + jnp.sum(p, -1, keepdims=True)
            out = out + dot(p.astype(BF), v_ref[k], (((1,), (0,)), ((), ())))
        inverse = 1.0 / total
        out = out * inverse
        o_ref[i] = out.astype(BF)
        do = do_ref[i]
        delta = jnp.sum(out * do.astype(F32), -1, keepdims=True)
        dq = jnp.zeros((m, HEAD_DIM), F32)
        for at, k in enumerate(pieces):
            p = s_ref[:, at * keys : (at + 1) * keys] * inverse
            dp = dot(do, v_ref[k], by_rows)
            ds = (p * (dp - delta)).astype(BF)
            dq = dq + dot(ds, k_ref[k], (((1,), (0,)), ((), ())))
            dk = dot(ds, q, by_tokens)
            dv = dot(p.astype(BF), do, by_tokens)
            if i == k:
                dk_ref[k] = dk
                dv_ref[k] = dv
            else:
                dk_ref[k] = dk_ref[k] + dk
                dv_ref[k] = dv_ref[k] + dv
        dq_ref[i] = dq * (1.0 / math.sqrt(HEAD_DIM))


def attention(prompt_runs, one_prompt, queries, d_out, keys, values, row_meta, col_meta):
    runs, m, _ = queries.shape
    count = keys.shape[1]
    return pl.pallas_call(
        functools.partial(attention_kernel, prompt_runs, one_prompt),
        out_shape=(
            jax.ShapeDtypeStruct(queries.shape, BF),
            jax.ShapeDtypeStruct(queries.shape, F32),
            jax.ShapeDtypeStruct(keys.shape, F32),
            jax.ShapeDtypeStruct(keys.shape, F32),
        ),
        in_specs=[VMEM] * 6,
        out_specs=(VMEM,) * 4,
        scratch_shapes=[pltpu.VMEM((m, (prompt_runs + 1) * count), F32)],
        compiler_params=pltpu.CompilerParams(vmem_limit_bytes=60 * 2**20),
    )(queries, d_out, keys, values, row_meta, col_meta)


def angles_of(positions):
    frequency = 10000.0 ** (-jnp.arange(0, ROT, 2, dtype=F32) / ROT)
    return positions.astype(F32)[:, None] * frequency[None, :]


def rotate(values, cosine, sine):
    half = ROT // 2
    leading, behind = values[:, :half], values[:, half:ROT]
    return jnp.concatenate(
        [leading * cosine - behind * sine, behind * cosine + leading * sine, values[:, ROT:]], -1
    )


def per_device(
    inputs, attn_norm_gain, attn_norm_bias, mlp_norm_gain, mlp_norm_bias, qkv_weight, qkv_bias, dense_weight,
    dense_bias, expand_weight, expand_bias, shrink_weight, shrink_bias, token_of_row, cont_parent, position_ids,
    cotangent,
):
    heads, blocks = lax.axis_size("head"), lax.axis_size("blk")
    devices = heads * blocks
    ways = blocks // (2 * HEADS)
    assert heads == 2 and blocks == ways * 2 * HEADS
    x = lax.axis_index("head")
    b = lax.axis_index("blk")
    me = x * blocks + b
    c, h, w = b % 2, (b // 2) % HEADS, b // (2 * HEADS)
    tok_dev, width = inputs.shape
    rows = qkv_weight.shape[0]
    hidden = expand_weight.shape[1] // HEADS
    runs = tok_dev // STRIPE
    run_size = devices * STRIPE
    prompt_total = token_of_row.shape[0] - cont_parent.shape[0] * CONT
    prompt_runs = prompt_total // run_size
    one_prompt = prompt_total == PROMPT
    assert prompt_runs * run_size == prompt_total
    group_rows = runs * HEADS * STRIPE
    head3 = 3 * HEAD_DIM
    block_columns = head3 + hidden

    by_device = token_of_row.reshape(devices, tok_dev)
    run_of = by_device // run_size
    big = jnp.int32(2**30)
    each_run = jnp.arange(runs, dtype=jnp.int32)
    base = jnp.min(jnp.where(run_of[:, :, None] == each_run, by_device[:, :, None], big), 1)
    mine = lax.dynamic_index_in_dim(by_device, me, 0, False)
    sorted_at = mine // run_size * STRIPE + mine % STRIPE
    pick = (sorted_at[None, :] == jnp.arange(tok_dev, dtype=jnp.int32)[:, None]).astype(BF)
    base_position = jnp.min(
        jnp.where((mine // run_size)[:, None] == each_run, position_ids[:, None], big), 0
    )

    def ordered(rows_in):
        return jnp.dot(pick, rows_in, preferred_element_type=F32).astype(BF)

    def restored(rows_in):
        return lax.dot_general(pick, rows_in, (((0,), (0,)), ((), ())), preferred_element_type=F32).astype(BF)

    states = ordered(inputs).astype(F32)
    grad_low = ordered(cotangent)
    grad_out = grad_low.astype(F32)
    average = jnp.mean(states, -1, keepdims=True)
    centered = states - average
    inverse_spread = lax.rsqrt(jnp.mean(centered * centered, -1, keepdims=True) + 1e-05)
    normed = centered * inverse_spread
    normed_low = normed.astype(BF)

    gain_one, shift_one = attn_norm_gain.astype(F32), attn_norm_bias.astype(F32)
    gain_two, shift_two = mlp_norm_gain.astype(F32), mlp_norm_bias.astype(F32)
    qkv_wide, expand_wide = qkv_weight.astype(F32), expand_weight.astype(F32)

    def split_qkv(values):
        return values.reshape(-1, 3, HEADS, HEAD_DIM).transpose(2, 0, 1, 3).reshape(HEADS, -1, head3)

    def split(values):
        return values.reshape(values.shape[0], HEADS, -1).transpose(1, 0, 2)

    weights = jnp.concatenate(
        [
            split_qkv((qkv_wide * gain_one[:, None]).astype(BF)),
            split((expand_wide * gain_two[:, None]).astype(BF)),
            split(dense_weight),
            split(shrink_weight),
        ],
        -1,
    )
    own_qkv_bias = lax.dynamic_update_slice_in_dim(
        jnp.zeros((3 * width,), F32), qkv_bias.astype(F32), me * qkv_bias.shape[0], 0
    )
    own_expand_bias = lax.dynamic_update_slice_in_dim(
        jnp.zeros((HEADS * hidden,), F32), expand_bias.astype(F32), me * expand_bias.shape[0], 0
    )
    bias_parts = jnp.concatenate(
        [
            split_qkv((jnp.sum(qkv_wide * shift_one[:, None], 0) + own_qkv_bias)[None])[:, 0],
            split((jnp.sum(expand_wide * shift_two[:, None], 0) + own_expand_bias)[None])[:, 0],
        ],
        -1,
    )
    lanes = 128
    note_rows = block_columns // lanes

    def padded(values):
        return jnp.pad(values, (0, lanes - values.shape[0]))

    tail = jnp.stack([padded(dense_bias.astype(F32) + shrink_bias.astype(F32)), padded(base_position.astype(F32))])
    notes = jnp.concatenate(
        [bias_parts.reshape(HEADS, note_rows, lanes), jnp.broadcast_to(tail[None], (HEADS, 2, lanes))], 1
    )

    n_all, g_all, w_all, m_all = gather_all(
        ways, normed_low.reshape(runs, STRIPE, width), grad_low.reshape(runs, STRIPE, width), weights, notes
    )
    n_all = n_all.reshape(group_rows, width)
    g_all = g_all.reshape(group_rows, width)
    w_all = w_all.reshape(width, block_columns + HEAD_DIM + hidden)
    bias_block = jnp.sum(m_all[..., :note_rows, :], (0, 1, 2, 3)).reshape(block_columns)
    out_bias = m_all[..., note_rows, :rows].reshape(width)
    group_position = lax.dynamic_index_in_dim(m_all[:, :, :, :, note_rows + 1, :runs], x, 0, False)
    group_position = lax.dynamic_index_in_dim(group_position, w, 0, False)
    group_position = lax.dynamic_index_in_dim(group_position, c, 1, False)
    within = jnp.arange(STRIPE, dtype=jnp.int32)
    position = (group_position.T[:, :, None] + within.astype(F32)).reshape(group_rows)
    angles = angles_of(position)
    cosine, sine = jnp.cos(angles), jnp.sin(angles)

    w_in = w_all[:, :block_columns]
    w_out = w_all[:, block_columns:]
    mixed = jnp.dot(n_all, w_in[:, :head3], preferred_element_type=F32) + bias_block[:head3]
    queries = (rotate(mixed[:, :HEAD_DIM], cosine, sine) * (1.0 / math.sqrt(HEAD_DIM))).astype(BF)
    keys = rotate(mixed[:, HEAD_DIM : 2 * HEAD_DIM], cosine, sine).astype(BF)
    values = mixed[:, 2 * HEAD_DIM :].astype(BF)
    rows_run = group_rows // runs
    pairs = exchange(ways, jnp.concatenate([keys, values], 1).reshape(runs, rows_run, 2 * HEAD_DIM))
    pairs = pairs.reshape(runs, run_size, 2 * HEAD_DIM)

    d_attended = jnp.dot(g_all, w_out[:, :HEAD_DIM], preferred_element_type=F32).astype(BF)
    expanded = jnp.dot(n_all, w_in[:, head3:], preferred_element_type=F32) + bias_block[head3:]
    activated, gelu_back = jax.vjp(lambda v: jax.nn.gelu(v, approximate=False), expanded)
    activated = activated.astype(BF)
    d_activated = jnp.dot(g_all, w_out[:, HEAD_DIM:], preferred_element_type=F32)
    d_expanded = gelu_back(d_activated)[0].astype(BF)

    bases = base.reshape(2, ways, HEADS, 2, runs)
    own_base = lax.dynamic_index_in_dim(bases, x, 0, False)
    own_base = lax.dynamic_index_in_dim(own_base, w, 0, False)
    own_base = lax.dynamic_index_in_dim(own_base, c, 1, False)
    row_tokens = (own_base.T[:, :, None] + within).reshape(runs, rows_run)
    col_tokens = (bases.transpose(4, 1, 0, 3, 2)[..., None] + within).reshape(runs, run_size)

    def meta(tokens):
        is_prompt = tokens < prompt_total
        cont = (tokens - prompt_total) // CONT
        if one_prompt:
            prompt = jnp.zeros_like(tokens)
        else:
            matches = cont[..., None] == jnp.arange(cont_parent.shape[0], dtype=jnp.int32)
            prompt = jnp.where(is_prompt, tokens // PROMPT, jnp.sum(jnp.where(matches, cont_parent, 0), -1))
        segment = jnp.where(is_prompt, -1 - tokens // PROMPT, cont)
        return tokens, segment, prompt

    row_meta = jnp.stack(meta(row_tokens), -1)
    col_meta = jnp.stack(meta(col_tokens), 1)
    attended, d_queries, d_keys, d_values = attention(
        prompt_runs, one_prompt,
        queries.reshape(runs, rows_run, HEAD_DIM), d_attended.reshape(runs, rows_run, HEAD_DIM),
        pairs[..., :HEAD_DIM], pairs[..., HEAD_DIM:], row_meta, col_meta,
    )
    attended = attended.reshape(group_rows, HEAD_DIM)

    contract = (((1,), (1,)), ((), ()))
    tokens_dims = (((0,), (0,)), ((), ()))
    left = jnp.concatenate([attended, activated], 1)
    out_part = lax.dot_general(left, w_out, contract, preferred_element_type=F32).astype(BF)
    out_sum = collect(ways, out_part.reshape(runs, HEADS, STRIPE, width), 3).reshape(tok_dev, width)
    output = restored((states + out_sum + out_bias).astype(BF))

    d_pairs = jnp.concatenate([d_keys, d_values], -1).astype(BF)
    d_pairs = fold(ways, d_pairs.reshape(runs, 4 * ways, rows_run, 2 * HEAD_DIM)).reshape(group_rows, 2 * HEAD_DIM)
    d_mixed = jnp.concatenate(
        [
            rotate(d_queries.reshape(group_rows, HEAD_DIM).astype(BF).astype(F32), cosine, -sine),
            rotate(d_pairs[:, :HEAD_DIM].astype(BF).astype(F32), cosine, -sine),
            d_pairs[:, HEAD_DIM:],
        ],
        1,
    ).astype(BF)

    right = jnp.concatenate([d_mixed, d_expanded], 1)
    e_part = lax.dot_general(right, w_in, contract, preferred_element_type=F32).astype(BF)
    e_sum = collect(ways, e_part.reshape(runs, HEADS, STRIPE, width), 4).reshape(tok_dev, width)
    dx = inverse_spread * (
        e_sum - jnp.mean(e_sum, -1, keepdims=True) - normed * jnp.mean(e_sum * normed, -1, keepdims=True)
    )
    input_grad = restored((grad_out + dx).astype(BF))

    part = jnp.concatenate(
        [
            lax.dot_general(n_all, right, tokens_dims, preferred_element_type=F32).astype(BF),
            lax.dot_general(g_all, left, tokens_dims, preferred_element_type=F32).astype(BF),
        ],
        1,
    )
    part = part.reshape(2, ways, HEADS, 2, rows, part.shape[1])
    sums = jnp.sum(right.astype(F32), 0).reshape(note_rows, lanes)
    g_sums = jnp.pad(jnp.sum(grad_out, 0).reshape(devices, 1, rows), ((0, 0), (0, 0), (0, lanes - rows)))
    sum_notes = jnp.concatenate(
        [
            jnp.broadcast_to(sums[None], (devices, note_rows, lanes)),
            g_sums,
            jnp.zeros((devices, 1, lanes), F32),
        ],
        1,
    ).reshape(2, ways, HEADS, 2, note_rows + 2, lanes)
    owned, owned_notes = to_owners(ways, part, sum_notes)
    owned = owned.astype(F32)

    def join_qkv(values):
        return values.reshape(HEADS, -1, 3, HEAD_DIM).transpose(1, 2, 0, 3).reshape(-1, 3 * width)

    def join(values):
        return values.transpose(1, 0, 2).reshape(values.shape[1], -1)

    raw_qkv = join_qkv(owned[..., :head3])
    raw_expand = join(owned[..., head3:block_columns])
    dense_grad = join(owned[..., block_columns : block_columns + HEAD_DIM])
    shrink_grad = join(owned[..., block_columns + HEAD_DIM :])
    column_sums = owned_notes[:, :note_rows].reshape(HEADS, 1, block_columns)
    qkv_sum = join_qkv(column_sums[..., :head3])
    expand_sum = join(column_sums[..., head3:])
    bias_grad = jnp.sum(owned_notes[:, note_rows, :rows], 0)
    qkv_grad = gain_one[:, None] * raw_qkv + shift_one[:, None] * qkv_sum
    expand_grad = gain_two[:, None] * raw_expand + shift_two[:, None] * expand_sum

    def own(values, count):
        return lax.dynamic_slice_in_dim(values, me * count, count, 0)

    return (
        output,
        input_grad,
        jnp.sum(qkv_wide * raw_qkv, 1),
        jnp.sum(qkv_wide * qkv_sum, 1),
        jnp.sum(expand_wide * raw_expand, 1),
        jnp.sum(expand_wide * expand_sum, 1),
        qkv_grad,
        own(qkv_sum[0, : 2 * width], 2 * width // devices),
        own(qkv_sum[0, 2 * width :], width // devices),
        dense_grad,
        bias_grad,
        expand_grad,
        own(expand_sum[0], HEADS * hidden // devices),
        shrink_grad,
        bias_grad,
    )


def solution(mesh):
    matrix, vector = P(("head", "blk"), None), P(("head", "blk"))
    return jax.shard_map(
        per_device,
        mesh=mesh,
        in_specs=(
            matrix, vector, vector, vector, vector, matrix, vector, matrix, vector, matrix, vector, matrix, vector,
            P(), P(), vector, matrix,
        ),
        out_specs=(
            matrix, matrix, vector, vector, vector, vector, matrix, vector, vector, matrix, vector, matrix, vector,
            matrix, vector,
        ),
        check_vma=False,
    )
```

time: 3820 us -> 702 us (0.18)
  waiting for transfers between devices: 2870 us -> 0 us
  Pallas kernels: 0 us -> 501 us
  matrix products: 330 us -> 79.6 us
  local copies, waits for them, and re-layouts: 242 us -> 56.5 us
  blocking collectives: 156 us -> 0 us
  other arithmetic: 175 us -> 53.4 us
    unnamed x14 -> x0, waiting for transfers between devices: 2350 us -> none
    all_gather x8 -> x0, waiting for transfers between devices: 517 us -> none  [the longest x1 179 us: per_device(): lax.all_gather(shrink_weight, ('head', 'blk'), axis=0, tiled=True)]
    pallas_call x0 -> x7, Pallas kernels: none -> 501 us  [the longest x6 479 us: call(): pl.pallas_call(body, out_shape=out_shape, in_specs=[in_spec] * len(ins),...]
    dot_general x68 -> x12, matrix products: 330 us -> 79.6 us  [the longest x1 17.7 us: per_device(): jnp.dot(n_all, w_in[:, head3:], preferred_element_type=F32)]
    concatenate x3 -> x6, other arithmetic: 134 us -> 20.8 us  [the longest x1 15.1 us: per_device(): jnp.concatenate([lax.dot_general(n_all, right, tokens_dims, preferred_ele...]
    unnamed x89 -> x87, local copies, waits for them, and re-layouts: 114 us -> 7.09 us
    all_gather x3 -> x0, blocking collectives: 69.6 us -> none  [the longest x1 34.6 us: per_device(): lax.all_gather(expand_bias, ('head', 'blk'), axis=0, tiled=True)]
    dynamic_slice x96 -> x5, local copies, waits for them, and re-layouts: 52.3 us -> 1.77 us  [the longest x3 1.74 us: own(): return lax.dynamic_slice_in_dim(values, me * count, count, 0)]
  transfers between devices with their start and end apart: 13 -> 0, of which waited for: 9 -> 0; matrix products, arithmetic and copies ran while one was open for 16% -> 0% of each run, Pallas kernels for 0% -> 0%
where the time goes in v1:
time: 702 us; the launch traced here: 693 us
  Pallas kernels  501 us (71%)
  matrix products  79.6 us (11%)
  local copies, waits for them, and re-layouts  56.5 us (8%)
  other arithmetic  53.4 us (8%)
    pallas_call x6, Pallas kernels, call(): pl.pallas_call(body, out_shape=out_shape, in_specs=[in_spec] * len(ins),...  479 us
    pallas_call x1, Pallas kernels, attention(): pl.pallas_call(functools.partial(attention_kernel, prompt_runs, one_promp...  22.5 us
    dot_general x1, matrix products, per_device(): jnp.dot(n_all, w_in[:, head3:], preferred_element_type=F32)  17.7 us
    concatenate x1, local copies, waits for them, and re-layouts, per_device(): jnp.concatenate([lax.dot_general(n_all, right, tokens_dims, preferred_ele...  16.6 us
    concatenate x1, other arithmetic, per_device(): jnp.concatenate([lax.dot_general(n_all, right, tokens_dims, preferred_ele...  15.1 us

profile of v1, /device:TPU:8, one launch (start us, length us, event | category | flops | bytes accessed | tf_op | source)
XLA Modules:
  0.0 692.5 jit_solution(15965319911105831170)
XLA Ops:
  10.6 1.7 copy.156
  13.3 2.1 convolution_convert_fusion.4
  23.9 1.9 pad_maximum_fusion.2.w_in
  25.7 172.5 %shard_map.271 = (bf16[8,8,16,2048]{3,2,1,0:T(8,128)(2,1)}, bf16[8,8,16,2048]{3,2,1,0:T(8,128)(2,1)}, bf16[2,1,8,2,64,3072]{5,4,3,2,1,0:T(8,128)(2,1)}, f32[2,1,8,2,16,128]{5,4,3,2,1,0:T(8,128)}) custom-call(bf16[8,16,2048]{2,1,0:T(8,128)(2,1)} %bitcast.172, bf16[8,16,2048]{2,1,0:T(8,128)(2,1)} %bitcast.159, bf16[8,64,3072]{2,1,0:T(8,128)(2,1)} %pad_maximum_fusion.2.w_in, ...), custom_call_target="tpu_custom_call" | custom-call | tf_op jit(solution)/shard_map/pallas_call | solution.py:73
  202.1 4.7 convolution_convert_fusion.6
  206.8 5.5 fusion.32
  212.3 1.7 copy-done.10
  215.0 1.7 slice.271
  220.1 33.7 %shard_map.272 = bf16[8,4,128,512]{3,2,1,0:T(8,128)(2,1)} custom-call(bf16[8,128,512]{2,1,0:T(8,128)(2,1)} %bitcast.162), custom_call_target="tpu_custom_call" | custom-call | tf_op jit(solution)/shard_map/pallas_call | solution.py:73
  253.8 4.6 fusion.104
  258.4 22.5 %shard_map.273 = (bf16[8,128,256]{2,1,0:T(8,128)(2,1)}, f32[8,128,256]{2,1,0:T(8,128)}, f32[8,512,256]{2,1,0:T(8,128)}, f32[8,512,256]{2,1,0:T(8,128)}) custom-call(bf16[8,128,256]{2,1,0:T(8,128)(2,1)} %fusion.41.q_ref, bf16[8,128,256]{2,1,0:T(8,128)(2,1)} %bitcast.176, bf16[8,512,256]{2,1,0:T(8,128)(2,1)} %get-tuple-element.48.k_ref, ...), custom_call_target="tpu_custom_call" | custom-call | tf_op jit(solution)/shard_map/pallas_call | solution.py:639
  280.9 2.0 copy.127
  284.6 2.6 convert.46
  288.1 2.4 pad_maximum_fusion.1.part
  290.5 32.3 %shard_map.275 = f32[8,128,512]{2,1,0:T(8,128)} custom-call(bf16[8,4,128,512]{3,2,1,0:T(8,128)(2,1)} %pad_maximum_fusion.1.part), custom_call_target="tpu_custom_call" | custom-call | tf_op jit(solution)/shard_map/pallas_call | solution.py:73
  322.8 1.7 convert.51
  330.0 17.7 %multiply_convert_fusion = (bf16[1024,1024]{0,1:T(8,128)(2,1)}, f32[1024,1024]{0,1:T(8,128)}, f32[1024,1024]{0,1:T(8,128)}) fusion(f32[1024]{0:T(1024)S(1)} %slice_bitcast_fusion.4, bf16[1024,2048]{1,0:T(8,128)(2,1)S(1)} %bitcast.204, bf16[2048,3072]{1,0:T(8,128)(2,1)} %bitcast.199), kind=kOutput, calls=%fused_computation.16 | convolution fusion | flops 4364173312 | bytes 18878464 | tf_op jit(solution)/shard_map/dot_general | solution.py:790
  347.8 9.6 %fusion.29 = bf16[1024,1792]{0,1:T(8,128)(2,1)S(1)} fusion(bf16[1024,1792]{0,1:T(8,128)(2,1)S(1)} %constant_dynamic-update-slice_fusion, f32[1024,1024]{0,1:T(8,128)} %get-tuple-element.44, bf16[1024,2048]{1,0:T(8,128)(2,1)S(1)} %bitcast.207, bf16[2048,3072]{1,0:T(8,128)(2,1)} %bitcast.200, f32[1024,1024]{0,1:T(8,128)} %get-tuple-element.64, ...), kind=kOutput, calls=%fused_computation.57 | convolution fusion | flops 4310695936 | bytes 18878464 | tf_op jit(solution)/shard_map/dot_general | solution.py:793
  358.0 7.8 %convolution_convert_fusion = bf16[2048,1280]{0,1:T(8,128)(2,1)S(1)} fusion(bf16[1024,2048]{1,0:T(8,128)(2,1)S(1)} %bitcast.208, bf16[1024,1024]{0,1:T(8,128)(2,1)} %get-tuple-element.43, bf16[1024,256]{0,1:T(8,128)(2,1)S(1)} %copy-done.13), kind=kOutput, calls=%fused_computation.1 | convolution fusion | flops 5376573440 | bytes 12058624 | tf_op jit(solution)/shard_map/dot_general | solution.py:852
  365.8 9.7 %fusion.14 = bf16[1024,2048]{1,0:T(8,128)(2,1)} fusion(bf16[2048,3072]{1,0:T(8,128)(2,1)} %bitcast.201, bf16[1024,1024]{0,1:T(8,128)(2,1)S(1)} %copy-done.36, bf16[1024,256]{0,1:T(8,128)(2,1)S(1)} %copy-done.13), kind=kOutput, calls=%fused_computation.30 | convolution fusion | flops 5376049152 | bytes 12058624 | tf_op jit(solution)/shard_map/dot_general | solution.py:826
  375.5 11.5 %fusion.17 = bf16[1024,2048]{1,0:T(8,128)(2,1)} fusion(bf16[1024,1792]{0,1:T(8,128)(2,1)S(1)} %fusion.29, bf16[2048,3072]{1,0:T(8,128)(2,1)} %bitcast.202), kind=kOutput, calls=%fused_computation.31 | convolution fusion | flops 7518289920 | bytes 15204352 | tf_op jit(solution)/shard_map/dot_general | solution.py:842
  387.0 8.3 %convolution_convert_fusion.1 = bf16[2048,1792]{0,1:T(8,128)(2,1)S(1)} fusion(bf16[1024,1792]{0,1:T(8,128)(2,1)S(1)} %fusion.29, bf16[1024,2048]{1,0:T(8,128)(2,1)S(1)} %bitcast.205), kind=kOutput, calls=%fused_computation.2 | convolution fusion | flops 7519862784 | bytes 15204352 | tf_op jit(solution)/shard_map/dot_general | solution.py:851
  395.3 15.1 %pad_maximum_fusion = bf16[2048,3072]{0,1:T(8,128)(2,1)} fusion(bf16[2048,1280]{0,1:T(8,128)(2,1)S(1)} %convolution_convert_fusion, bf16[2048,1792]{0,1:T(8,128)(2,1)S(1)} %convolution_convert_fusion.1), kind=kLoop, calls=%fused_computation | loop fusion | flops 25165824 | bytes 25165824 | tf_op jit(solution)/shard_map/concatenate | solution.py:849
  410.4 16.6 %copy.132 = bf16[2048,3072]{1,0:T(8,128)(2,1)} copy(bf16[2048,3072]{0,1:T(8,128)(2,1)} %pad_maximum_fusion) | data formatting | bytes 25165824 | tf_op jit(solution)/shard_map/concatenate | solution.py:849
  427.0 76.3 %shard_map.276 = f32[8,16,2048]{2,1,0:T(8,128)} custom-call(bf16[8,8,16,2048]{3,2,1,0:T(8,128)(2,1)} %bitcast.161), custom_call_target="tpu_custom_call" | custom-call | tf_op jit(solution)/shard_map/pallas_call | solution.py:73
  503.4 65.2 %shard_map.274 = f32[8,16,2048]{2,1,0:T(8,128)} custom-call(bf16[8,8,16,2048]{3,2,1,0:T(8,128)(2,1)} %bitcast.160), custom_call_target="tpu_custom_call" | custom-call | tf_op jit(solution)/shard_map/pallas_call | solution.py:73
  569.2 2.0 fusion.39
  574.3 98.5 %shard_map.277 = (bf16[8,64,3072]{2,1,0:T(8,128)(2,1)}, f32[8,16,128]{2,1,0:T(8,128)}) custom-call(bf16[2,1,8,2,64,3072]{5,4,3,2,1,0:T(8,128)(2,1)} %bitcast.149, f32[2,1,8,2,16,128]{5,4,3,2,1,0:T(8,128)} %bitcast.173), custom_call_target="tpu_custom_call" | custom-call | tf_op jit(solution)/shard_map/pallas_call | solution.py:73
  676.3 2.4 slice.198
  678.7 2.6 reshape.651
  682.8 2.2 fusion.38
  689.1 2.5 fusion.28
  (192 shorter events, 49.0 us)
Async XLA Ops:
  0.6 18.1 %copy-start = (bf16[128,2048]{1,0:T(8,128)(2,1)S(1)}, bf16[128,2048]{1,0:T(8,128)(2,1)}, u32[]{:S(2)}) copy-start(bf16[128,2048]{1,0:T(8,128)(2,1)} %param.17) | copy-start | bytes 1572868
  0.7 16.3 %copy-start.31 = (bf16[192]{0:T(256)(128)(2,1)S(1)}, bf16[192]{0:T(256)(128)(2,1)}, u32[]{:S(2)}) copy-start(bf16[192]{0:T(256)(128)(2,1)} %param.23) | copy-start | bytes 1156
  1.5 17.2 %copy-start.17 = (s32[128]{0:T(128)}, s32[128]{0:T(128)S(1)}, u32[]{:S(2)}) copy-start(s32[128]{0:T(128)S(1)} %fusion.100) | copy-start | bytes 1540
  3.6 15.1 %copy-start.21 = (f32[64]{0:T(128)}, f32[64]{0:T(128)S(1)}, u32[]{:S(2)}) copy-start(f32[64]{0:T(128)S(1)} %convert_element_type.135) | copy-start | bytes 772
  4.3 14.5 %copy-start.23 = (f32[64]{0:T(128)}, f32[64]{0:T(128)S(1)}, u32[]{:S(2)}) copy-start(f32[64]{0:T(128)S(1)} %convert_element_type.140) | copy-start | bytes 772
  4.9 16.1 %copy-start.25 = (f32[64]{0:T(128)}, f32[64]{0:T(128)S(1)}, u32[]{:S(2)}) copy-start(f32[64]{0:T(128)S(1)} %convert_element_type.138) | copy-start | bytes 772
  5.6 15.5 %copy-start.27 = (f32[64]{0:T(128)}, f32[64]{0:T(128)S(1)}, u32[]{:S(2)}) copy-start(f32[64]{0:T(128)S(1)} %convert_element_type.142) | copy-start | bytes 772
  17.3 3.7 copy-start.8
  17.8 3.8 copy-start.32
  19.1 4.7 copy-start.15
  19.4 4.5 copy-start.12
  20.1 5.6 copy-start.19
  202.1 4.7 copy-start.33
  214.8 3.5 slice-start
  284.4 3.5 copy-start.7
  330.0 17.7 %copy-start.35 = (bf16[8,8,16,2048]{3,2,1,0:T(8,128)(2,1)S(1)}, bf16[8,8,16,2048]{3,2,1,0:T(8,128)(2,1)}, u32[]{:S(2)}) copy-start(bf16[8,8,16,2048]{3,2,1,0:T(8,128)(2,1)} %get-tuple-element.28) | copy-start | bytes 12582916
  347.8 10.2 %copy-start.13 = (bf16[1024,256]{0,1:T(8,128)(2,1)S(1)}, bf16[1024,256]{0,1:T(8,128)(2,1)}, u32[]{:S(2)}) copy-start(bf16[1024,256]{0,1:T(8,128)(2,1)} %copy.127) | copy-start | bytes 1572868
  358.0 7.8 %copy-start.36 = (bf16[1024,1024]{0,1:T(8,128)(2,1)S(1)}, bf16[1024,1024]{0,1:T(8,128)(2,1)}, u32[]{:S(2)}) copy-start(bf16[1024,1024]{0,1:T(8,128)(2,1)} %get-tuple-element.43) | copy-start | bytes 6291460
  427.0 141.6 %copy-start.3 = (f32[128,2048]{1,0:T(8,128)S(1)}, f32[128,2048]{1,0:T(8,128)}, u32[]{:S(2)}) copy-start(f32[128,2048]{1,0:T(8,128)} %copy-done.2) | copy-start | bytes 3145732
  427.0 141.6 %copy-start.16 = (f32[128]{0:T(128)S(1)}, f32[128]{0:T(128)}, u32[]{:S(2)}) copy-start(f32[128]{0:T(128)} %copy-done.15) | copy-start | bytes 1540
  427.0 141.6 %copy-start.20 = (f32[128]{0:T(128)S(1)}, f32[128]{0:T(128)}, u32[]{:S(2)}) copy-start(f32[128]{0:T(128)} %copy-done.19) | copy-start | bytes 1540
  503.4 65.2 %copy-start.4 = (f32[8,16,2048]{2,1,0:T(8,128)S(1)}, f32[8,16,2048]{2,1,0:T(8,128)}, u32[]{:S(2)}) copy-start(f32[8,16,2048]{2,1,0:T(8,128)} %shard_map.276) | copy-start | bytes 3145732
  503.4 65.8 %copy-start.6 = (bf16[128,2048]{1,0:T(8,128)(2,1)S(1)}, bf16[128,2048]{1,0:T(8,128)(2,1)}, u32[]{:S(2)}) copy-start(bf16[128,2048]{1,0:T(8,128)(2,1)} %convolution_convert_fusion.4) | copy-start | bytes 1572868
  503.4 65.8 %copy-start.14 = (f32[2048]{0:T(1024)S(1)}, f32[2048]{0:T(1024)}, u32[]{:S(2)}) copy-start(f32[2048]{0:T(1024)} %add.330) | copy-start | bytes 24580
  568.6 2.5 copy-start.18
  568.9 4.6 copy-start.29
  673.6 18.0 %copy-start.30 = (f32[64]{0:T(128)}, f32[64]{0:T(128)S(1)}, u32[]{:S(2)}) copy-start(f32[64]{0:T(128)S(1)} %slice_reduce_fusion.2) | copy-start | bytes 772
  682.3 2.7 copy-start.5
  686.6 2.5 copy-start.9
  686.6 2.5 copy-start.26
  686.6 2.5 copy-start.28
  688.9 3.2 copy-start.1
  (6 other events, 9.4 us)

commit v2 on v1

--- a/solution.py
+++ b/solution.py
@@ -317,15 +317,35 @@
     )
 
 
-def fold_kernel(ways, part, total, from_c, from_x, from_w, s_c, r_c, s_x, r_x, s_w, r_w):
+def turn(u, tables, sign):
+    cosine, lower, upper = tables
+    front = u[:, :128]
+    moved = pltpu.roll(front, 96, 1) * lower + pltpu.roll(front, 32, 1) * upper
+    return jnp.concatenate([front * cosine + moved * sign, u[:, 128:]], 1)
+
+
+def finish_kernel(ways, att, act, dexp, dq, dkv, tables, w_out, w_in, n_all, g_all, note,
+                  out_sum, e_sum, own_a, own_b, note_all,
+                  v_left, v_right, v_w, v_turn, kv_own, kv_c, kv_x,
+                  o_p, o_y, o_1, o_2, e_p, e_y, e_1, e_2,
+                  raw, flat, ring, a_c, a_x, a_w, b_c, b_x, b_w, n_mine, n_c, n_x, n_w,
+                  load, load_raw, kv_load, kv_s, kv_r, kvx_s, kvx_r,
+                  oy_s, oy_r, o1_s, o1_r, o2_s, o2_r, ey_s, ey_r, e1_s, e1_r, e2_s, e2_r,
+                  ac_s, ac_r, ax_s, ax_r, aw_s, aw_r, ah_s, ah_r,
+                  bc_s, bc_r, bx_s, bx_r, bw_s, bw_r, bh_s, bh_r, keep, n_s, n_r):
     place = Place(ways)
-    x, w, c = place.x, place.w, place.c
-    runs = part.shape[0]
-    greet(place.peers_w() + [place.peer_x(), place.peer_c()])
-
-    def slot(ws, xs, cs):
-        return ws * 4 + xs * 2 + cs
-
+    x, w, h, c, hy, hz = place.x, place.w, place.h, place.c, place.hy, place.hz
+    d0, d1 = hz % 2, hz // 2
+    runs = v_left.shape[0]
+    chunks = o_p.shape[0]
+    wide = o_p.shape[-1]
+    rows = own_a.shape[1]
+    hp = 256 // (2 * rows)
+    tiles = HEADS // hp
+    a_cols, b_cols = own_a.shape[2], own_b.shape[2]
+    inner = w_out.shape[1]
+    head3 = 3 * HEAD_DIM
+    group = runs * HEADS * STRIPE
     sends = []
 
     def send(src, dst, s, r, device):
@@ -334,246 +354,423 @@
         sends.append(copy)
         return copy
 
-    order = [(w + k) % ways for k in range(1, ways)] + [w]
-    first = []
-    for i, ws in enumerate(order):
-        for xs, k in ((1 - x, 0), (x, 1)):
-            first.append(
-                send(part.at[:, slot(ws, xs, 1 - c)], from_c.at[:, i, k], s_c.at[i, k], r_c.at[i, k], place.peer_c())
+    greet(place.peers_h() + place.peers_w() + [place.peer_x(), place.peer_c()])
+
+    def fetch(src, dst, k):
+        copy = pltpu.make_async_copy(src, dst, load.at[k])
+        copy.start()
+        return copy
+
+    early = [
+        fetch(att, v_left.at[..., :HEAD_DIM], 0),
+        fetch(act, v_left.at[..., HEAD_DIM:], 1),
+        fetch(w_out, v_w.at[:, :inner], 2),
+    ]
+
+    kv_first, kv_mine = [], []
+    for k, xs in ((0, 1 - x), (1, x)):
+        kv_first.append(send(dkv.at[:, xs * 2 + 1 - c], kv_c.at[:, k], kv_s.at[k], kv_r.at[k], place.peer_c()))
+        kv_mine.append(pltpu.make_async_copy(dkv.at[:, xs * 2 + c], kv_own.at[:, k], kv_load.at[k]))
+        kv_mine[k].start()
+    late = [
+        fetch(dexp, v_right.at[..., head3:], 3),
+        fetch(dq, v_right.at[..., :HEAD_DIM], 4),
+        fetch(tables, v_turn, 5),
+    ]
+
+    def partial(src, q, buf, depth):
+        @pl.loop(0, wide // 256)
+        def _(k):
+            at = pl.multiple_of(k * 256, 256)
+            value = lax.dot_general(
+                src[...].reshape(group, depth),
+                v_w[pl.ds(pl.multiple_of(q * wide + at, 256), 256), :depth],
+                (((1,), (1,)), ((), ())),
+                preferred_element_type=F32,
             )
-
-    def add(i, k, ws, xs, extra):
+            buf[q, :, :, :, :, :, pl.ds(at, 256)] = value.astype(BF).reshape(runs, 2, 2, 2, STRIPE, 256)
+
+    def sums(buf, y, one, two, s_y, r_y, s_1, r_1, s_2, r_2, total):
+        def start(q):
+            return send(buf.at[q, :, :, :, 1 - hy], y.at[q], s_y.at[q], r_y.at[q], place.peer_y())
+
+        def after_y(q, copy):
+            copy.wait_recv()
+
+            @pl.loop(0, runs)
+            def _(run):
+                for t in range(LINE):
+                    value = y[q, run, t // 2, t % 2].astype(F32) + buf[q, run, t // 2, t % 2, hy].astype(F32)
+                    y[q, run, t // 2, t % 2] = value.astype(BF)
+
+            target = place.device(h=(hz + 1 - 2 * d0) * 2 + hy)
+            return send(y.at[q, :, :, 1 - d0], one.at[q], s_1.at[q], r_1.at[q], target)
+
+        def after_1(q, copy):
+            copy.wait_recv()
+
+            @pl.loop(0, runs)
+            def _(run):
+                for t in range(2):
+                    value = one[q, run, t].astype(F32) + y[q, run, t, d0].astype(F32)
+                    one[q, run, t] = value.astype(BF)
+
+            target = place.device(h=((1 - d1) * 2 + d0) * 2 + hy)
+            return send(one.at[q, :, 1 - d1], two.at[q], s_2.at[q], r_2.at[q], target)
+
+        def after_2(q, copy):
+            copy.wait_recv()
+
+            @pl.loop(0, runs)
+            def _(run):
+                total[run, :, q * wide : (q + 1) * wide] = two[q, run].astype(F32) + one[q, run, d1].astype(F32)
+
+        return start, after_y, after_1, after_2
+
+    o_start, o_after_y, o_after_1, o_after_2 = sums(o_p, o_y, o_1, o_2, oy_s, oy_r, o1_s, o1_r, o2_s, o2_r, out_sum)
+    e_start, e_after_y, e_after_1, e_after_2 = sums(e_p, e_y, e_1, e_2, ey_s, ey_r, e1_s, e1_r, e2_s, e2_r, e_sum)
+
+    for copy in early:
+        copy.wait()
+    o_step = {}
+    for q in range(chunks):
+        partial(v_left, q, o_p, inner)
+        o_step[q] = o_start(q)
+    w_load = fetch(w_in, v_w, 6)
+
+    def kv_add(k, final):
+        kv_mine[k].wait()
+        kv_first[k].wait_recv()
+
         @pl.loop(0, runs)
         def _(run):
-            value = part[run, slot(ws, xs, c)].astype(F32) + from_c[run, i, k].astype(F32)
-            if extra:
-                value = value + from_x[run, i].astype(F32)
-            if extra and i == ways - 1:
-                for q in range(ways - 1):
-                    value = value + from_w[run, q].astype(F32)
-                total[run] = value
+            value = kv_own[run, k].astype(F32) + kv_c[run, k].astype(F32)
+            if final:
+                value = value + kv_x[run].astype(F32)
+                back = turn(value[:, :HEAD_DIM].astype(BF).astype(F32), [v_turn[t, run] for t in range(3)], -1.0)
+                shape = (LINE, 2, STRIPE, HEAD_DIM)
+                v_right[run, :, :, :, HEAD_DIM : 2 * HEAD_DIM] = back.astype(BF).reshape(shape)
+                v_right[run, :, :, :, 2 * HEAD_DIM : head3] = value[:, HEAD_DIM:].astype(BF).reshape(shape)
             else:
-                from_c[run, i, k] = value.astype(BF)
-
-    for i, ws in enumerate(order):
-        first[2 * i].wait_recv()
-        add(i, 0, ws, 1 - x, False)
-        send(from_c.at[:, i, 0], from_x.at[:, i], s_x.at[i], r_x.at[i], place.peer_x())
-    for i, ws in enumerate(order):
-        first[2 * i + 1].wait_recv()
-        remote(from_x.at[:, i], from_x.at[:, i], s_x.at[i], r_x.at[i], place.peer_x()).wait_recv()
-        if i == ways - 1:
-            for q in range(ways - 1):
-                remote(from_w.at[:, q], from_w.at[:, q], s_w.at[q], r_w.at[q], place.peer_x()).wait_recv()
-        add(i, 1, ws, x, True)
-        if i < ways - 1:
-            send(from_c.at[:, i, 1], from_w.at[:, i], s_w.at[i], r_w.at[i], place.device(w=ws))
+                kv_c[run, k] = value.astype(BF)
+
+    kv_add(0, False)
+    kv_second = remote(kv_c.at[:, 0], kv_x, kvx_s.at[0], kvx_r.at[0], place.peer_x())
+    kv_second.start()
+    for copy in late:
+        copy.wait()
+
+    order_t = [(k, dw, dt) for k in range(2) for dw in list(range(1, ways)) + [0] for dt in list(range(1, tiles)) + [0]]
+    own_t = h // hp
+
+    def where(k, dw, dt):
+        return (1 - x if k == 0 else x), (w + dw) % ways, (own_t + dt) % tiles
+
+    def raw_copy(n, src, buf):
+        xs, ws, t = where(*order_t[n])
+        at = pl.multiple_of(((xs * ways + ws) * tiles + t) * 256, 256)
+        return pltpu.make_async_copy(src.at[:, pl.ds(at, 256)], raw.at[n % 2, buf], load_raw.at[n % 2, buf])
+
+    def product(n, buf, src, first, count, at):
+        flat[...] = raw[n % 2, buf].T
+
+        @pl.loop(0, count // 256)
+        def _(k):
+            col = pl.multiple_of(k * 256, 256)
+            value = jnp.dot(
+                flat[...], src[..., pl.ds(first + col, 256)].reshape(group, 256), preferred_element_type=F32
+            )
+            ring[n % 3, :, :, :, pl.ds(at + col, 256)] = value.astype(BF).reshape(hp, 2, rows, 256)
+
+    def grads(cols, from_c, from_x, from_w, c_s, c_r, x_s, x_r, w_s, w_r, h_s, h_r, out, fill, need, flag):
+        first, second, third, last = {}, {}, {}, []
+
+        def begin(n):
+            for buf, src in need:
+                raw_copy(n, src, buf).start()
+
+        def make(n):
+            if n >= 3:
+                first[n - 3].wait_send()
+            for buf, src in need:
+                raw_copy(n, src, buf).wait()
+            fill(n)
+            if n + 1 < len(order_t):
+                begin(n + 1)
+            k, dw, dt = order_t[n]
+            first[n] = remote(
+                ring.at[n % 3, :, 1 - c, :, pl.ds(0, cols)], from_c.at[k, dw, dt], c_s.at[n], c_r.at[n], place.peer_c()
+            )
+            first[n].start()
+
+        def mine(n):
+            k, dw, dt = order_t[n]
+            first[n].wait_recv()
+
+            @pl.loop(0, hp)
+            def _(q):
+                value = from_c[k, dw, dt, q].astype(F32) + ring[n % 3, q, c, :, :cols].astype(F32)
+                from_c[k, dw, dt, q] = value.astype(BF)
+
+        def cross(n):
+            k, dw, dt = order_t[n]
+            second[dw, dt] = send(from_c.at[0, dw, dt], from_x.at[dw, dt], x_s.at[dw, dt], x_r.at[dw, dt], place.peer_x())
+
+        def close(n):
+            k, dw, dt = order_t[n]
+            _, ws, t = where(k, dw, dt)
+            second[dw, dt].wait_recv()
+            more = [from_x.at[dw, dt]]
+            if dw == 0:
+                for dv in range(1, ways):
+                    third[dv, dt].wait_recv()
+                    more.append(from_w.at[dv - 1, dt])
+
+            @pl.loop(0, hp)
+            def _(q):
+                value = from_c[1, dw, dt, q].astype(F32)
+                for ref in more:
+                    value = value + ref[q].astype(F32)
+                from_c[1, dw, dt, q] = value.astype(BF)
+
+            if dw != 0:
+                third[dw, dt] = send(from_c.at[1, dw, dt], from_w.at[dw - 1, dt], w_s.at[dw - 1, dt], w_r.at[dw - 1, dt], place.device(w=ws))
+                return
+            for q in range(hp):
+                hs = t * hp + q
+                at = dt * hp + q
+
+                @pl.when(hs != h)
+                def _():
+                    remote(from_c.at[1, 0, dt, q], out.at[h], h_s.at[at], h_r.at[h], place.device(h=hs)).start()
+
+                @pl.when(hs == h)
+                def _():
+                    pltpu.make_async_copy(from_c.at[1, 0, dt, q], out.at[h], keep.at[flag]).start()
+
+        def drain():
+            for n in range(max(len(order_t) - 3, 0), len(order_t)):
+                first[n].wait_send()
+
+        def end():
+            for n in range(len(order_t)):
+                k, dw, dt = order_t[n]
+                if k == 1 and dw == 0:
+                    _, _, t = where(k, dw, dt)
+                    for q in range(hp):
+                        hs = t * hp + q
+
+                        @pl.when(hs != h)
+                        def _():
+                            remote(from_c.at[1, 0, dt, q], out.at[h], h_s.at[dt * hp + q], h_r.at[h], place.device(h=hs)).wait_send()
+            for dh in range(1, HEADS):
+                hs = (h + dh) % HEADS
+                remote(out.at[hs], out.at[hs], h_s.at[0], h_r.at[hs], place.peer_x()).wait_recv()
+            pltpu.make_async_copy(from_c.at[1, 0, 0, 0], out.at[h], keep.at[flag]).wait()
+
+        return begin, make, mine, cross, close, drain, end
+
+    def fill_a(n):
+        product(n, 1, v_left, 0, inner, 0)
+        product(n, 0, v_right, head3, a_cols - inner, inner)
+
+    def fill_b(n):
+        product(n, 0, v_right, 0, head3, 0)
+
+    a_begin, a_make, a_mine, a_cross, a_close, a_drain, a_end = grads(
+        a_cols, a_c, a_x, a_w, ac_s, ac_r, ax_s, ax_r, aw_s, aw_r, ah_s, ah_r, own_a, fill_a, ((0, n_all), (1, g_all)), 0
+    )
+    b_begin, b_make, b_mine, b_cross, b_close, b_drain, b_end = grads(
+        b_cols, b_c, b_x, b_w, bc_s, bc_r, bx_s, bx_r, bw_s, bw_r, bh_s, bh_r, own_b, fill_b, ((0, n_all),), 1
+    )
+    count = len(order_t)
+    half = count // 2
+    a_begin(0)
+    for n in range(half):
+        a_make(n)
+        a_mine(n)
+        if n == 0:
+            kv_second.wait_send()
+        a_cross(n)
+        if n == 1:
+            o_step[0] = o_after_y(0, o_step[0])
+    o_step[1] = o_after_y(1, o_step[1])
+    o_step[0] = o_after_1(0, o_step[0])
+
+    kv_second.wait_recv()
+    kv_add(1, True)
+    w_load.wait()
+    e_step = {}
+    for q in range(chunks):
+        partial(v_right, q, e_p, v_right.shape[-1])
+        e_step[q] = e_start(q)
+        if q == 1:
+            o_step[2] = o_after_y(2, o_step[2])
+            o_step[1] = o_after_1(1, o_step[1])
+    o_after_2(0, o_step[0])
+
+    def fold_columns(first, cols, row):
+        @pl.loop(0, cols // 128)
+        def _(k):
+            at = pl.multiple_of(k * 128, 128)
+            value = v_right[..., pl.ds(first + at, 128)].reshape(group, 128).astype(F32)
+            n_mine[pl.ds(row + k, 1), :] = jnp.sum(value, 0, keepdims=True)
+
+    n_load = pltpu.make_async_copy(note, n_mine, keep.at[2])
+    n_load.start()
+    n_load.wait()
+    fold_columns(0, v_right.shape[-1], 0)
+    note_copy = send(n_mine, n_c, n_s.at[0], n_r.at[0], place.peer_c())
+
+    note_w = []
+    for n in range(half, count):
+        a_make(n)
+        a_mine(n)
+        if n == half:
+            note_copy.wait_recv()
+            n_c[...] = n_c[...] + n_mine[...]
+            note_copy = send(n_c, n_x, n_s.at[1], n_r.at[1], place.peer_x())
+        a_close(n)
+        if n == half + 1:
+            note_copy.wait_recv()
+            n_x[...] = n_x[...] + n_c[...]
+            for k, device in enumerate(place.peers_w()):
+                note_w.append(send(n_x, n_w.at[k], n_s.at[2 + k], n_r.at[2 + k], device))
+            o_step[3] = o_after_y(3, o_step[3])
+            o_step[2] = o_after_1(2, o_step[2])
+    o_after_2(1, o_step[1])
+    o_step[3] = o_after_1(3, o_step[3])
+    for k, copy in enumerate(note_w):
+        copy.wait()
+    total = n_x[...]
+    for k in range(ways - 1):
+        total = total + n_w[k]
+    n_x[...] = total
+    base = 1 + ways
+    for dh in range(1, HEADS):
+        send(n_x, note_all.at[h], n_s.at[base + dh], n_r.at[base + h], place.device(h=(h + dh) % HEADS))
+    n_keep = pltpu.make_async_copy(n_x, note_all.at[h], keep.at[3])
+    n_keep.start()
+
+    a_drain()
+    b_begin(0)
+    for n in range(half):
+        b_make(n)
+        b_mine(n)
+        b_cross(n)
+        if n == 0:
+            e_step[0] = e_after_y(0, e_step[0])
+        if n == 1:
+            o_after_2(2, o_step[2])
+    e_step[1] = e_after_y(1, e_step[1])
+    e_step[0] = e_after_1(0, e_step[0])
+    o_after_2(3, o_step[3])
+    for n in range(half, count):
+        b_make(n)
+        b_mine(n)
+    e_step[2] = e_after_y(2, e_step[2])
+    e_step[1] = e_after_1(1, e_step[1])
+    e_after_2(0, e_step[0])
+    for n in range(half, count):
+        b_close(n)
+    e_step[3] = e_after_y(3, e_step[3])
+    e_step[2] = e_after_1(2, e_step[2])
+    e_after_2(1, e_step[1])
+    e_step[3] = e_after_1(3, e_step[3])
+    e_after_2(2, e_step[2])
+    e_after_2(3, e_step[3])
+    a_end()
+    b_drain()
+    b_end()
+    n_keep.wait()
+    for dh in range(1, HEADS):
+        hs = (h + dh) % HEADS
+        remote(note_all.at[hs], note_all.at[hs], n_s.at[0], n_r.at[base + hs], place.peer_x()).wait_recv()
     for copy in sends:
-        copy.wait_send()
-
-
-def fold(ways, part):
-    runs, _, rows, columns = part.shape
+        if not any(copy is other for other in note_w):
+            copy.wait_send()
+
+
+def finish(ways, rows, att, act, dexp, dq, dkv, tables, w_out, w_in, n_all, g_all, note):
+    width, inner = w_out.shape
+    right = w_in.shape[1]
+    head3 = 3 * HEAD_DIM
+    a_cols, b_cols = inner + right - head3, head3
+    group = n_all.shape[0]
+    runs, _, per_run, pair = dkv.shape
+    lines = (runs, LINE, 2, STRIPE)
+    hp = 256 // (2 * rows)
+    tiles = HEADS // hp
+    chunks, wide = 4, width // 4
     extra = max(ways - 1, 1)
-    return call(
-        functools.partial(fold_kernel, ways),
-        jax.ShapeDtypeStruct((runs, rows, columns), F32),
-        (part,),
+    count = 2 * ways * tiles
+
+    def vm(shape, kind=BF):
+        return pltpu.VMEM(shape, kind)
+
+    def row_buffers():
+        return [
+            vm((chunks, runs, 2, 2, 2, STRIPE, wide)),
+            vm((chunks, runs, 2, 2, STRIPE, wide)),
+            vm((chunks, runs, 2, STRIPE, wide)),
+            vm((chunks, runs, STRIPE, wide)),
+        ]
+
+    def spare(shape):
+        return shape if ways > 1 else (1,) * (len(shape) - 2) + (16, 128)
+
+    def gradient_buffers(cols):
+        return [
+            vm((2, ways, tiles, hp, rows, cols)),
+            vm((ways, tiles, hp, rows, cols)),
+            vm(spare((extra, tiles, hp, rows, cols))),
+        ]
+
+    def gradient_sems():
+        return [
+            DMA((count,)), DMA((count,)), DMA((ways, tiles)), DMA((ways, tiles)), DMA((extra, tiles)), DMA((extra, tiles)),
+            DMA((HEADS,)), DMA((HEADS,)),
+        ]
+
+    scratch = (
         [
-            pltpu.VMEM((runs, ways, 2, rows, columns), BF),
-            pltpu.VMEM((runs, ways, rows, columns), BF),
-            pltpu.VMEM((runs, extra, rows, columns), BF),
-            DMA((ways, 2)), DMA((ways, 2)), DMA((ways,)), DMA((ways,)), DMA((extra,)), DMA((extra,)),
-        ],
-        2,
-        VMEM,
-        VMEM,
-    )
-
-
-def collect_kernel(ways, part, total, from_y, from_z, s_y, r_y, s_z, r_z):
-    place = Place(ways)
-    hz, hy = place.hz, place.hy
-    runs = part.shape[0]
-    others = [(hz + k) % LINE for k in range(1, LINE)]
-    greet([place.peer_y()] + [place.device(h=z * 2 + hy) for z in others])
-    order = others + [hz]
-    sends, first = [], []
-    for i, z in enumerate(order):
-        copy = remote(part.at[:, z * 2 + 1 - hy], from_y.at[:, i], s_y.at[i], r_y.at[i], place.peer_y())
-        copy.start()
-        sends.append(copy)
-    for i, z in enumerate(order):
-        sends[i].wait_recv()
-        if i < LINE - 1:
-            @pl.loop(0, runs)
-            def _(run):
-                value = part[run, z * 2 + hy].astype(F32) + from_y[run, i].astype(F32)
-                from_y[run, i] = value.astype(BF)
-
-            copy = remote(from_y.at[:, i], from_z.at[:, i], s_z.at[i], r_z.at[i], place.device(h=z * 2 + hy))
-            copy.start()
-            first.append(copy)
-    for copy in first:
-        copy.wait_recv()
-
-    @pl.loop(0, runs)
-    def _(run):
-        value = part[run, hz * 2 + hy].astype(F32) + from_y[run, LINE - 1].astype(F32)
-        for i in range(LINE - 1):
-            value = value + from_z[run, i].astype(F32)
-        total[run] = value
-
-    for copy in sends + first:
-        copy.wait_send()
-
-
-def collect(ways, part, ident):
-    runs, _, rows, width = part.shape
-    return call(
-        functools.partial(collect_kernel, ways),
-        jax.ShapeDtypeStruct((runs, rows, width), F32),
-        (part,),
-        [
-            pltpu.VMEM((runs, LINE, rows, width), BF),
-            pltpu.VMEM((runs, LINE - 1, rows, width), BF),
-            DMA((LINE,)), DMA((LINE,)), DMA((LINE - 1,)), DMA((LINE - 1,)),
-        ],
-        ident,
-        VMEM,
-        VMEM,
-    )
-
-
-def owners_kernel(ways, part, note, out, note_out, from_c, from_x, from_w, note_c, note_x, note_w,
-                  local, s_c, r_c, s_x, r_x, s_w, r_w, s_h, r_h, ns_c, nr_c, ns_x, nr_x, ns_w, nr_w, ns_h, nr_h):
-    place = Place(ways)
-    x, w, h, c = place.x, place.w, place.h, place.c
-    rows = part.shape[4]
-    piece = min(rows, 16)
-    greet(place.peers_h() + place.peers_w() + [place.peer_x(), place.peer_c()])
-    order = [(dw, dh) for dh in list(range(1, HEADS)) + [0] for dw in list(range(1, ways)) + [0]]
-    sends = []
-
-    def send(src, dst, s, r, device):
-        copy = remote(src, dst, s, r, device)
-        copy.start()
-        sends.append(copy)
-        return copy
-
-    def both(src, nsrc, dst, ndst, s, ns, r, nr, device):
-        return send(src, dst, s, r, device), send(nsrc, ndst, ns, nr, device)
-
-    first = {}
-    for k, xs in ((0, 1 - x), (1, x)):
-        for dw, dh in order:
-            ws, hs = (w + dw) % ways, (h + dh) % HEADS
-            first[k, dw, dh] = both(
-                part.at[xs, ws, hs, 1 - c], note.at[xs, ws, hs, 1 - c],
-                from_c.at[k, dw, dh], note_c.at[k, dw, dh],
-                s_c.at[k, dw, dh], ns_c.at[k, dw, dh], r_c.at[k, dw, dh], nr_c.at[k, dw, dh], place.peer_c(),
-            )
-
-    def add(k, dw, dh, xs, more):
-        ws, hs = (w + dw) % ways, (h + dh) % HEADS
-
-        @pl.loop(0, rows // piece)
-        def _(q):
-            at = pl.ds(pl.multiple_of(q * piece, piece), piece)
-            value = part[xs, ws, hs, c, at].astype(F32) + from_c[k, dw, dh, at].astype(F32)
-            for ref in more:
-                value = value + ref[at].astype(F32)
-            from_c[k, dw, dh, at] = value.astype(BF)
-
-    second = {}
-    for dw, dh in order:
-        ws, hs = (w + dw) % ways, (h + dh) % HEADS
-        for copy in first[0, dw, dh]:
-            copy.wait_recv()
-        add(0, dw, dh, 1 - x, [])
-        note_c[0, dw, dh] = note_c[0, dw, dh] + note[1 - x, ws, hs, c]
-        second[dw, dh] = both(
-            from_c.at[0, dw, dh], note_c.at[0, dw, dh], from_x.at[dw, dh], note_x.at[dw, dh],
-            s_x.at[dw, dh], ns_x.at[dw, dh], r_x.at[dw, dh], nr_x.at[dw, dh], place.peer_x(),
-        )
-    third = {}
-    last = []
-    for dw, dh in order:
-        ws, hs = (w + dw) % ways, (h + dh) % HEADS
-        for copy in first[1, dw, dh] + second[dw, dh]:
-            copy.wait_recv()
-        more = [from_x.at[dw, dh]]
-        summed = note_c[1, dw, dh] + note[x, ws, hs, c] + note_x[dw, dh]
-        if dw == 0:
-            for dv in range(1, ways):
-                for copy in third[dv, dh]:
-                    copy.wait_recv()
-                more.append(from_w.at[dv - 1, dh])
-                summed = summed + note_w[dv - 1, dh]
-        add(1, dw, dh, x, more)
-        note_c[1, dw, dh] = summed
-        if dw != 0:
-            third[dw, dh] = both(
-                from_c.at[1, dw, dh], note_c.at[1, dw, dh], from_w.at[dw - 1, dh], note_w.at[dw - 1, dh],
-                s_w.at[dw - 1, dh], ns_w.at[dw - 1, dh], r_w.at[dw - 1, dh], nr_w.at[dw - 1, dh], place.device(w=ws),
-            )
-        elif dh != 0:
-            last.append(both(
-                from_c.at[1, 0, dh], note_c.at[1, 0, dh], out.at[h], note_out.at[h],
-                s_h.at[dh], ns_h.at[dh], r_h.at[h], nr_h.at[h], place.device(h=hs),
-            ))
-        else:
-            keep = [
-                pltpu.make_async_copy(from_c.at[1, 0, 0], out.at[h], local.at[0]),
-                pltpu.make_async_copy(note_c.at[1, 0, 0], note_out.at[h], local.at[1]),
-            ]
-            for copy in keep:
-                copy.start()
-    for dh in range(1, HEADS):
-        hs = (h - dh) % HEADS
-        remote(out.at[hs], out.at[hs], s_h.at[0], r_h.at[hs], place.peer_x()).wait_recv()
-        remote(note_out.at[hs], note_out.at[hs], ns_h.at[0], nr_h.at[hs], place.peer_x()).wait_recv()
-    for copy in keep:
-        copy.wait()
-    for copy in sends:
-        copy.wait_send()
-
-
-def to_owners(ways, part, note):
-    rows, columns = part.shape[4:]
-    extra = max(ways - 1, 1)
-
-    def sems():
-        return [
-            DMA((2, ways, HEADS)), DMA((2, ways, HEADS)), DMA((ways, HEADS)), DMA((ways, HEADS)),
-            DMA((extra, HEADS)), DMA((extra, HEADS)), DMA((HEADS,)), DMA((HEADS,)),
+            vm(lines + (inner,)), vm(lines + (right,)), vm((width, right)), vm(tables.shape, F32),
+            vm((runs, 2, per_run, pair)), vm((runs, 2, per_run, pair)), vm((runs, per_run, pair)),
         ]
-
-    def slots(shape, kind):
-        return [
-            pltpu.VMEM((2, ways, HEADS) + shape, kind),
-            pltpu.VMEM((ways, HEADS) + shape, kind),
-            pltpu.VMEM((extra, HEADS) + shape if ways > 1 else (1, 1) + shape, kind),
-        ]
-
-    return call(
-        functools.partial(owners_kernel, ways),
-        (
-            jax.ShapeDtypeStruct((HEADS, rows, columns), BF),
-            jax.ShapeDtypeStruct((HEADS,) + note.shape[4:], F32),
-        ),
-        (part, note),
-        slots((rows, columns), BF) + slots(note.shape[4:], F32) + [DMA((2,))] + sems() + sems(),
-        5,
-        VMEM,
-        VMEM,
-    )
-
-
-def attention_kernel(prompt_runs, one_prompt, q_ref, do_ref, k_ref, v_ref, row_ref, col_ref,
-                     o_ref, dq_ref, dk_ref, dv_ref, s_ref):
+        + row_buffers() + row_buffers()
+        + [vm((2, 2, group, 256)), vm((256, group)), vm((3, hp, 2, rows, a_cols))]
+        + gradient_buffers(a_cols) + gradient_buffers(b_cols)
+        + [vm(note.shape, F32)] * 3 + [vm((extra,) + note.shape, F32)]
+        + [DMA((7,)), DMA((2, 2)), DMA((2,)), DMA((2,)), DMA((2,)), DMA((1,)), DMA((1,))]
+        + [DMA((chunks,))] * 12
+        + gradient_sems() + gradient_sems()
+        + [DMA((4,)), DMA((1 + ways + HEADS,)), DMA((1 + ways + HEADS,))]
+    )
+    shapes = (
+        jax.ShapeDtypeStruct((runs, STRIPE, width), F32),
+        jax.ShapeDtypeStruct((runs, STRIPE, width), F32),
+        jax.ShapeDtypeStruct((HEADS, rows, a_cols), BF),
+        jax.ShapeDtypeStruct((HEADS, rows, b_cols), BF),
+        jax.ShapeDtypeStruct((HEADS,) + note.shape, F32),
+    )
+    ins = (
+        att.reshape(lines + (HEAD_DIM,)), act.reshape(lines + (inner - HEAD_DIM,)), dexp.reshape(lines + (right - head3,)),
+        dq.reshape(lines + (HEAD_DIM,)), dkv, tables, w_out, w_in, n_all, g_all, note,
+    )
+    return pl.pallas_call(
+        functools.partial(finish_kernel, ways),
+        out_shape=shapes,
+        in_specs=[ANY] * len(ins),
+        out_specs=(VMEM, VMEM, ANY, ANY, ANY),
+        scratch_shapes=scratch,
+        compiler_params=pltpu.CompilerParams(collective_id=2, has_side_effects=True, vmem_limit_bytes=62 * 2**20),
+    )(*ins)
+
+
+def attention_kernel(prompt_runs, one_prompt, q_ref, do_ref, kv_ref, row_ref, col_ref, turn_ref,
+                     o_ref, dq_ref, dkv_ref, s_ref, sum_ref):
     runs, m, _ = q_ref.shape
-    keys = k_ref.shape[1]
+    keys = kv_ref.shape[1]
     by_rows = (((1,), (1,)), ((), ()))
     by_tokens = (((0,), (0,)), ((), ()))
 
@@ -582,7 +779,7 @@
 
     def mask(i, k):
         rows, cols = row_ref[i], col_ref[k]
-        if isinstance(i, int) and isinstance(k, int) and i == k:
+        if i == k:
             return (rows[:, 1:2] == cols[1:2, :]) & (cols[0:1, :] <= rows[:, 0:1])
         if one_prompt:
             return None
@@ -593,7 +790,7 @@
         q = q_ref[i]
         peak = None
         for at, k in enumerate(pieces):
-            s = dot(q, k_ref[k], by_rows)
+            s = dot(q, kv_ref[k, :, :HEAD_DIM], by_rows)
             keep = mask(i, k)
             if keep is not None:
                 s = jnp.where(keep, s, -1e30)
@@ -610,7 +807,7 @@
                 p = jnp.where(keep, p, 0.0)
             s_ref[:, at * keys : (at + 1) * keys] = p
             total = total + jnp.sum(p, -1, keepdims=True)
-            out = out + dot(p.astype(BF), v_ref[k], (((1,), (0,)), ((), ())))
+            out = out + dot(p.astype(BF), kv_ref[k, :, HEAD_DIM:], (((1,), (0,)), ((), ())))
         inverse = 1.0 / total
         out = out * inverse
         o_ref[i] = out.astype(BF)
@@ -619,36 +816,37 @@
         dq = jnp.zeros((m, HEAD_DIM), F32)
         for at, k in enumerate(pieces):
             p = s_ref[:, at * keys : (at + 1) * keys] * inverse
-            dp = dot(do, v_ref[k], by_rows)
+            dp = dot(do, kv_ref[k, :, HEAD_DIM:], by_rows)
             ds = (p * (dp - delta)).astype(BF)
-            dq = dq + dot(ds, k_ref[k], (((1,), (0,)), ((), ())))
+            dq = dq + dot(ds, kv_ref[k, :, :HEAD_DIM], (((1,), (0,)), ((), ())))
             dk = dot(ds, q, by_tokens)
             dv = dot(p.astype(BF), do, by_tokens)
             if i == k:
-                dk_ref[k] = dk
-                dv_ref[k] = dv
+                sum_ref[k, :, :HEAD_DIM] = dk
+                sum_ref[k, :, HEAD_DIM:] = dv
             else:
-                dk_ref[k] = dk_ref[k] + dk
-                dv_ref[k] = dv_ref[k] + dv
-        dq_ref[i] = dq * (1.0 / math.sqrt(HEAD_DIM))
-
-
-def attention(prompt_runs, one_prompt, queries, d_out, keys, values, row_meta, col_meta):
-    runs, m, _ = queries.shape
-    count = keys.shape[1]
+                sum_ref[k, :, :HEAD_DIM] = sum_ref[k, :, :HEAD_DIM] + dk
+                sum_ref[k, :, HEAD_DIM:] = sum_ref[k, :, HEAD_DIM:] + dv
+        dq = (dq * (1.0 / math.sqrt(HEAD_DIM))).astype(BF).astype(F32)
+        dq_ref[i] = turn(dq, [turn_ref[t, i] for t in range(3)], -1.0).astype(BF)
+    dkv_ref[...] = sum_ref[...].astype(BF)
+
+
+def attention(prompt_runs, one_prompt, queries, d_out, pairs, row_meta, col_meta, tables):
+    m = queries.shape[1]
+    count = pairs.shape[1]
     return pl.pallas_call(
         functools.partial(attention_kernel, prompt_runs, one_prompt),
         out_shape=(
             jax.ShapeDtypeStruct(queries.shape, BF),
-            jax.ShapeDtypeStruct(queries.shape, F32),
-            jax.ShapeDtypeStruct(keys.shape, F32),
-            jax.ShapeDtypeStruct(keys.shape, F32),
+            jax.ShapeDtypeStruct(queries.shape, BF),
+            jax.ShapeDtypeStruct(pairs.shape, BF),
         ),
         in_specs=[VMEM] * 6,
-        out_specs=(VMEM,) * 4,
-        scratch_shapes=[pltpu.VMEM((m, (prompt_runs + 1) * count), F32)],
+        out_specs=(VMEM,) * 3,
+        scratch_shapes=[pltpu.VMEM((m, (prompt_runs + 1) * count), F32), pltpu.VMEM(pairs.shape, F32)],
         compiler_params=pltpu.CompilerParams(vmem_limit_bytes=60 * 2**20),
-    )(queries, d_out, keys, values, row_meta, col_meta)
+    )(queries, d_out, pairs, row_meta, col_meta, tables)
 
 
 def angles_of(positions):
@@ -775,6 +973,15 @@
     position = (group_position.T[:, :, None] + within.astype(F32)).reshape(group_rows)
     angles = angles_of(position)
     cosine, sine = jnp.cos(angles), jnp.sin(angles)
+    rows_run = group_rows // runs
+    rest = ((0, 0), (0, 128 - ROT))
+    tables = jnp.stack(
+        [
+            jnp.pad(jnp.concatenate([cosine, cosine], 1), rest, constant_values=1.0),
+            jnp.pad(-sine, ((0, 0), (0, 128 - ROT // 2))),
+            jnp.pad(sine, ((0, 0), (ROT // 2, 128 - ROT))),
+        ]
+    ).reshape(3, runs, rows_run, 128)
 
     w_in = w_all[:, :block_columns]
     w_out = w_all[:, block_columns:]
@@ -782,7 +989,6 @@
     queries = (rotate(mixed[:, :HEAD_DIM], cosine, sine) * (1.0 / math.sqrt(HEAD_DIM))).astype(BF)
     keys = rotate(mixed[:, HEAD_DIM : 2 * HEAD_DIM], cosine, sine).astype(BF)
     values = mixed[:, 2 * HEAD_DIM :].astype(BF)
-    rows_run = group_rows // runs
     pairs = exchange(ways, jnp.concatenate([keys, values], 1).reshape(runs, rows_run, 2 * HEAD_DIM))
     pairs = pairs.reshape(runs, run_size, 2 * HEAD_DIM)
 
@@ -813,59 +1019,34 @@
 
     row_meta = jnp.stack(meta(row_tokens), -1)
     col_meta = jnp.stack(meta(col_tokens), 1)
-    attended, d_queries, d_keys, d_values = attention(
+    attended, d_queries, d_pairs = attention(
         prompt_runs, one_prompt,
         queries.reshape(runs, rows_run, HEAD_DIM), d_attended.reshape(runs, rows_run, HEAD_DIM),
-        pairs[..., :HEAD_DIM], pairs[..., HEAD_DIM:], row_meta, col_meta,
-    )
-    attended = attended.reshape(group_rows, HEAD_DIM)
-
-    contract = (((1,), (1,)), ((), ()))
-    tokens_dims = (((0,), (0,)), ((), ()))
-    left = jnp.concatenate([attended, activated], 1)
-    out_part = lax.dot_general(left, w_out, contract, preferred_element_type=F32).astype(BF)
-    out_sum = collect(ways, out_part.reshape(runs, HEADS, STRIPE, width), 3).reshape(tok_dev, width)
-    output = restored((states + out_sum + out_bias).astype(BF))
-
-    d_pairs = jnp.concatenate([d_keys, d_values], -1).astype(BF)
-    d_pairs = fold(ways, d_pairs.reshape(runs, 4 * ways, rows_run, 2 * HEAD_DIM)).reshape(group_rows, 2 * HEAD_DIM)
-    d_mixed = jnp.concatenate(
-        [
-            rotate(d_queries.reshape(group_rows, HEAD_DIM).astype(BF).astype(F32), cosine, -sine),
-            rotate(d_pairs[:, :HEAD_DIM].astype(BF).astype(F32), cosine, -sine),
-            d_pairs[:, HEAD_DIM:],
-        ],
-        1,
-    ).astype(BF)
-
-    right = jnp.concatenate([d_mixed, d_expanded], 1)
-    e_part = lax.dot_general(right, w_in, contract, preferred_element_type=F32).astype(BF)
-    e_sum = collect(ways, e_part.reshape(runs, HEADS, STRIPE, width), 4).reshape(tok_dev, width)
+        pairs, row_meta, col_meta, tables,
+    )
+
+    d_pairs = d_pairs.reshape(runs, ways, 4, rows_run, 2 * HEAD_DIM)
+    if ways > 1:
+        alike = [[w2 * 2 * HEADS + k for w2 in range(ways)] for k in range(2 * HEADS)]
+        d_pairs = lax.psum_scatter(
+            d_pairs.astype(F32), "blk", scatter_dimension=1, axis_index_groups=alike, tiled=True
+        ).astype(BF)
+    d_pairs = d_pairs[:, 0]
+    own_sums = jnp.sum(grad_out, 0).reshape(width // lanes, lanes)
+    sum_note = jnp.concatenate(
+        [jnp.zeros((note_rows, lanes), F32), own_sums, jnp.zeros((-(note_rows + width // lanes) % 8, lanes), F32)]
+    )
+    out_sum, e_sum, owned_a, owned_b, owned_notes = finish(
+        ways, rows, attended, activated, d_expanded, d_queries, d_pairs,
+        tables, w_out, w_in, n_all, g_all, sum_note,
+    )
+    output = restored((states + out_sum.reshape(tok_dev, width) + out_bias).astype(BF))
+    e_sum = e_sum.reshape(tok_dev, width)
     dx = inverse_spread * (
         e_sum - jnp.mean(e_sum, -1, keepdims=True) - normed * jnp.mean(e_sum * normed, -1, keepdims=True)
     )
     input_grad = restored((grad_out + dx).astype(BF))
-
-    part = jnp.concatenate(
-        [
-            lax.dot_general(n_all, right, tokens_dims, preferred_element_type=F32).astype(BF),
-            lax.dot_general(g_all, left, tokens_dims, preferred_element_type=F32).astype(BF),
-        ],
-        1,
-    )
-    part = part.reshape(2, ways, HEADS, 2, rows, part.shape[1])
-    sums = jnp.sum(right.astype(F32), 0).reshape(note_rows, lanes)
-    g_sums = jnp.pad(jnp.sum(grad_out, 0).reshape(devices, 1, rows), ((0, 0), (0, 0), (0, lanes - rows)))
-    sum_notes = jnp.concatenate(
-        [
-            jnp.broadcast_to(sums[None], (devices, note_rows, lanes)),
-            g_sums,
-            jnp.zeros((devices, 1, lanes), F32),
-        ],
-        1,
-    ).reshape(2, ways, HEADS, 2, note_rows + 2, lanes)
-    owned, owned_notes = to_owners(ways, part, sum_notes)
-    owned = owned.astype(F32)
+    owned_a, owned_b = owned_a.astype(F32), owned_b.astype(F32)
 
     def join_qkv(values):
         return values.reshape(HEADS, -1, 3, HEAD_DIM).transpose(1, 2, 0, 3).reshape(-1, 3 * width)
@@ -873,14 +1054,15 @@
     def join(values):
         return values.transpose(1, 0, 2).reshape(values.shape[1], -1)
 
-    raw_qkv = join_qkv(owned[..., :head3])
-    raw_expand = join(owned[..., head3:block_columns])
-    dense_grad = join(owned[..., block_columns : block_columns + HEAD_DIM])
-    shrink_grad = join(owned[..., block_columns + HEAD_DIM :])
+    raw_qkv = join_qkv(owned_b)
+    dense_grad = join(owned_a[..., :HEAD_DIM])
+    shrink_grad = join(owned_a[..., HEAD_DIM : HEAD_DIM + hidden])
+    raw_expand = join(owned_a[..., HEAD_DIM + hidden :])
     column_sums = owned_notes[:, :note_rows].reshape(HEADS, 1, block_columns)
     qkv_sum = join_qkv(column_sums[..., :head3])
     expand_sum = join(column_sums[..., head3:])
-    bias_grad = jnp.sum(owned_notes[:, note_rows, :rows], 0)
+    all_sums = jnp.sum(owned_notes[:, note_rows : note_rows + width // lanes], 0).reshape(width)
+    bias_grad = lax.dynamic_slice_in_dim(all_sums, me * rows, rows, 0)
     qkv_grad = gain_one[:, None] * raw_qkv + shift_one[:, None] * qkv_sum
     expand_grad = gain_two[:, None] * raw_expand + shift_two[:, None] * expand_sum
 

time: 702 us -> 553 us (0.79)
  Pallas kernels: 501 us -> 428 us
  matrix products: 79.6 us -> 42.1 us
  other arithmetic: 53.4 us -> 28.2 us
  local copies, waits for them, and re-layouts: 56.5 us -> 42.5 us
    pallas_call x6 -> x2, Pallas kernels: 479 us -> 206 us  [call(): pl.pallas_call(body, out_shape=out_shape, in_specs=[in_spec] * len(ins),...]
    pallas_call x0 -> x1, Pallas kernels: none -> 201 us  [finish(): pl.pallas_call(functools.partial(finish_kernel, ways), out_shape=shapes,...]
    dot_general x4 -> x0, matrix products: 37.3 us -> none  [the longest x1 11.5 us: per_device(): lax.dot_general(right, w_in, contract, preferred_element_type=F32)]
    concatenate x3 -> x2, other arithmetic: 18.3 us -> 0.7 us  [the longest x1 0.68 us: per_device(): jnp.concatenate([jnp.zeros((note_rows, lanes), F32), own_sums, jnp.zeros(...]
    concatenate x2, local copies, waits for them, and re-layouts: 17.2 us -> 0.08 us  [per_device(): jnp.concatenate([jnp.zeros((note_rows, lanes), F32), own_sums, jnp.zeros(...]
where the time goes in v2:
time: 553 us; the launch traced here: 543 us
  Pallas kernels  428 us (77%)
  local copies, waits for them, and re-layouts  42.5 us (8%)
  matrix products  42.1 us (8%)
  other arithmetic  28.2 us (5%)
    pallas_call x2, Pallas kernels, call(): pl.pallas_call(body, out_shape=out_shape, in_specs=[in_spec] * len(ins),...  206 us
    pallas_call x1, Pallas kernels, finish(): pl.pallas_call(functools.partial(finish_kernel, ways), out_shape=shapes,...  201 us
    pallas_call x1, Pallas kernels, attention(): pl.pallas_call(functools.partial(attention_kernel, prompt_runs, one_promp...  21.4 us
    dot_general x1, matrix products, per_device(): jnp.dot(n_all, w_in[:, head3:], preferred_element_type=F32)  17.8 us

profile of v2, /device:TPU:8, one launch (start us, length us, event | category | flops | bytes accessed | tf_op | source)
XLA Modules:
  0.0 543.0 jit_solution(14255159893612424042)
XLA Ops:
  1.7 1.4 fusion.67
  4.4 1.4 fusion.16
  7.5 1.7 convert_reduce_fusion
  9.2 3.1 bitcast_bitcast_fusion
  13.9 3.0 pad_maximum_fusion.w_in
  17.0 172.5 %shard_map.271 = (bf16[8,8,16,2048]{3,2,1,0:T(8,128)(2,1)}, bf16[8,8,16,2048]{3,2,1,0:T(8,128)(2,1)}, bf16[2,1,8,2,64,3072]{5,4,3,2,1,0:T(8,128)(2,1)}, f32[2,1,8,2,16,128]{5,4,3,2,1,0:T(8,128)}) custom-call(bf16[8,16,2048]{2,1,0:T(8,128)(2,1)} %bitcast.176, bf16[8,16,2048]{2,1,0:T(8,128)(2,1)} %bitcast.154, bf16[8,64,3072]{2,1,0:T(8,128)(2,1)} %pad_maximum_fusion.w_in, ...), custom_call_target="tpu_custom_call" | custom-call | tf_op jit(solution)/shard_map/pallas_call | solution.py:73
  190.5 17.8 %multiply_convert_fusion = (bf16[1024,1024]{1,0:T(8,128)(2,1)}, f32[1024,1024]{1,0:T(8,128)S(1)}, f32[1024,1024]{1,0:T(8,128)}) fusion(f32[1024]{0:T(1024)S(1)} %slice_bitcast_fusion.4, bf16[1024,2048]{1,0:T(8,128)(2,1)} %bitcast.155, bf16[2048,3072]{1,0:T(8,128)(2,1)} %bitcast.144), kind=kOutput, calls=%fused_computation.7 | convolution fusion | flops 4364173312 | bytes 18878464 | tf_op jit(solution)/shard_map/dot_general | solution.py:996
  208.3 9.1 %add_convert_fusion = bf16[1024,1024]{1,0:T(8,128)(2,1)} fusion(f32[1024,1024]{1,0:T(8,128)S(1)} %get-tuple-element.44, f32[1024,1024]{1,0:T(8,128)} %get-tuple-element.72, bf16[1024,2048]{1,0:T(8,128)(2,1)S(1)} %bitcast.160, bf16[2048,3072]{1,0:T(8,128)(2,1)S(1)} %bitcast.148, f32[1024]{0:T(1024)S(1)} %slice_bitcast_fusion.4), kind=kOutput, calls=%fused_computation.6 | convolution fusion | flops 4310695936 | bytes 18878464 | tf_op jit(solution)/shard_map/dot_general | solution.py:999
  217.4 5.2 fusion.19
  223.9 2.4 multiply_cosine_fusion
  227.2 1.3 pad_maximum_fusion.1.turn_ref.tables
  229.6 1.3 copy.111
  231.0 33.7 %shard_map.272 = bf16[8,4,128,512]{3,2,1,0:T(8,128)(2,1)} custom-call(bf16[8,128,512]{2,1,0:T(8,128)(2,1)} %bitcast.163), custom_call_target="tpu_custom_call" | custom-call | tf_op jit(solution)/shard_map/pallas_call | solution.py:73
  264.7 4.6 convolution_convert_fusion.4
  270.9 2.5 fusion.28.q_ref
  274.4 1.0 copy.117.row_ref
  276.6 21.4 %shard_map.273 = (bf16[8,128,256]{2,1,0:T(8,128)(2,1)}, bf16[8,128,256]{2,1,0:T(8,128)(2,1)}, bf16[8,512,512]{2,1,0:T(8,128)(2,1)}) custom-call(bf16[8,128,256]{2,1,0:T(8,128)(2,1)} %fusion.28.q_ref, bf16[8,128,256]{2,1,0:T(8,128)(2,1)} %bitcast.181, bf16[8,512,512]{2,1,0:T(8,128)(2,1)} %bitcast.143, s32[8,128,3]{2,1,0:T(8,128)} %copy.117.row_ref, ...), custom_call_target="tpu_custom_call" | custom-call | tf_op jit(solution)/shard_map/pallas_call | solution.py:838
  298.1 6.4 %slice.138.w_in = bf16[2048,1792]{1,0:T(8,128)(2,1)} slice(bf16[2048,3072]{1,0:T(8,128)(2,1)} %bitcast.146), slice={[0:2048], [0:1792]} | slice | bytes 14680064 | tf_op jit(solution)/shard_map/slice | solution.py:986
  304.5 5.1 slice.137.w_out
  310.4 200.7 %shard_map.274 = (f32[8,16,2048]{2,1,0:T(8,128)}, f32[8,16,2048]{2,1,0:T(8,128)}, bf16[8,64,2304]{2,1,0:T(8,128)(2,1)}, bf16[8,64,768]{2,1,0:T(8,128)(2,1)}, f32[8,32,128]{2,1,0:T(8,128)}) custom-call(bf16[8,4,2,16,256]{4,3,2,1,0:T(8,128)(2,1)} %bitcast.179, bf16[8,4,2,16,1024]{4,3,2,1,0:T(8,128)(2,1)} %bitcast.168, bf16[8,4,2,16,1024]{4,3,2,1,0:T(8,128)(2,1)} %bitcast.169, ...), custom_call_target="tpu_custom_call" | custom-call | tf_op jit(solution)/shard_map/pallas_call | solution.py:760
  511.1 2.1 convert_element_type.128
  513.2 2.4 slice_bitcast_fusion
  516.1 1.5 copy.128
  517.9 4.2 fusion.18
  522.0 3.2 copy.130
  525.2 2.1 reshape.661
  527.3 2.6 copy.118
  530.4 2.2 fusion.25
  532.6 1.1 slice_bitcast_fusion.2
  536.2 1.9 fusion.26
  538.1 1.1 convolution_convert_fusion
  539.2 1.1 convolution_convert_fusion.1
  (188 shorter events, 20.2 us)
Async XLA Ops:
  0.7 6.9 %copy-start = (bf16[128,2048]{1,0:T(8,128)(2,1)S(1)}, bf16[128,2048]{1,0:T(8,128)(2,1)}, u32[]{:S(2)}) copy-start(bf16[128,2048]{1,0:T(8,128)(2,1)} %param.32) | copy-start | bytes 1572868
  0.7 6.0 %copy-start.18 = (s32[4096]{0:T(1024)S(1)}, s32[4096]{0:T(1024)}, u32[]{:S(2)}) copy-start(s32[4096]{0:T(1024)} %param.30) | copy-start | bytes 49156
  0.7 3.7 copy-start.37
  0.7 3.7 copy-start.8
  0.7 5.1 copy-start.34
  0.7 5.2 copy-start.38
  0.7 5.2 copy-start.39
  0.7 5.3 copy-start.11
  0.8 5.6 %copy-start.35 = (bf16[192]{0:T(256)(128)(2,1)S(1)}, bf16[192]{0:T(256)(128)(2,1)}, u32[]{:S(2)}) copy-start(bf16[192]{0:T(256)(128)(2,1)} %param.23) | copy-start | bytes 1156
  0.8 5.9 %copy-start.40 = (s32[128]{0:T(128)S(1)}, s32[128]{0:T(128)}, u32[]{:S(2)}) copy-start(s32[128]{0:T(128)} %param.31) | copy-start | bytes 1540
  0.8 6.0 %copy-start.42 = (bf16[64]{0:T(256)(128)(2,1)S(1)}, bf16[64]{0:T(256)(128)(2,1)}, u32[]{:S(2)}) copy-start(bf16[64]{0:T(256)(128)(2,1)} %param.25) | copy-start | bytes 388
  0.8 6.0 %copy-start.41 = (bf16[64]{0:T(256)(128)(2,1)S(1)}, bf16[64]{0:T(256)(128)(2,1)}, u32[]{:S(2)}) copy-start(bf16[64]{0:T(256)(128)(2,1)} %param.29) | copy-start | bytes 388
  1.7 5.9 %copy-start.22 = (s32[128]{0:T(128)}, s32[128]{0:T(128)S(1)}, u32[]{:S(2)}) copy-start(s32[128]{0:T(128)S(1)} %fusion.65) | copy-start | bytes 1540
  4.4 8.0 %copy-start.32 = (f32[64]{0:T(128)}, f32[64]{0:T(128)S(1)}, u32[]{:S(2)}) copy-start(f32[64]{0:T(128)S(1)} %convert_element_type.113) | copy-start | bytes 772
  6.0 6.6 %copy-start.26 = (f32[64]{0:T(128)}, f32[64]{0:T(128)S(1)}, u32[]{:S(2)}) copy-start(f32[64]{0:T(128)S(1)} %convert_element_type.106) | copy-start | bytes 772
  6.0 6.5 %copy-start.28 = (f32[64]{0:T(128)}, f32[64]{0:T(128)S(1)}, u32[]{:S(2)}) copy-start(f32[64]{0:T(128)S(1)} %convert_element_type.111) | copy-start | bytes 772
  9.2 4.7 copy-start.15
  190.5 17.8 %copy-start.3 = (bf16[2,1,8,2,64,3072]{5,4,3,2,1,0:T(8,128)(2,1)S(1)}, bf16[2,1,8,2,64,3072]{5,4,3,2,1,0:T(8,128)(2,1)}, u32[]{:S(2)}) copy-start(bf16[2,1,8,2,64,3072]{5,4,3,2,1,0:T(8,128)(2,1)} %get-tuple-element.28) | copy-start | bytes 37748740
  190.5 17.8 %copy-start.7 = (bf16[8,8,16,2048]{3,2,1,0:T(8,128)(2,1)S(1)}, bf16[8,8,16,2048]{3,2,1,0:T(8,128)(2,1)}, u32[]{:S(2)}) copy-start(bf16[8,8,16,2048]{3,2,1,0:T(8,128)(2,1)} %get-tuple-element.30) | copy-start | bytes 12582916
  208.3 9.1 %copy-start.6 = (bf16[8,8,16,2048]{3,2,1,0:T(8,128)(2,1)S(1)}, bf16[8,8,16,2048]{3,2,1,0:T(8,128)(2,1)}, u32[]{:S(2)}) copy-start(bf16[8,8,16,2048]{3,2,1,0:T(8,128)(2,1)} %get-tuple-element.27) | copy-start | bytes 12582916
  264.7 4.6 copy-start.14
  264.7 5.8 %slice-start = ((f32[1024,768]{0,1:T(8,128)}), f32[1024,192]{0,1:T(8,128)S(1)}, s32[]{:S(2)}) async-start(f32[1024,768]{0,1:T(8,128)} %fusion.19), calls=%async_computation | async-start | bytes 1572864 | tf_op jit(solution)/shard_map/slice | solution.py:861
  304.5 5.2 copy-start.19
  517.9 7.3 %copy-start.13 = (bf16[8,64,768]{2,1,0:T(8,128)(2,1)S(1)}, bf16[8,64,768]{2,1,0:T(8,128)(2,1)}, u32[]{:S(2)}) copy-start(bf16[8,64,768]{2,1,0:T(8,128)(2,1)} %get-tuple-element.36) | copy-start | bytes 2359300
  525.2 5.2 copy-start.27
  525.2 5.2 copy-start.29
  529.9 4.7 copy-start.4
  530.3 4.4 copy-start.21
  530.4 4.4 copy-start.25
  530.4 5.7 %copy-start.5 = (bf16[128,2048]{1,0:T(8,128)(2,1)S(1)}, bf16[128,2048]{1,0:T(8,128)(2,1)}, u32[]{:S(2)}) copy-start(bf16[128,2048]{1,0:T(8,128)(2,1)} %get-tuple-element.74) | copy-start | bytes 1572868
  534.7 8.0 %copy-start.1 = (bf16[128,2048]{1,0:T(8,128)(2,1)S(1)}, bf16[128,2048]{1,0:T(8,128)(2,1)}, u32[]{:S(2)}) copy-start(bf16[128,2048]{1,0:T(8,128)(2,1)} %param.32) | copy-start | bytes 1572868
  534.8 7.3 %copy-start.17 = (f32[8,32,128]{2,1,0:T(8,128)S(1)}, f32[8,32,128]{2,1,0:T(8,128)}, u32[]{:S(2)}) copy-start(f32[8,32,128]{2,1,0:T(8,128)} %get-tuple-element.37) | copy-start | bytes 393220
  (13 other events, 27.8 us)

commit v3 on v2

--- a/solution.py
+++ b/solution.py
@@ -85,148 +85,349 @@
 LINE = HEADS // 2
 
 
-def spread_rows(place, own, full, up, down, side, recv):
+def relay_rows(place, own, full, s, r):
     hz, hy = place.hz, place.hy
-
-    def piece(src, z, target, send):
-        idx = z * 2 + hy
-        return remote(src, full.at[:, idx], send, recv.at[idx], target)
-
-    def up_to():
-        return place.device(h=place.h + 2)
-
-    def down_to():
-        return place.device(h=place.h - 2)
+    d0, d1 = hz % 2, hz // 2
+
+    def index(e1, e0, y):
+        return (e1 * 2 + e0) * 2 + y
+
+    far = place.device(h=index(1 - d1, d0, hy))
+    near = place.device(h=index(d1, 1 - d0, hy))
+    side = place.peer_y()
+    made = []
+
+    def push(src, idx, k, device):
+        copy = remote(src, full.at[:, idx], s.at[k], r.at[idx], device)
+        copy.start()
+        made.append(copy)
+
+    def arrived(idx):
+        remote(full.at[:, idx], full.at[:, idx], s.at[0], r.at[idx], side).wait_recv()
 
     def first():
-        @pl.when(hz < LINE - 1)
-        def _():
-            piece(own, hz, up_to(), up.at[0]).start()
-
-        @pl.when(hz > 0)
-        def _():
-            piece(own, hz, down_to(), down.at[0]).start()
-
-        piece(own, hz, place.peer_y(), side.at[0]).start()
-
-    def arrived(idx):
-        remote(full.at[:, idx], full.at[:, idx], side.at[0], recv.at[idx], place.peer_y()).wait_recv()
-
-    def step(s):
-        low, high = hz - s - 1, hz + s + 1
-
-        @pl.when(low >= 0)
-        def _():
-            arrived(low * 2 + hy)
-            src = full.at[:, low * 2 + hy]
-
-            @pl.when(hz < LINE - 1)
-            def _():
-                piece(src, low, up_to(), up.at[s + 1]).start()
-
-            piece(src, low, place.peer_y(), side.at[low + 1]).start()
-
-        @pl.when(high < LINE)
-        def _():
-            arrived(high * 2 + hy)
-            src = full.at[:, high * 2 + hy]
-
-            @pl.when(hz > 0)
-            def _():
-                piece(src, high, down_to(), down.at[s + 1]).start()
-
-            piece(src, high, place.peer_y(), side.at[high + 1]).start()
-
-    def finish():
+        for k, device in enumerate((far, near, side)):
+            push(own, place.h, k, device)
+
+    def from_far():
+        idx = index(1 - d1, d0, hy)
+        arrived(idx)
+        push(full.at[:, idx], idx, 3, near)
+        push(full.at[:, idx], idx, 4, side)
+
+    def from_near():
+        idx = index(d1, 1 - d0, hy)
+        arrived(idx)
+        push(full.at[:, idx], idx, 5, side)
+
+    def from_near_far():
+        idx = index(1 - d1, 1 - d0, hy)
+        arrived(idx)
+        push(full.at[:, idx], idx, 6, side)
+
+    def from_side():
         for z in range(LINE):
             arrived(z * 2 + 1 - hy)
 
     def sent():
-        piece(own, hz, place.peer_y(), side.at[0]).wait_send()
-        for z in range(LINE):
-            @pl.when(z != hz)
-            def _():
-                piece(own, z, place.peer_y(), side.at[z + 1]).wait_send()
-        for s in range(LINE - 1):
-            @pl.when((hz < LINE - 1) & (hz - s >= 0))
-            def _():
-                piece(own, hz, up_to(), up.at[s]).wait_send()
-
-            @pl.when((hz > 0) & (hz + s < LINE))
-            def _():
-                piece(own, hz, down_to(), down.at[s]).wait_send()
-
-    return first, step, finish, sent
-
-
-def gather_kernel(ways, n_in, g_in, w_in, m_in, n_all, g_all, w_all, m_all,
-                  local, nu, nd, ns, nr, gu, gd, gs, gr, wa, wx, wc, wr, ma, mx, mc, mr):
+        for copy in made:
+            copy.wait_send()
+
+    return first, from_far, from_near, from_near_far, from_side, sent
+
+
+def gelu_slope(v):
+    return 0.5 * (1.0 + lax.erf(v * math.sqrt(0.5))) + v * jnp.exp(-0.5 * v * v) * (1.0 / math.sqrt(2 * math.pi))
+
+
+def open_kernel(ways, cuts, fuse, prompt_runs, prompt_total, *refs):
+    names = ["n_in", "g_in", "w_in", "note_in", "trig_in", "step_in", "row_tok", "col_tok", "n_out", "g_out", "w_out", "note_out", "turn_out"]
+    if fuse:
+        names += ["att_out", "act_out", "dexp_out", "dq_out", "dkv_out"]
+    names += ["v_n", "v_g", "v_w", "v_turn", "trig", "note", "note_c", "note_x", "note_w", "note_h", "own", "put"]
+    names += ["ns", "nr", "gs", "gr", "wa", "wr", "xs", "xr", "cs", "cr", "t_s", "t_r", "nc_s", "nc_r", "nx_s", "nx_r", "nw_s", "nw_r", "nh_s", "nh_r"]
+    if fuse:
+        names += ["v_q", "v_do", "v_kv", "v_exp", "v_act", "v_dexp", "v_att", "v_dq", "v_dkv", "s_ref", "sum_ref", "kx_s", "kx_r", "kc_s", "kc_r"]
+    at = dict(zip(names, refs, strict=True))
+    (n_in, g_in, w_in, note_in, trig_in, step_in, n_out, g_out, w_out, note_out, turn_out, v_n, v_g, v_w, v_turn) = (
+        at[k] for k in ["n_in", "g_in", "w_in", "note_in", "trig_in", "step_in", "n_out", "g_out", "w_out", "note_out", "turn_out", "v_n", "v_g", "v_w", "v_turn"]
+    )
+    trig, note, note_c, note_x, note_w, note_h, own, put = (
+        at[k] for k in ["trig", "note", "note_c", "note_x", "note_w", "note_h", "own", "put"]
+    )
     place = Place(ways)
     x, w, h, c = place.x, place.w, place.h, place.c
+    runs = v_n.shape[0]
+    width = v_n.shape[-1]
+    per_run = HEADS * STRIPE
     stage_a = [(dw, dh) for dw in range(ways) for dh in range(HEADS) if (dw, dh) != (0, 0)]
     greet(
         [place.device(w=(w + dw) % ways, h=(h + dh) % HEADS) for dw, dh in stage_a]
         + [place.peer_x(), place.peer_c()]
     )
-    n_first, n_step, n_finish, n_sent = spread_rows(place, n_in, n_all, nu, nd, ns, nr)
-    g_first, g_step, g_finish, g_sent = spread_rows(place, g_in, g_all, gu, gd, gs, gr)
-    copies = [
-        pltpu.make_async_copy(n_in, n_all.at[:, h], local.at[0]),
-        pltpu.make_async_copy(g_in, g_all.at[:, h], local.at[1]),
-        pltpu.make_async_copy(w_in.at[h], w_all.at[x, w, h, c], local.at[2]),
-        pltpu.make_async_copy(m_in.at[h], m_all.at[x, w, h, c], local.at[3]),
-    ]
-    n_first()
-    sends = []
+    sends, puts = [], []
 
     def send(src, dst, s, r, device):
         copy = remote(src, dst, s, r, device)
         copy.start()
         sends.append(copy)
-
-    pairs = ((w_all, wa, wx, wc, wr), (m_all, ma, mx, mc, mr))
-    for k, (dw, dh) in enumerate(stage_a):
-        h2 = (h + dh) % HEADS
-        target = place.device(w=(w + dw) % ways, h=h2)
-        send(w_in.at[h2], w_all.at[x, w, h, c], wa.at[k], wr.at[x, w, h, c], target)
-        send(m_in.at[h2], m_all.at[x, w, h, c], ma.at[k], mr.at[x, w, h, c], target)
-    send(w_in.at[h], w_all.at[x, w, h, c], wx.at[w, h], wr.at[x, w, h, c], place.peer_x())
-    send(m_in.at[h], m_all.at[x, w, h, c], mx.at[w, h], mr.at[x, w, h, c], place.peer_x())
-    send(w_in.at[h], w_all.at[x, w, h, c], wc.at[x, w, h], wr.at[x, w, h, c], place.peer_c())
-    send(m_in.at[h], m_all.at[x, w, h, c], mc.at[x, w, h], mr.at[x, w, h, c], place.peer_c())
+        return copy
+
+    def save(src, dst):
+        copy = pltpu.make_async_copy(src, dst, put.at[len(puts)])
+        copy.start()
+        puts.append(copy)
+
+    mine = [
+        pltpu.make_async_copy(w_in.at[h], v_w.at[x, w, h, c], own.at[0]),
+        pltpu.make_async_copy(n_in, v_n.at[:, h], own.at[1]),
+        pltpu.make_async_copy(g_in, v_g.at[:, h], own.at[2]),
+        pltpu.make_async_copy(trig_in, trig.at[h], own.at[3]),
+        pltpu.make_async_copy(note_in, note, own.at[4]),
+    ]
+    for copy in (mine[4], mine[0], mine[3], mine[1], mine[2]):
+        copy.start()
+    n_first, n_far, n_near, n_last, n_side, n_sent = relay_rows(place, n_in, v_n, at["ns"], at["nr"])
+    g_first, g_far, g_near, g_last, g_side, g_sent = relay_rows(place, g_in, v_g, at["gs"], at["gr"])
+    wa, wr, xs, xr, cs, cr = (at[k] for k in ["wa", "wr", "xs", "xr", "cs", "cr"])
+
+    def columns(g):
+        return pl.ds(cuts[g][0], cuts[g][1])
+
+    def w_first(g):
+        for k, (dw, dh) in enumerate(stage_a):
+            h2 = (h + dh) % HEADS
+            send(w_in.at[h2, :, columns(g)], v_w.at[x, w, h, c, :, columns(g)], wa.at[g, k], wr.at[g, w, h],
+                 place.device(w=(w + dw) % ways, h=h2))
+
+    def w_across(g):
+        for dw, dh in stage_a:
+            ws, hs = (w - dw) % ways, (h - dh) % HEADS
+            spot = v_w.at[x, ws, hs, c, :, columns(g)]
+            remote(spot, spot, wa.at[g, 0], wr.at[g, ws, hs], place.peer_x()).wait_recv()
+        block = v_w.at[x, :, :, c, :, columns(g)]
+        send(block, block, xs.at[g], xr.at[g], place.peer_x())
+        send(block, block, cs.at[g, 0], cr.at[g, 0], place.peer_c())
+
+    def w_beside(g):
+        block = v_w.at[1 - x, :, :, c, :, columns(g)]
+        remote(block, block, xs.at[g], xr.at[g], place.peer_x()).wait_recv()
+        send(block, block, cs.at[g, 1], cr.at[g, 1], place.peer_c())
+
+    def w_ready(g):
+        for k, xx in ((0, x), (1, 1 - x)):
+            block = v_w.at[xx, :, :, 1 - c, :, columns(g)]
+            remote(block, block, cs.at[g, k], cr.at[g, k], place.peer_c()).wait_recv()
+        save(v_w.at[..., columns(g)], w_out.at[..., columns(g)])
+
+    n_first()
+    for k in range(1, HEADS):
+        send(trig_in, trig.at[h], at["t_s"].at[k], at["t_r"].at[h], place.device(h=(h + k) % HEADS))
+    mine[4].wait()
+    send(note, note_c, at["nc_s"].at[0], at["nc_r"].at[0], place.peer_c())
+    w_first(0)
+    mine[0].wait()
+    sends[HEADS - 1].wait_recv()
+    note_c[...] = note_c[...] + note[...]
+    copy = send(note_c, note_x, at["nx_s"].at[0], at["nx_r"].at[0], place.peer_x())
+    n_far()
+    n_near()
+    copy.wait_recv()
+    note_x[...] = note_x[...] + note_c[...]
+    if ways > 1:
+        crossed = [
+            send(note_x, note_w.at[k], at["nw_s"].at[k], at["nw_r"].at[k], device)
+            for k, device in enumerate(place.peers_w())
+        ]
+        for copy in crossed:
+            copy.wait_recv()
+        total = note_x[...]
+        for k in range(ways - 1):
+            total = total + note_w[k]
+        note_c_sent = [one for one in sends if one.src_ref is note_c]
+        for copy in note_c_sent:
+            copy.wait_send()
+        sends[:] = [one for one in sends if one.src_ref is not note_c]
+        note_c[...] = total
+        summed = note_c
+    else:
+        summed = note_x
+    for k in range(1, HEADS):
+        h2 = (h + k) % HEADS
+        send(summed.at[h2], note_h.at[h], at["nh_s"].at[k], at["nh_r"].at[h], place.device(h=h2))
+    n_last()
+    w_across(0)
+    w_first(1)
+
+    mine[3].wait()
+    for k in range(1, HEADS):
+        hs = (h - k) % HEADS
+        remote(trig.at[hs], trig.at[hs], at["t_s"].at[k], at["t_r"].at[hs], place.peer_x()).wait_recv()
+    lane = lax.broadcasted_iota(jnp.int32, (STRIPE, 128), 1)
+    for hh in range(HEADS):
+        @pl.loop(0, runs)
+        def _(run):
+            cosine, sine = trig[hh, 0, pl.ds(run, 1)], trig[hh, 1, pl.ds(run, 1)]
+            full = sine * step_in[0] + cosine * step_in[1]
+            here = pl.ds(hh * STRIPE, STRIPE)
+            v_turn[0, run, here] = cosine * step_in[0] - sine * step_in[1]
+            v_turn[1, run, here] = jnp.where(lane < ROT // 2, -full, 0.0)
+            v_turn[2, run, here] = jnp.where(lane < ROT // 2, 0.0, full)
+    save(v_turn, turn_out)
+    w_beside(0)
     g_first()
-    for copy in copies:
-        copy.start()
-
-    def arrived(full, recv, xs, ws, hs, cs):
-        place_ref = full.at[xs, ws, hs, cs]
-        remote(place_ref, place_ref, local.at[0], recv.at[xs, ws, hs, cs], place.peer_x()).wait_recv()
-
-    for s in range(LINE - 1):
-        n_step(s)
-    for dw, dh in stage_a:
-        ws, hs = (w - dw) % ways, (h - dh) % HEADS
-        for full, _, to_x, to_c, recv in pairs:
-            arrived(full, recv, x, ws, hs, c)
-            block = full.at[x, ws, hs, c]
-            send(block, block, to_x.at[ws, hs], recv.at[x, ws, hs, c], place.peer_x())
-            send(block, block, to_c.at[x, ws, hs], recv.at[x, ws, hs, c], place.peer_c())
-    for s in range(LINE - 1):
-        g_step(s)
-    for dw, dh in [(0, 0)] + stage_a:
-        ws, hs = (w - dw) % ways, (h - dh) % HEADS
-        for full, _, _, to_c, recv in pairs:
-            arrived(full, recv, 1 - x, ws, hs, c)
-            block = full.at[1 - x, ws, hs, c]
-            send(block, block, to_c.at[1 - x, ws, hs], recv.at[1 - x, ws, hs, c], place.peer_c())
-    n_finish()
-    g_finish()
-    for dw, dh in [(0, 0)] + stage_a:
-        ws, hs = (w - dw) % ways, (h - dh) % HEADS
-        for full, _, _, _, recv in pairs:
-            for xs in (x, 1 - x):
-                arrived(full, recv, xs, ws, hs, 1 - c)
-    for copy in copies:
+    w_first(2)
+    bias = summed[h]
+    for k in range(1, HEADS):
+        hs = (h - k) % HEADS
+        remote(note_h.at[hs], note_h.at[hs], at["nh_s"].at[k], at["nh_r"].at[hs], place.peer_x()).wait_recv()
+        bias = bias + note_h[hs]
+    note_h[h] = bias
+    save(note_h.at[h], note_out)
+    mine[1].wait()
+    n_side()
+    save(v_n, n_out)
+    w_ready(0)
+
+    shrink = list(range(3, len(cuts)))
+    if not fuse:
+        g_far()
+        w_across(1)
+        for g in shrink:
+            w_first(g)
+        g_near()
+        g_last()
+        w_beside(1)
+        w_ready(1)
+        w_across(2)
+        w_beside(2)
+        for g in shrink:
+            w_across(g)
+        mine[2].wait()
+        g_side()
+        save(v_g, g_out)
+        w_ready(2)
+        for g in shrink:
+            w_beside(g)
+            w_ready(g)
+    else:
+        v_q, v_do, v_kv, v_exp, v_act, v_dexp, v_att, v_dq, v_dkv, s_ref, sum_ref, kx_s, kx_r, kc_s, kc_r = (
+            at[k] for k in ["v_q", "v_do", "v_kv", "v_exp", "v_act", "v_dexp", "v_att", "v_dq", "v_dkv", "s_ref", "sum_ref", "kx_s", "kx_r", "kc_s", "kc_r"]
+        )
+        tile = 256
+
+        def weight(first):
+            return v_w[..., first : first + tile].reshape(width, tile)
+
+        def bias_of(t):
+            return jnp.concatenate([note_h[h, 2 * t : 2 * t + 1], note_h[h, 2 * t + 1 : 2 * t + 2]], 1)
+
+        parts = 4
+        span = runs // parts
+        slot = x * 2 + c
+
+        def project(p):
+            lo = p * span
+            left = v_n[lo : lo + span].reshape(span * per_run, width)
+            tables = [v_turn[t, lo : lo + span].reshape(span * per_run, 128) for t in range(3)]
+            for t in range(3):
+                value = jnp.dot(left, weight(t * HEAD_DIM), preferred_element_type=F32) + bias_of(t)
+                if t < 2:
+                    value = turn(value, tables, 1.0)
+                if t == 0:
+                    v_q[lo : lo + span] = (value * (1.0 / math.sqrt(HEAD_DIM))).astype(BF).reshape(span, per_run, HEAD_DIM)
+                else:
+                    here = pl.ds((t - 1) * HEAD_DIM, HEAD_DIM)
+                    v_kv[lo : lo + span, slot, :, here] = value.astype(BF).reshape(span, per_run, HEAD_DIM)
+            block = v_kv.at[lo : lo + span, slot]
+            send(block, block, kx_s.at[p], kx_r.at[p], place.peer_x())
+            send(block, block, kc_s.at[0, p], kc_r.at[0, p], place.peer_c())
+
+        def kv_beside(p):
+            block = v_kv.at[pl.ds(p * span, span), (1 - x) * 2 + c]
+            remote(block, block, kx_s.at[p], kx_r.at[p], place.peer_x()).wait_recv()
+            send(block, block, kc_s.at[1, p], kc_r.at[1, p], place.peer_c())
+
+        def kv_ready(p):
+            for k, xx in ((0, x), (1, 1 - x)):
+                block = v_kv.at[pl.ds(p * span, span), xx * 2 + 1 - c]
+                remote(block, block, kc_s.at[k, p], kc_r.at[k, p], place.peer_c()).wait_recv()
+
+        half = runs * per_run // 2
+
+        def expand(m, t):
+            left = v_n[m * runs // 2 : (m + 1) * runs // 2].reshape(half, width)
+            value = jnp.dot(left, weight(cuts[1][0] + t * tile), preferred_element_type=F32) + bias_of(3 + t)
+            v_exp[m * half : (m + 1) * half, t * tile : (t + 1) * tile] = value
+            active = 0.5 * value * (1.0 + lax.erf(value * math.sqrt(0.5)))
+            v_act[m * half : (m + 1) * half, t * tile : (t + 1) * tile] = active.astype(BF)
+
+        def shrink_back(m, t):
+            left = v_g[m * runs // 2 : (m + 1) * runs // 2].reshape(half, width)
+            value = jnp.dot(left, weight(cuts[3][0] + t * tile), preferred_element_type=F32)
+            slope = gelu_slope(v_exp[m * half : (m + 1) * half, t * tile : (t + 1) * tile])
+            v_dexp[m * half : (m + 1) * half, t * tile : (t + 1) * tile] = (value * slope).astype(BF)
+
+        for p in range(parts):
+            project(p)
+        g_far()
+        w_across(1)
+        for g in shrink:
+            w_first(g)
+        g_near()
+        for p in range(parts):
+            kv_beside(p)
+        g_last()
+        w_beside(1)
+        for p in range(parts):
+            kv_ready(p)
+        w_ready(1)
+        w_across(2)
+        for t in range(v_act.shape[1] // tile):
+            for m in range(2):
+                expand(m, t)
+            if t == 0:
+                w_beside(2)
+        save(v_act, at["act_out"])
+        mine[2].wait()
+        g_side()
+        save(v_g, g_out)
+        w_ready(2)
+        for m in range(2):
+            left = v_g[m * runs // 2 : (m + 1) * runs // 2].reshape(half, width)
+            value = jnp.dot(left, weight(cuts[2][0]), preferred_element_type=F32)
+            v_do[m * runs // 2 : (m + 1) * runs // 2] = value.astype(BF).reshape(runs // 2, per_run, HEAD_DIM)
+
+        row_tok, col_tok = at["row_tok"], at["col_tok"]
+
+        def segment(tokens):
+            return jnp.where(tokens < prompt_total, -1 - tokens // PROMPT, (tokens - prompt_total) // CONT)
+
+        def mask(i, k):
+            if i != k:
+                return None
+            rows, cols = row_tok[i], col_tok[k]
+            return (segment(rows) == segment(cols)) & (cols <= rows)
+
+        for i in range(runs):
+            attention_step(
+                i, prompt_runs, mask, v_q, v_do, lambda k: v_kv[k, :, :, :HEAD_DIM].reshape(4 * per_run, HEAD_DIM),
+                lambda k: v_kv[k, :, :, HEAD_DIM:].reshape(4 * per_run, HEAD_DIM), v_turn, v_att, v_dq, s_ref, sum_ref,
+            )
+            if i < len(shrink):
+                w_across(shrink[i])
+            elif i < 2 * len(shrink):
+                w_beside(shrink[i - len(shrink)])
+        v_dkv[...] = sum_ref[...].astype(BF).reshape(v_dkv.shape)
+        save(v_att, at["att_out"])
+        save(v_dq, at["dq_out"])
+        save(v_dkv, at["dkv_out"])
+        for t, g in enumerate(shrink):
+            w_ready(g)
+            for m in range(2):
+                shrink_back(m, t)
+        save(v_dexp, at["dexp_out"])
+    for copy in puts:
         copy.wait()
     for copy in sends:
         copy.wait_send()
@@ -234,25 +435,60 @@
     g_sent()
 
 
-def gather_all(ways, normed, grads, weights, notes):
+def open_all(ways, rows, hidden, prompt_runs, prompt_total, normed, grads, weights, notes, trig, steps, row_tok, col_tok):
     runs, _, width = normed.shape
-    _, rows, columns = weights.shape
-    blocks = (2, ways, HEADS, 2)
-    shapes = (
-        jax.ShapeDtypeStruct((runs, HEADS, STRIPE, width), BF),
-        jax.ShapeDtypeStruct((runs, HEADS, STRIPE, width), BF),
-        jax.ShapeDtypeStruct(blocks + (rows, columns), BF),
-        jax.ShapeDtypeStruct(blocks + notes.shape[1:], F32),
-    )
-    row_sems = [DMA((LINE,)), DMA((LINE,)), DMA((LINE + 1,)), DMA((HEADS,))]
-    block_sems = [DMA((ways * HEADS,)), DMA((ways, HEADS)), DMA((2, ways, HEADS)), DMA(blocks)]
-    return call(
-        functools.partial(gather_kernel, ways),
-        shapes,
-        (normed, grads, weights, notes),
-        [DMA((4,))] + row_sems + row_sems + block_sems + block_sems,
-        0,
-    )
+    columns = weights.shape[2]
+    fuse = ways == 1 and prompt_total == PROMPT
+    head3 = 3 * HEAD_DIM
+    cuts = [(0, head3), (head3, hidden), (head3 + hidden, HEAD_DIM)]
+    cuts += [(head3 + hidden + HEAD_DIM + k * 256, 256) for k in range(hidden // 256)]
+    blocks = (2, ways, HEADS, 2, rows, columns)
+    group = runs * HEADS * STRIPE
+    per_run = HEADS * STRIPE
+
+    def shape(dims, kind=BF):
+        return jax.ShapeDtypeStruct(dims, kind)
+
+    gathered = (runs, HEADS, STRIPE, width)
+    tables = (3, runs, per_run, 128)
+    outs = [shape(gathered), shape(gathered), shape(blocks), shape(notes.shape[1:], F32), shape(tables, F32)]
+    if fuse:
+        outs += [
+            shape((runs, per_run, HEAD_DIM)), shape((group, hidden)), shape((group, hidden)),
+            shape((runs, per_run, HEAD_DIM)), shape((runs, 4, per_run, 2 * HEAD_DIM)),
+        ]
+    extra = max(ways - 1, 1)
+    count = len(cuts)
+    scratch = [
+        pltpu.VMEM(gathered, BF), pltpu.VMEM(gathered, BF), pltpu.VMEM(blocks, BF), pltpu.VMEM(tables, F32),
+        pltpu.VMEM((HEADS,) + trig.shape, F32),
+        pltpu.VMEM(notes.shape, F32), pltpu.VMEM(notes.shape, F32), pltpu.VMEM(notes.shape, F32),
+        pltpu.VMEM((extra,) + notes.shape, F32), pltpu.VMEM(notes.shape, F32),
+        DMA((5,)), DMA((count + 10,)),
+        DMA((7,)), DMA((HEADS,)), DMA((7,)), DMA((HEADS,)),
+        DMA((count, ways * HEADS)), DMA((count, ways, HEADS)), DMA((count,)), DMA((count,)), DMA((count, 2)), DMA((count, 2)),
+        DMA((HEADS,)), DMA((HEADS,)), DMA((1,)), DMA((1,)), DMA((1,)), DMA((1,)), DMA((extra,)), DMA((extra,)),
+        DMA((HEADS,)), DMA((HEADS,)),
+    ]
+    if fuse:
+        scratch += [
+            pltpu.VMEM((runs, per_run, HEAD_DIM), BF), pltpu.VMEM((runs, per_run, HEAD_DIM), BF),
+            pltpu.VMEM((runs, 4, per_run, 2 * HEAD_DIM), BF), pltpu.VMEM((group, hidden), F32),
+            pltpu.VMEM((group, hidden), BF), pltpu.VMEM((group, hidden), BF),
+            pltpu.VMEM((runs, per_run, HEAD_DIM), BF), pltpu.VMEM((runs, per_run, HEAD_DIM), BF),
+            pltpu.VMEM((runs, 4, per_run, 2 * HEAD_DIM), BF),
+            pltpu.VMEM((per_run, (prompt_runs + 1) * 4 * per_run), F32),
+            pltpu.VMEM((runs, 4 * per_run, 2 * HEAD_DIM), F32),
+            DMA((4,)), DMA((4,)), DMA((2, 4)), DMA((2, 4)),
+        ]
+    return fuse, pl.pallas_call(
+        functools.partial(open_kernel, ways, tuple(cuts), fuse, prompt_runs, prompt_total),
+        out_shape=tuple(outs),
+        in_specs=[ANY] * 5 + [VMEM] * 3,
+        out_specs=(ANY,) * len(outs),
+        scratch_shapes=scratch,
+        compiler_params=pltpu.CompilerParams(collective_id=0, has_side_effects=True, vmem_limit_bytes=62 * 2**20),
+    )(normed, grads, weights, notes, trig, steps, row_tok, col_tok)
 
 
 def exchange_kernel(ways, own, full, local, to_w, to_x, to_c, recv):
@@ -324,7 +560,7 @@
     return jnp.concatenate([front * cosine + moved * sign, u[:, 128:]], 1)
 
 
-def finish_kernel(ways, att, act, dexp, dq, dkv, tables, w_out, w_in, n_all, g_all, note,
+def finish_kernel(ways, att, act, dexp, dq, dkv, tables, w_all, n_all, g_all, note,
                   out_sum, e_sum, own_a, own_b, note_all,
                   v_left, v_right, v_w, v_turn, kv_own, kv_c, kv_x,
                   o_p, o_y, o_1, o_2, e_p, e_y, e_1, e_2,
@@ -343,7 +579,7 @@
     hp = 256 // (2 * rows)
     tiles = HEADS // hp
     a_cols, b_cols = own_a.shape[2], own_b.shape[2]
-    inner = w_out.shape[1]
+    inner = v_left.shape[-1]
     head3 = 3 * HEAD_DIM
     group = runs * HEADS * STRIPE
     sends = []
@@ -364,7 +600,7 @@
     early = [
         fetch(att, v_left.at[..., :HEAD_DIM], 0),
         fetch(act, v_left.at[..., HEAD_DIM:], 1),
-        fetch(w_out, v_w.at[:, :inner], 2),
+        fetch(w_all.at[:, pl.ds(v_right.shape[-1], inner)], v_w.at[:, :inner], 2),
     ]
 
     kv_first, kv_mine = [], []
@@ -436,7 +672,7 @@
     for q in range(chunks):
         partial(v_left, q, o_p, inner)
         o_step[q] = o_start(q)
-    w_load = fetch(w_in, v_w, 6)
+    w_load = fetch(w_all.at[:, pl.ds(0, v_right.shape[-1])], v_w, 6)
 
     def kv_add(k, final):
         kv_mine[k].wait()
@@ -691,9 +927,10 @@
             copy.wait_send()
 
 
-def finish(ways, rows, att, act, dexp, dq, dkv, tables, w_out, w_in, n_all, g_all, note):
-    width, inner = w_out.shape
-    right = w_in.shape[1]
+def finish(ways, rows, att, act, dexp, dq, dkv, tables, w_all, n_all, g_all, note):
+    width = w_all.shape[0]
+    inner = att.shape[-1] + act.shape[-1]
+    right = w_all.shape[1] - inner
     head3 = 3 * HEAD_DIM
     a_cols, b_cols = inner + right - head3, head3
     group = n_all.shape[0]
@@ -755,7 +992,7 @@
     )
     ins = (
         att.reshape(lines + (HEAD_DIM,)), act.reshape(lines + (inner - HEAD_DIM,)), dexp.reshape(lines + (right - head3,)),
-        dq.reshape(lines + (HEAD_DIM,)), dkv, tables, w_out, w_in, n_all, g_all, note,
+        dq.reshape(lines + (HEAD_DIM,)), dkv, tables, w_all, n_all, g_all, note,
     )
     return pl.pallas_call(
         functools.partial(finish_kernel, ways),
@@ -767,16 +1004,61 @@
     )(*ins)
 
 
+def attention_step(i, prompt_runs, mask, q_ref, do_ref, key, value_of, turn_ref, o_ref, dq_ref, s_ref, sum_ref):
+    m = q_ref.shape[1]
+    keys = sum_ref.shape[1]
+    by_rows = (((1,), (1,)), ((), ()))
+    by_tokens = (((0,), (0,)), ((), ()))
+
+    def dot(a, b, dims=(((1,), (0,)), ((), ()))):
+        return lax.dot_general(a, b, dims, preferred_element_type=F32)
+
+    pieces = list(range(min(i + 1, prompt_runs))) + ([i] if i >= prompt_runs else [])
+    q = q_ref[i]
+    peak = None
+    for at, k in enumerate(pieces):
+        s = dot(q, key(k), by_rows)
+        keep = mask(i, k)
+        if keep is not None:
+            s = jnp.where(keep, s, -1e30)
+        s_ref[:, at * keys : (at + 1) * keys] = s
+        top = jnp.max(s, -1, keepdims=True)
+        peak = top if peak is None else jnp.maximum(peak, top)
+    total = jnp.zeros((m, 1), F32)
+    out = jnp.zeros((m, HEAD_DIM), F32)
+    for at, k in enumerate(pieces):
+        p = jnp.exp(s_ref[:, at * keys : (at + 1) * keys] - peak)
+        keep = mask(i, k)
+        if keep is not None:
+            p = jnp.where(keep, p, 0.0)
+        s_ref[:, at * keys : (at + 1) * keys] = p
+        total = total + jnp.sum(p, -1, keepdims=True)
+        out = out + dot(p.astype(BF), value_of(k))
+    inverse = 1.0 / total
+    out = out * inverse
+    o_ref[i] = out.astype(BF)
+    do = do_ref[i]
+    delta = jnp.sum(out * do.astype(F32), -1, keepdims=True)
+    dq = jnp.zeros((m, HEAD_DIM), F32)
+    for at, k in enumerate(pieces):
+        p = s_ref[:, at * keys : (at + 1) * keys] * inverse
+        dp = dot(do, value_of(k), by_rows)
+        ds = (p * (dp - delta)).astype(BF)
+        dq = dq + dot(ds, key(k))
+        dk = dot(ds, q, by_tokens)
+        dv = dot(p.astype(BF), do, by_tokens)
+        if i == k:
+            sum_ref[k, :, :HEAD_DIM] = dk
+            sum_ref[k, :, HEAD_DIM:] = dv
+        else:
+            sum_ref[k, :, :HEAD_DIM] = sum_ref[k, :, :HEAD_DIM] + dk
+            sum_ref[k, :, HEAD_DIM:] = sum_ref[k, :, HEAD_DIM:] + dv
+    dq = (dq * (1.0 / math.sqrt(HEAD_DIM))).astype(BF).astype(F32)
+    dq_ref[i] = turn(dq, [turn_ref[t, i] for t in range(3)], -1.0).astype(BF)
+
+
 def attention_kernel(prompt_runs, one_prompt, q_ref, do_ref, kv_ref, row_ref, col_ref, turn_ref,
                      o_ref, dq_ref, dkv_ref, s_ref, sum_ref):
-    runs, m, _ = q_ref.shape
-    keys = kv_ref.shape[1]
-    by_rows = (((1,), (1,)), ((), ()))
-    by_tokens = (((0,), (0,)), ((), ()))
-
-    def dot(a, b, dims):
-        return lax.dot_general(a, b, dims, preferred_element_type=F32)
-
     def mask(i, k):
         rows, cols = row_ref[i], col_ref[k]
         if i == k:
@@ -785,50 +1067,11 @@
             return None
         return rows[:, 2:3] == cols[2:3, :]
 
-    for i in range(runs):
-        pieces = list(range(min(i + 1, prompt_runs))) + ([i] if i >= prompt_runs else [])
-        q = q_ref[i]
-        peak = None
-        for at, k in enumerate(pieces):
-            s = dot(q, kv_ref[k, :, :HEAD_DIM], by_rows)
-            keep = mask(i, k)
-            if keep is not None:
-                s = jnp.where(keep, s, -1e30)
-            s_ref[:, at * keys : (at + 1) * keys] = s
-            top = jnp.max(s, -1, keepdims=True)
-            peak = top if peak is None else jnp.maximum(peak, top)
-        total = jnp.zeros((m, 1), F32)
-        out = jnp.zeros((m, HEAD_DIM), F32)
-        for at, k in enumerate(pieces):
-            s = s_ref[:, at * keys : (at + 1) * keys]
-            p = jnp.exp(s - peak)
-            keep = mask(i, k)
-            if keep is not None:
-                p = jnp.where(keep, p, 0.0)
-            s_ref[:, at * keys : (at + 1) * keys] = p
-            total = total + jnp.sum(p, -1, keepdims=True)
-            out = out + dot(p.astype(BF), kv_ref[k, :, HEAD_DIM:], (((1,), (0,)), ((), ())))
-        inverse = 1.0 / total
-        out = out * inverse
-        o_ref[i] = out.astype(BF)
-        do = do_ref[i]
-        delta = jnp.sum(out * do.astype(F32), -1, keepdims=True)
-        dq = jnp.zeros((m, HEAD_DIM), F32)
-        for at, k in enumerate(pieces):
-            p = s_ref[:, at * keys : (at + 1) * keys] * inverse
-            dp = dot(do, kv_ref[k, :, HEAD_DIM:], by_rows)
-            ds = (p * (dp - delta)).astype(BF)
-            dq = dq + dot(ds, kv_ref[k, :, :HEAD_DIM], (((1,), (0,)), ((), ())))
-            dk = dot(ds, q, by_tokens)
-            dv = dot(p.astype(BF), do, by_tokens)
-            if i == k:
-                sum_ref[k, :, :HEAD_DIM] = dk
-                sum_ref[k, :, HEAD_DIM:] = dv
-            else:
-                sum_ref[k, :, :HEAD_DIM] = sum_ref[k, :, :HEAD_DIM] + dk
-                sum_ref[k, :, HEAD_DIM:] = sum_ref[k, :, HEAD_DIM:] + dv
-        dq = (dq * (1.0 / math.sqrt(HEAD_DIM))).astype(BF).astype(F32)
-        dq_ref[i] = turn(dq, [turn_ref[t, i] for t in range(3)], -1.0).astype(BF)
+    for i in range(q_ref.shape[0]):
+        attention_step(
+            i, prompt_runs, mask, q_ref, do_ref, lambda k: kv_ref[k, :, :HEAD_DIM], lambda k: kv_ref[k, :, HEAD_DIM:],
+            turn_ref, o_ref, dq_ref, s_ref, sum_ref,
+        )
     dkv_ref[...] = sum_ref[...].astype(BF)
 
 
@@ -950,54 +1193,32 @@
     lanes = 128
     note_rows = block_columns // lanes
 
-    def padded(values):
-        return jnp.pad(values, (0, lanes - values.shape[0]))
-
-    tail = jnp.stack([padded(dense_bias.astype(F32) + shrink_bias.astype(F32)), padded(base_position.astype(F32))])
+    slice_rows = width // lanes
+    own_out_bias = lax.dynamic_update_slice_in_dim(
+        jnp.zeros((width,), F32), dense_bias.astype(F32) + shrink_bias.astype(F32), me * rows, 0
+    )
     notes = jnp.concatenate(
-        [bias_parts.reshape(HEADS, note_rows, lanes), jnp.broadcast_to(tail[None], (HEADS, 2, lanes))], 1
-    )
-
-    n_all, g_all, w_all, m_all = gather_all(
-        ways, normed_low.reshape(runs, STRIPE, width), grad_low.reshape(runs, STRIPE, width), weights, notes
-    )
-    n_all = n_all.reshape(group_rows, width)
-    g_all = g_all.reshape(group_rows, width)
-    w_all = w_all.reshape(width, block_columns + HEAD_DIM + hidden)
-    bias_block = jnp.sum(m_all[..., :note_rows, :], (0, 1, 2, 3)).reshape(block_columns)
-    out_bias = m_all[..., note_rows, :rows].reshape(width)
-    group_position = lax.dynamic_index_in_dim(m_all[:, :, :, :, note_rows + 1, :runs], x, 0, False)
-    group_position = lax.dynamic_index_in_dim(group_position, w, 0, False)
-    group_position = lax.dynamic_index_in_dim(group_position, c, 1, False)
+        [
+            bias_parts.reshape(HEADS, note_rows, lanes),
+            jnp.broadcast_to(own_out_bias.reshape(1, slice_rows, lanes), (HEADS, slice_rows, lanes)),
+            jnp.zeros((HEADS, -(note_rows + slice_rows) % 8, lanes), F32),
+        ],
+        1,
+    )
+
+    def trig_of(positions):
+        angles = angles_of(positions)
+        cosine, sine = jnp.cos(angles), jnp.sin(angles)
+        rest = ((0, 0), (0, lanes - ROT))
+        return jnp.stack(
+            [
+                jnp.pad(jnp.concatenate([cosine, cosine], 1), rest, constant_values=1.0),
+                jnp.pad(jnp.concatenate([sine, sine], 1), rest),
+            ]
+        )
+
     within = jnp.arange(STRIPE, dtype=jnp.int32)
-    position = (group_position.T[:, :, None] + within.astype(F32)).reshape(group_rows)
-    angles = angles_of(position)
-    cosine, sine = jnp.cos(angles), jnp.sin(angles)
     rows_run = group_rows // runs
-    rest = ((0, 0), (0, 128 - ROT))
-    tables = jnp.stack(
-        [
-            jnp.pad(jnp.concatenate([cosine, cosine], 1), rest, constant_values=1.0),
-            jnp.pad(-sine, ((0, 0), (0, 128 - ROT // 2))),
-            jnp.pad(sine, ((0, 0), (ROT // 2, 128 - ROT))),
-        ]
-    ).reshape(3, runs, rows_run, 128)
-
-    w_in = w_all[:, :block_columns]
-    w_out = w_all[:, block_columns:]
-    mixed = jnp.dot(n_all, w_in[:, :head3], preferred_element_type=F32) + bias_block[:head3]
-    queries = (rotate(mixed[:, :HEAD_DIM], cosine, sine) * (1.0 / math.sqrt(HEAD_DIM))).astype(BF)
-    keys = rotate(mixed[:, HEAD_DIM : 2 * HEAD_DIM], cosine, sine).astype(BF)
-    values = mixed[:, 2 * HEAD_DIM :].astype(BF)
-    pairs = exchange(ways, jnp.concatenate([keys, values], 1).reshape(runs, rows_run, 2 * HEAD_DIM))
-    pairs = pairs.reshape(runs, run_size, 2 * HEAD_DIM)
-
-    d_attended = jnp.dot(g_all, w_out[:, :HEAD_DIM], preferred_element_type=F32).astype(BF)
-    expanded = jnp.dot(n_all, w_in[:, head3:], preferred_element_type=F32) + bias_block[head3:]
-    activated, gelu_back = jax.vjp(lambda v: jax.nn.gelu(v, approximate=False), expanded)
-    activated = activated.astype(BF)
-    d_activated = jnp.dot(g_all, w_out[:, HEAD_DIM:], preferred_element_type=F32)
-    d_expanded = gelu_back(d_activated)[0].astype(BF)
 
     bases = base.reshape(2, ways, HEADS, 2, runs)
     own_base = lax.dynamic_index_in_dim(bases, x, 0, False)
@@ -1006,24 +1227,51 @@
     row_tokens = (own_base.T[:, :, None] + within).reshape(runs, rows_run)
     col_tokens = (bases.transpose(4, 1, 0, 3, 2)[..., None] + within).reshape(runs, run_size)
 
-    def meta(tokens):
-        is_prompt = tokens < prompt_total
-        cont = (tokens - prompt_total) // CONT
-        if one_prompt:
-            prompt = jnp.zeros_like(tokens)
-        else:
+    fuse, opened = open_all(
+        ways, rows, hidden, prompt_runs, prompt_total,
+        normed_low.reshape(runs, STRIPE, width), grad_low.reshape(runs, STRIPE, width), weights, notes,
+        trig_of(base_position), trig_of(within), row_tokens[:, :, None], col_tokens[:, None, :],
+    )
+    n_all, g_all, w_all, note, tables = opened[:5]
+    n_all = n_all.reshape(group_rows, width)
+    g_all = g_all.reshape(group_rows, width)
+    w_all = w_all.reshape(width, block_columns + HEAD_DIM + hidden)
+    bias_block = note[:note_rows].reshape(block_columns)
+    out_bias = note[note_rows : note_rows + slice_rows].reshape(width)
+    if fuse:
+        attended, activated, d_expanded, d_queries, d_pairs = opened[5:]
+        attended = attended.reshape(group_rows, HEAD_DIM)
+    else:
+        flat = tables.reshape(3, group_rows, lanes)
+        cosine, sine = flat[0, :, : ROT // 2], flat[2, :, ROT // 2 : ROT]
+        w_in, w_out = w_all[:, :block_columns], w_all[:, block_columns:]
+        mixed = jnp.dot(n_all, w_in[:, :head3], preferred_element_type=F32) + bias_block[:head3]
+        queries = (rotate(mixed[:, :HEAD_DIM], cosine, sine) * (1.0 / math.sqrt(HEAD_DIM))).astype(BF)
+        keys = rotate(mixed[:, HEAD_DIM : 2 * HEAD_DIM], cosine, sine).astype(BF)
+        values = mixed[:, 2 * HEAD_DIM :].astype(BF)
+        pairs = exchange(ways, jnp.concatenate([keys, values], 1).reshape(runs, rows_run, 2 * HEAD_DIM))
+        pairs = pairs.reshape(runs, run_size, 2 * HEAD_DIM)
+        d_attended = jnp.dot(g_all, w_out[:, :HEAD_DIM], preferred_element_type=F32).astype(BF)
+        expanded = jnp.dot(n_all, w_in[:, head3:], preferred_element_type=F32) + bias_block[head3:]
+        activated, gelu_back = jax.vjp(lambda v: jax.nn.gelu(v, approximate=False), expanded)
+        activated = activated.astype(BF)
+        d_activated = jnp.dot(g_all, w_out[:, HEAD_DIM:], preferred_element_type=F32)
+        d_expanded = gelu_back(d_activated)[0].astype(BF)
+
+        def meta(tokens):
+            is_prompt = tokens < prompt_total
+            cont = (tokens - prompt_total) // CONT
             matches = cont[..., None] == jnp.arange(cont_parent.shape[0], dtype=jnp.int32)
             prompt = jnp.where(is_prompt, tokens // PROMPT, jnp.sum(jnp.where(matches, cont_parent, 0), -1))
-        segment = jnp.where(is_prompt, -1 - tokens // PROMPT, cont)
-        return tokens, segment, prompt
-
-    row_meta = jnp.stack(meta(row_tokens), -1)
-    col_meta = jnp.stack(meta(col_tokens), 1)
-    attended, d_queries, d_pairs = attention(
-        prompt_runs, one_prompt,
-        queries.reshape(runs, rows_run, HEAD_DIM), d_attended.reshape(runs, rows_run, HEAD_DIM),
-        pairs, row_meta, col_meta, tables,
-    )
+            segment = jnp.where(is_prompt, -1 - tokens // PROMPT, cont)
+            return tokens, segment, prompt
+
+        attended, d_queries, d_pairs = attention(
+            prompt_runs, one_prompt,
+            queries.reshape(runs, rows_run, HEAD_DIM), d_attended.reshape(runs, rows_run, HEAD_DIM),
+            pairs, jnp.stack(meta(row_tokens), -1), jnp.stack(meta(col_tokens), 1), tables,
+        )
+        attended = attended.reshape(group_rows, HEAD_DIM)
 
     d_pairs = d_pairs.reshape(runs, ways, 4, rows_run, 2 * HEAD_DIM)
     if ways > 1:
@@ -1038,7 +1286,7 @@
     )
     out_sum, e_sum, owned_a, owned_b, owned_notes = finish(
         ways, rows, attended, activated, d_expanded, d_queries, d_pairs,
-        tables, w_out, w_in, n_all, g_all, sum_note,
+        tables, w_all, n_all, g_all, sum_note,
     )
     output = restored((states + out_sum.reshape(tok_dev, width) + out_bias).astype(BF))
     e_sum = e_sum.reshape(tok_dev, width)

time: 553 us -> 430 us (0.78)
  the two profiles are of different devices: /device:TPU:8 before, /device:TPU:0 now
where the time goes in v3:
time: 430 us; the launch traced here: 425 us
  Pallas kernels  379 us (88%)
  other arithmetic  25.4 us (6%)
  local copies, waits for them, and re-layouts  15.6 us (4%)
    pallas_call x1, Pallas kernels, finish(): pl.pallas_call(functools.partial(finish_kernel, ways), out_shape=shapes,...  192 us
    pallas_call x1, Pallas kernels, open_all(): pl.pallas_call(functools.partial(open_kernel, ways, tuple(cuts), fuse, pr...  187 us

profile of v3, /device:TPU:0, one launch (start us, length us, event | category | flops | bytes accessed | tf_op | source)
XLA Modules:
  0.0 425.0 jit_solution(4485053791587941940)
XLA Ops:
  0.7 0.8 fusion.29
  1.5 0.7 and_select_fusion
  2.2 0.8 select_reduce_fusion.1
  3.0 0.7 convert_element_type.97
  3.6 0.7 convert_element_type.102
  4.3 0.7 convert_element_type.100
  5.0 0.7 convert_element_type.104
  6.6 0.8 add_dynamic-update-slice_fusion.2
  8.2 0.7 add_select_fusion
  8.9 1.3 select_reduce_fusion
  11.4 1.0 copy.100
  12.7 0.9 broadcast_add_fusion.refs_6_
  13.6 1.1 convert_reduce_fusion
  14.7 0.7 maximum_maximum_fusion.1.note
  16.6 1.7 reshape.308
  18.9 1.0 fusion.15
  20.6 0.7 maximum_maximum_fusion.refs_3_
  21.3 1.5 bitcast_bitcast_fusion
  22.8 1.9 pad_maximum_fusion.refs_2_
  24.8 187.1 %shard_map.271 = (bf16[8,8,16,2048]{3,2,1,0:T(8,128)(2,1)}, bf16[8,8,16,2048]{3,2,1,0:T(8,128)(2,1)}, bf16[2,1,8,2,64,3072]{5,4,3,2,1,0:T(8,128)(2,1)}, f32[32,1...) custom-call(bf16[8,16,2048]{2,1,0:T(8,128)(2,1)} %bitcast.144, ...), custom_call_target="tpu_custom_call" | custom-call | tf_op jit(solution)/shard_map/pallas_call | solution.py:484
  211.9 191.9 %shard_map.272 = (f32[8,16,2048]{2,1,0:T(8,128)}, f32[8,16,2048]{2,1,0:T(8,128)}, bf16[8,64,2304]{2,1,0:T(8,128)(2,1)}, bf16[8,64,768]{2,1,0:T(8,128)(2,1)}, f32[8,32,128]{2,1,0:T(8,128)}) custom-call(bf16[8,4,2,16,256]{4,3,2,1,0:T(8,128)(2,1)} %bitcast.147, bf16[8,4,2,16,1024]{4,3,2,1,0:T(8,128)(2,1)} %bitcast.141, bf16[8,4,2,16,1024]{4,3,2,1,0:T(8,128)(2,1)} %bitcast.142, ...), custom_call_target="tpu_custom_call" | custom-call | tf_op jit(solution)/shard_map/pallas_call | solution.py:997
  403.8 1.6 fusion.12
  405.8 1.9 fusion.9
  407.7 1.1 convolution_convert_fusion
  408.9 1.1 convolution_convert_fusion.1
  411.8 1.0 reshape.337
  412.9 0.9 copy.79
  414.9 2.2 fusion.8
  418.3 1.5 copy.88
  419.7 0.8 copy.87
  420.7 1.1 copy-done.5
  421.8 2.5 fusion.4
  (99 shorter events, 10.8 us)
Async XLA Ops:
  0.6 13.0 %copy-start = (bf16[128,2048]{1,0:T(8,128)(2,1)S(1)}, bf16[128,2048]{1,0:T(8,128)(2,1)}, u32[]{:S(2)}) copy-start(bf16[128,2048]{1,0:T(8,128)(2,1)} %param.32) | copy-start | bytes 1572868
  0.7 14.7 %copy-start.7 = (bf16[64,6144]{1,0:T(8,128)(2,1)S(1)}, bf16[64,6144]{1,0:T(8,128)(2,1)}, u32[]{:S(2)}) copy-start(bf16[64,6144]{1,0:T(8,128)(2,1)} %param.22) | copy-start | bytes 2359300
  12.4 3.3 copy-start.14
  16.1 2.1 copy-start.11
  18.2 1.6 copy-start.4
  18.9 1.4 copy-start.15
  21.3 1.5 copy-start.6
  403.7 1.7 copy-start.2
  403.8 1.9 copy-start.12
  403.8 2.0 copy-start.13
  403.8 2.0 copy-start.3
  405.8 18.5 %copy-start.16 = (f32[64]{0:T(128)}, f32[64]{0:T(128)S(1)}, u32[]{:S(2)}) copy-start(f32[64]{0:T(128)S(1)} %dynamic_slice.34) | copy-start | bytes 772
  407.7 4.1 copy-start.10
  413.8 1.1 copy-start.8
  414.3 2.8 copy-start.9
  420.6 1.2 copy-start.5
  420.7 4.1 copy-start.1

commit v4 on v3

--- a/solution.py
+++ b/solution.py
@@ -83,6 +83,8 @@
 
 
 LINE = HEADS // 2
+A_ORDER = (0, 4, 1, 5, 2, 6, 3, 7)
+EARLY = 2
 
 
 def relay_rows(place, own, full, s, r):
@@ -105,9 +107,12 @@
     def arrived(idx):
         remote(full.at[:, idx], full.at[:, idx], s.at[0], r.at[idx], side).wait_recv()
 
-    def first():
-        for k, device in enumerate((far, near, side)):
-            push(own, place.h, k, device)
+    def first_z():
+        push(own, place.h, 0, far)
+        push(own, place.h, 1, near)
+
+    def first_y():
+        push(own, place.h, 2, side)
 
     def from_far():
         idx = index(1 - d1, d0, hy)
@@ -133,24 +138,21 @@
         for copy in made:
             copy.wait_send()
 
-    return first, from_far, from_near, from_near_far, from_side, sent
-
-
-def gelu_slope(v):
-    return 0.5 * (1.0 + lax.erf(v * math.sqrt(0.5))) + v * jnp.exp(-0.5 * v * v) * (1.0 / math.sqrt(2 * math.pi))
+    return first_z, first_y, from_far, from_near, from_near_far, from_side, sent
 
 
 def open_kernel(ways, cuts, fuse, prompt_runs, prompt_total, *refs):
     names = ["n_in", "g_in", "w_in", "note_in", "trig_in", "step_in", "row_tok", "col_tok", "n_out", "g_out", "w_out", "note_out", "turn_out"]
     if fuse:
-        names += ["att_out", "act_out", "dexp_out", "dq_out", "dkv_out"]
+        names += ["left_out", "right_out", "half_out", "part_out"]
     names += ["v_n", "v_g", "v_w", "v_turn", "trig", "note", "note_c", "note_x", "note_w", "note_h", "own", "put"]
     names += ["ns", "nr", "gs", "gr", "wa", "wr", "xs", "xr", "cs", "cr", "t_s", "t_r", "nc_s", "nc_r", "nx_s", "nx_r", "nw_s", "nw_r", "nh_s", "nh_r"]
     if fuse:
-        names += ["v_q", "v_do", "v_kv", "v_exp", "v_act", "v_dexp", "v_att", "v_dq", "v_dkv", "s_ref", "sum_ref", "kx_s", "kx_r", "kc_s", "kc_r"]
+        names += ["v_q", "v_do", "v_kv", "v_slope", "v_left", "v_right", "v_out", "lse", "s_ref", "sum_ref", "kv_c", "kv_x", "o_p", "o_y", "flat", "flat_sem"]
+        names += ["kx_s", "kx_r", "kc_s", "kc_r", "fc_s", "fc_r", "fx_s", "fx_r", "oy_s", "oy_r"]
     at = dict(zip(names, refs, strict=True))
-    (n_in, g_in, w_in, note_in, trig_in, step_in, n_out, g_out, w_out, note_out, turn_out, v_n, v_g, v_w, v_turn) = (
-        at[k] for k in ["n_in", "g_in", "w_in", "note_in", "trig_in", "step_in", "n_out", "g_out", "w_out", "note_out", "turn_out", "v_n", "v_g", "v_w", "v_turn"]
+    (n_in, g_in, w_in, note_in, trig_in, step_in, n_out, g_out, w_out, turn_out, v_n, v_g, v_w, v_turn) = (
+        at[k] for k in ["n_in", "g_in", "w_in", "note_in", "trig_in", "step_in", "n_out", "g_out", "w_out", "turn_out", "v_n", "v_g", "v_w", "v_turn"]
     )
     trig, note, note_c, note_x, note_w, note_h, own, put = (
         at[k] for k in ["trig", "note", "note_c", "note_x", "note_w", "note_h", "own", "put"]
@@ -187,15 +189,17 @@
     ]
     for copy in (mine[4], mine[0], mine[3], mine[1], mine[2]):
         copy.start()
-    n_first, n_far, n_near, n_last, n_side, n_sent = relay_rows(place, n_in, v_n, at["ns"], at["nr"])
-    g_first, g_far, g_near, g_last, g_side, g_sent = relay_rows(place, g_in, v_g, at["gs"], at["gr"])
+    n_first_z, n_first_y, n_far, n_near, n_last, n_side, n_sent = relay_rows(place, n_in, v_n, at["ns"], at["nr"])
+    g_first_z, g_first_y, g_far, g_near, g_last, g_side, g_sent = relay_rows(place, g_in, v_g, at["gs"], at["gr"])
     wa, wr, xs, xr, cs, cr = (at[k] for k in ["wa", "wr", "xs", "xr", "cs", "cr"])
 
     def columns(g):
         return pl.ds(cuts[g][0], cuts[g][1])
 
-    def w_first(g):
+    def w_first(g, odd):
         for k, (dw, dh) in enumerate(stage_a):
+            if dh % 2 != odd:
+                continue
             h2 = (h + dh) % HEADS
             send(w_in.at[h2, :, columns(g)], v_w.at[x, w, h, c, :, columns(g)], wa.at[g, k], wr.at[g, w, h],
                  place.device(w=(w + dw) % ways, h=h2))
@@ -218,102 +222,147 @@
         for k, xx in ((0, x), (1, 1 - x)):
             block = v_w.at[xx, :, :, 1 - c, :, columns(g)]
             remote(block, block, cs.at[g, k], cr.at[g, k], place.peer_c()).wait_recv()
-        save(v_w.at[..., columns(g)], w_out.at[..., columns(g)])
-
-    n_first()
-    for k in range(1, HEADS):
-        send(trig_in, trig.at[h], at["t_s"].at[k], at["t_r"].at[h], place.device(h=(h + k) % HEADS))
-    mine[4].wait()
-    send(note, note_c, at["nc_s"].at[0], at["nc_r"].at[0], place.peer_c())
-    w_first(0)
-    mine[0].wait()
-    sends[HEADS - 1].wait_recv()
-    note_c[...] = note_c[...] + note[...]
-    copy = send(note_c, note_x, at["nx_s"].at[0], at["nx_r"].at[0], place.peer_x())
-    n_far()
-    n_near()
-    copy.wait_recv()
-    note_x[...] = note_x[...] + note_c[...]
-    if ways > 1:
-        crossed = [
-            send(note_x, note_w.at[k], at["nw_s"].at[k], at["nw_r"].at[k], device)
-            for k, device in enumerate(place.peers_w())
-        ]
-        for copy in crossed:
-            copy.wait_recv()
-        total = note_x[...]
-        for k in range(ways - 1):
-            total = total + note_w[k]
-        note_c_sent = [one for one in sends if one.src_ref is note_c]
-        for copy in note_c_sent:
-            copy.wait_send()
-        sends[:] = [one for one in sends if one.src_ref is not note_c]
-        note_c[...] = total
-        summed = note_c
-    else:
+        if cuts[g][0] < w_out.shape[-1]:
+            save(v_w.at[..., columns(g)], w_out.at[..., columns(g)])
+
+    plan = []
+
+    def step(time, body, *given):
+        plan.append((time, len(plan), body, given))
+
+    state = {}
+
+    def trig_send():
+        for k in range(1, HEADS):
+            send(trig_in, trig.at[h], at["t_s"].at[k], at["t_r"].at[h], place.device(h=(h + k) % HEADS))
+
+    def note_first():
+        mine[4].wait()
+        state["note"] = send(note, note_c, at["nc_s"].at[0], at["nc_r"].at[0], place.peer_c())
+
+    def note_cross():
+        state["note"].wait_recv()
+        note_c[...] = note_c[...] + note[...]
+        state["note"] = send(note_c, note_x, at["nx_s"].at[0], at["nx_r"].at[0], place.peer_x())
+
+    def note_out():
+        state["note"].wait_recv()
+        note_x[...] = note_x[...] + note_c[...]
         summed = note_x
-    for k in range(1, HEADS):
-        h2 = (h + k) % HEADS
-        send(summed.at[h2], note_h.at[h], at["nh_s"].at[k], at["nh_r"].at[h], place.device(h=h2))
-    n_last()
-    w_across(0)
-    w_first(1)
-
-    mine[3].wait()
-    for k in range(1, HEADS):
-        hs = (h - k) % HEADS
-        remote(trig.at[hs], trig.at[hs], at["t_s"].at[k], at["t_r"].at[hs], place.peer_x()).wait_recv()
-    lane = lax.broadcasted_iota(jnp.int32, (STRIPE, 128), 1)
-    for hh in range(HEADS):
-        @pl.loop(0, runs)
-        def _(run):
-            cosine, sine = trig[hh, 0, pl.ds(run, 1)], trig[hh, 1, pl.ds(run, 1)]
-            full = sine * step_in[0] + cosine * step_in[1]
-            here = pl.ds(hh * STRIPE, STRIPE)
-            v_turn[0, run, here] = cosine * step_in[0] - sine * step_in[1]
-            v_turn[1, run, here] = jnp.where(lane < ROT // 2, -full, 0.0)
-            v_turn[2, run, here] = jnp.where(lane < ROT // 2, 0.0, full)
-    save(v_turn, turn_out)
-    w_beside(0)
-    g_first()
-    w_first(2)
-    bias = summed[h]
-    for k in range(1, HEADS):
-        hs = (h - k) % HEADS
-        remote(note_h.at[hs], note_h.at[hs], at["nh_s"].at[k], at["nh_r"].at[hs], place.peer_x()).wait_recv()
-        bias = bias + note_h[hs]
-    note_h[h] = bias
-    save(note_h.at[h], note_out)
-    mine[1].wait()
-    n_side()
-    save(v_n, n_out)
-    w_ready(0)
-
-    shrink = list(range(3, len(cuts)))
-    if not fuse:
-        g_far()
-        w_across(1)
-        for g in shrink:
-            w_first(g)
-        g_near()
-        g_last()
-        w_beside(1)
-        w_ready(1)
-        w_across(2)
-        w_beside(2)
-        for g in shrink:
-            w_across(g)
-        mine[2].wait()
-        g_side()
-        save(v_g, g_out)
-        w_ready(2)
-        for g in shrink:
-            w_beside(g)
-            w_ready(g)
-    else:
-        v_q, v_do, v_kv, v_exp, v_act, v_dexp, v_att, v_dq, v_dkv, s_ref, sum_ref, kx_s, kx_r, kc_s, kc_r = (
-            at[k] for k in ["v_q", "v_do", "v_kv", "v_exp", "v_act", "v_dexp", "v_att", "v_dq", "v_dkv", "s_ref", "sum_ref", "kx_s", "kx_r", "kc_s", "kc_r"]
+        if ways > 1:
+            crossed = [
+                send(note_x, note_w.at[k], at["nw_s"].at[k], at["nw_r"].at[k], device)
+                for k, device in enumerate(place.peers_w())
+            ]
+            for copy in crossed:
+                copy.wait_recv()
+            total = note_x[...]
+            for k in range(ways - 1):
+                total = total + note_w[k]
+            state["note"].wait_send()
+            sends[:] = [one for one in sends if one is not state["note"]]
+            note_c[...] = total
+            summed = note_c
+        for k in range(1, HEADS):
+            h2 = (h + k) % HEADS
+            send(summed.at[h2], note_h.at[h], at["nh_s"].at[k], at["nh_r"].at[h], place.device(h=h2))
+        state["summed"] = summed
+
+    def note_sum():
+        bias = state["summed"][h]
+        for k in range(1, HEADS):
+            hs = (h - k) % HEADS
+            remote(note_h.at[hs], note_h.at[hs], at["nh_s"].at[k], at["nh_r"].at[hs], place.peer_x()).wait_recv()
+            bias = bias + note_h[hs]
+        note_h[h] = bias
+        save(note_h.at[h], at["note_out"])
+
+    def turn_tables():
+        mine[3].wait()
+        for k in range(1, HEADS):
+            hs = (h - k) % HEADS
+            remote(trig.at[hs], trig.at[hs], at["t_s"].at[k], at["t_r"].at[hs], place.peer_x()).wait_recv()
+        lane = lax.broadcasted_iota(jnp.int32, (STRIPE, 128), 1)
+        for hh in range(HEADS):
+            @pl.loop(0, runs)
+            def _(run):
+                cosine, sine = trig[hh, 0, pl.ds(run, 1)], trig[hh, 1, pl.ds(run, 1)]
+                full = sine * step_in[0] + cosine * step_in[1]
+                here = pl.ds(hh * STRIPE, STRIPE)
+                v_turn[0, run, here] = cosine * step_in[0] - sine * step_in[1]
+                v_turn[1, run, here] = jnp.where(lane < ROT // 2, -full, 0.0)
+                v_turn[2, run, here] = jnp.where(lane < ROT // 2, 0.0, full)
+        if not fuse:
+            save(v_turn, turn_out)
+
+    def rows_done(copy, side, src, dst):
+        copy.wait()
+        side()
+        if not fuse:
+            save(src, dst)
+
+    flipped = []
+
+    def flip(src, dst, t):
+        spot = at["flat"].at[len(flipped) % 2]
+        if len(flipped) >= 2:
+            flipped[-2].wait()
+        spot[...] = src[..., t * 256 : (t + 1) * 256].reshape(runs * per_run, 256).T
+        copy = pltpu.make_async_copy(spot, dst.at[t * 256 : (t + 1) * 256], at["flat_sem"].at[len(flipped) % 2])
+        copy.start()
+        flipped.append(copy)
+
+    expand_at, dense_at = 3, 4
+    shrink = list(range(5, len(cuts)))
+    step(0, trig_send)
+    step(0.01, n_first_z)
+    step(0.01, n_first_y)
+    for k in range(3):
+        step(0.02, w_first, k, 1)
+        step(0.02, w_first, k, 0)
+    step(0.2, note_first)
+    step(2, mine[0].wait)
+    step(3, note_cross)
+    step(6, note_out)
+    for k in range(3):
+        step(31 + 4 * k, w_across, k)
+        step(43 + 5 * k, w_beside, k)
+        step(66, w_ready, k)
+    step(16, n_near)
+    step(27, n_far)
+    step(36.1, w_first, expand_at, 0)
+    step(52, n_last)
+    step(52.1, w_first, expand_at, 1)
+    step(52.2, w_first, dense_at, 1)
+    step(52.3, w_first, dense_at, 0)
+    step(52.4, g_first_z)
+    step(52.5, g_first_y)
+    step(55, turn_tables)
+    step(57, note_sum)
+    step(65, rows_done, mine[1], n_side, v_n, n_out)
+    step(75.5, w_across, expand_at)
+    step(86, w_across, dense_at)
+    step(86.1, g_near)
+    step(98, g_far)
+    for g in shrink:
+        step(98.1, w_first, g, 1)
+        step(98.2, w_first, g, 0)
+    step(112, w_beside, expand_at)
+    step(113, w_ready, expand_at)
+    step(117, g_last)
+    step(121.5, w_beside, dense_at)
+    step(134, rows_done, mine[2], g_side, v_g, g_out)
+    step(134.1, w_ready, dense_at)
+    for k, g in enumerate(shrink):
+        step((125, 130, 135, 140)[k], w_across, g)
+        step((135.6, 142, 147, 152)[k], w_beside, g)
+        step(156, w_ready, g)
+    if fuse:
+        v_q, v_do, v_kv, v_slope, v_left, v_right, v_out, lse, s_ref, sum_ref, kv_c, kv_x, o_p, o_y = (
+            at[k] for k in ["v_q", "v_do", "v_kv", "v_slope", "v_left", "v_right", "v_out", "lse", "s_ref", "sum_ref", "kv_c", "kv_x", "o_p", "o_y"]
         )
+        kx_s, kx_r, kc_s, kc_r = (at[k] for k in ["kx_s", "kx_r", "kc_s", "kc_r"])
+        kv_sends = []
         tile = 256
 
         def weight(first):
@@ -340,13 +389,13 @@
                     here = pl.ds((t - 1) * HEAD_DIM, HEAD_DIM)
                     v_kv[lo : lo + span, slot, :, here] = value.astype(BF).reshape(span, per_run, HEAD_DIM)
             block = v_kv.at[lo : lo + span, slot]
-            send(block, block, kx_s.at[p], kx_r.at[p], place.peer_x())
-            send(block, block, kc_s.at[0, p], kc_r.at[0, p], place.peer_c())
+            kv_sends.append(send(block, block, kx_s.at[p], kx_r.at[p], place.peer_x()))
+            kv_sends.append(send(block, block, kc_s.at[0, p], kc_r.at[0, p], place.peer_c()))
 
         def kv_beside(p):
             block = v_kv.at[pl.ds(p * span, span), (1 - x) * 2 + c]
             remote(block, block, kx_s.at[p], kx_r.at[p], place.peer_x()).wait_recv()
-            send(block, block, kc_s.at[1, p], kc_r.at[1, p], place.peer_c())
+            kv_sends.append(send(block, block, kc_s.at[1, p], kc_r.at[1, p], place.peer_c()))
 
         def kv_ready(p):
             for k, xx in ((0, x), (1, 1 - x)):
@@ -357,46 +406,19 @@
 
         def expand(m, t):
             left = v_n[m * runs // 2 : (m + 1) * runs // 2].reshape(half, width)
-            value = jnp.dot(left, weight(cuts[1][0] + t * tile), preferred_element_type=F32) + bias_of(3 + t)
-            v_exp[m * half : (m + 1) * half, t * tile : (t + 1) * tile] = value
-            active = 0.5 * value * (1.0 + lax.erf(value * math.sqrt(0.5)))
-            v_act[m * half : (m + 1) * half, t * tile : (t + 1) * tile] = active.astype(BF)
+            value = jnp.dot(left, weight(cuts[expand_at][0] + t * tile), preferred_element_type=F32) + bias_of(3 + t)
+            sigma = 0.5 * (1.0 + lax.erf(value * math.sqrt(0.5)))
+            slope = sigma + value * jnp.exp(-0.5 * value * value) * (1.0 / math.sqrt(2 * math.pi))
+            v_slope[m * half : (m + 1) * half, t * tile : (t + 1) * tile] = slope
+            first = HEAD_DIM + t * tile
+            v_left[m * half : (m + 1) * half, first : first + tile] = (value * sigma).astype(BF)
 
         def shrink_back(m, t):
             left = v_g[m * runs // 2 : (m + 1) * runs // 2].reshape(half, width)
-            value = jnp.dot(left, weight(cuts[3][0] + t * tile), preferred_element_type=F32)
-            slope = gelu_slope(v_exp[m * half : (m + 1) * half, t * tile : (t + 1) * tile])
-            v_dexp[m * half : (m + 1) * half, t * tile : (t + 1) * tile] = (value * slope).astype(BF)
-
-        for p in range(parts):
-            project(p)
-        g_far()
-        w_across(1)
-        for g in shrink:
-            w_first(g)
-        g_near()
-        for p in range(parts):
-            kv_beside(p)
-        g_last()
-        w_beside(1)
-        for p in range(parts):
-            kv_ready(p)
-        w_ready(1)
-        w_across(2)
-        for t in range(v_act.shape[1] // tile):
-            for m in range(2):
-                expand(m, t)
-            if t == 0:
-                w_beside(2)
-        save(v_act, at["act_out"])
-        mine[2].wait()
-        g_side()
-        save(v_g, g_out)
-        w_ready(2)
-        for m in range(2):
-            left = v_g[m * runs // 2 : (m + 1) * runs // 2].reshape(half, width)
-            value = jnp.dot(left, weight(cuts[2][0]), preferred_element_type=F32)
-            v_do[m * runs // 2 : (m + 1) * runs // 2] = value.astype(BF).reshape(runs // 2, per_run, HEAD_DIM)
+            value = jnp.dot(left, weight(cuts[shrink[0]][0] + t * tile), preferred_element_type=F32)
+            value = value * v_slope[m * half : (m + 1) * half, t * tile : (t + 1) * tile]
+            first = 3 * HEAD_DIM + t * tile
+            v_right[m * half : (m + 1) * half, first : first + tile] = value.astype(BF)
 
         row_tok, col_tok = at["row_tok"], at["col_tok"]
 
@@ -409,25 +431,123 @@
             rows, cols = row_tok[i], col_tok[k]
             return (segment(rows) == segment(cols)) & (cols <= rows)
 
+        def attended_back():
+            for m in range(2):
+                left = v_g[m * runs // 2 : (m + 1) * runs // 2].reshape(half, width)
+                value = jnp.dot(left, weight(cuts[dense_at][0]), preferred_element_type=F32)
+                v_do[m * runs // 2 : (m + 1) * runs // 2] = value.astype(BF).reshape(runs // 2, per_run, HEAD_DIM)
+
+        def key(k):
+            return v_kv[k, :, :, :HEAD_DIM].reshape(4 * per_run, HEAD_DIM)
+
+        def value_of(k):
+            return v_kv[k, :, :, HEAD_DIM:].reshape(4 * per_run, HEAD_DIM)
+
+        def attend(i):
+            here = slice(i * per_run, (i + 1) * per_run)
+            out, total = attention_forward(i, prompt_runs, mask, v_q, key, value_of, s_ref)
+            v_out[here], lse[here] = out, total
+            v_left[here, :HEAD_DIM] = out.astype(BF)
+
+        def attend_back(i):
+            here = slice(i * per_run, (i + 1) * per_run)
+            back = attention_backward(
+                i, prompt_runs, mask, v_q, v_do, key, value_of, v_out[here], lse[here], v_turn, sum_ref
+            )
+            v_right[here, :HEAD_DIM] = back.astype(BF)
+
+        def fold_first():
+            for copy in kv_sends:
+                copy.wait_send()
+            sends[:] = [one for one in sends if not any(one is other for other in kv_sends)]
+            v_kv[...] = sum_ref[...].astype(BF).reshape(v_kv.shape)
+            for k, xx in ((0, 1 - x), (1, x)):
+                state["fold", k] = send(
+                    v_kv.at[:, xx * 2 + 1 - c], kv_c.at[:, k], at["fc_s"].at[k], at["fc_r"].at[k], place.peer_c()
+                )
+
+        def fold_add(k, final):
+            state["fold", k].wait_recv()
+            mine_slot = (x if k else 1 - x) * 2 + c
+
+            @pl.loop(0, runs)
+            def _(run):
+                value = v_kv[run, mine_slot].astype(F32) + kv_c[run, k].astype(F32)
+                if final:
+                    value = value + kv_x[run].astype(F32)
+                    back = turn(value[:, :HEAD_DIM].astype(BF).astype(F32), [v_turn[t, run] for t in range(3)], -1.0)
+                    here = pl.ds(pl.multiple_of(run * per_run, per_run), per_run)
+                    v_right[here, HEAD_DIM : 2 * HEAD_DIM] = back.astype(BF)
+                    v_right[here, 2 * HEAD_DIM : 3 * HEAD_DIM] = value[:, HEAD_DIM:].astype(BF)
+                else:
+                    kv_c[run, k] = value.astype(BF)
+
+        def fold_cross():
+            fold_add(0, False)
+            state["fold_x"] = send(kv_c.at[:, 0], kv_x, at["fx_s"].at[0], at["fx_r"].at[0], place.peer_x())
+
+        def fold_close():
+            state["fold_x"].wait_recv()
+            fold_add(1, True)
+            save(v_right.at[:, pl.ds(0, 3 * HEAD_DIM)], at["right_out"].at[:, pl.ds(0, 3 * HEAD_DIM)])
+
+        chunks, early, wide = o_p.shape[0], o_y.shape[0], o_p.shape[-1]
+
+        def out_part(q):
+            for k in range(wide // tile):
+                n = q * (wide // tile) + k
+                per_x = width // 2 // tile
+                low = n % per_x * HEADS // per_x
+                some = v_w[n // per_x, 0, low : low + HEADS // per_x, :, :, cuts[dense_at][0] :]
+                value = lax.dot_general(
+                    v_left[...], some.reshape(tile, v_left.shape[1]), (((1,), (1,)), ((), ())), preferred_element_type=F32
+                )
+                o_p[q, :, :, :, :, :, k * tile : (k + 1) * tile] = value.astype(BF).reshape(runs, 2, 2, 2, STRIPE, tile)
+            if q < early:
+                state["out", q] = send(
+                    o_p.at[q, :, :, :, 1 - place.hy], o_y.at[q], at["oy_s"].at[q], at["oy_r"].at[q], place.peer_y()
+                )
+            else:
+                save(o_p.at[q], at["part_out"].at[q - early])
+
+        def out_side(q):
+            state["out", q].wait_recv()
+
+            @pl.loop(0, runs)
+            def _(run):
+                for t in range(LINE):
+                    value = o_y[q, run, t // 2, t % 2].astype(F32) + o_p[q, run, t // 2, t % 2, place.hy].astype(F32)
+                    o_y[q, run, t // 2, t % 2] = value.astype(BF)
+
+            save(o_y.at[q], at["half_out"].at[q])
+
+        for p in range(parts):
+            step(67 + 2 * p, project, p)
+            step(80.5 + 6 * p, kv_beside, p)
+            step(101, kv_ready, p)
         for i in range(runs):
-            attention_step(
-                i, prompt_runs, mask, v_q, v_do, lambda k: v_kv[k, :, :, :HEAD_DIM].reshape(4 * per_run, HEAD_DIM),
-                lambda k: v_kv[k, :, :, HEAD_DIM:].reshape(4 * per_run, HEAD_DIM), v_turn, v_att, v_dq, s_ref, sum_ref,
-            )
-            if i < len(shrink):
-                w_across(shrink[i])
-            elif i < 2 * len(shrink):
-                w_beside(shrink[i - len(shrink)])
-        v_dkv[...] = sum_ref[...].astype(BF).reshape(v_dkv.shape)
-        save(v_att, at["att_out"])
-        save(v_dq, at["dq_out"])
-        save(v_dkv, at["dkv_out"])
-        for t, g in enumerate(shrink):
-            w_ready(g)
+            step(105.5 + 1.2 * i, attend, i)
+            step(135 + 2 * i, attend_back, i)
+            step(75, flip, v_n, n_out, i)
+            step(163, flip, v_g, g_out, i)
+        count = v_slope.shape[1] // tile
+        for t in range(count):
             for m in range(2):
-                shrink_back(m, t)
-        save(v_dexp, at["dexp_out"])
-    for copy in puts:
+                step(117.5 + 0.1 * t + 0.05 * m, expand, m, t)
+                step(161 + 0.1 * t, shrink_back, m, t)
+        step(134.5, attended_back)
+        step(151.5, fold_first)
+        step(155, fold_cross)
+        for q in range(chunks):
+            step(156.5 + 0.1 * q if q < early else 162, out_part, q)
+        for q in range(early):
+            step(172 + 12 * q, out_side, q)
+        step(157, save, v_left, at["left_out"])
+        step(161.9, save, v_right.at[:, pl.ds(3 * HEAD_DIM, v_slope.shape[1])], at["right_out"].at[:, pl.ds(3 * HEAD_DIM, v_slope.shape[1])])
+        step(183, fold_close)
+    for _, _, body, given in sorted(plan, key=lambda one: one[:2]):
+        body(*given)
+    for copy in puts + flipped[-2:]:
         copy.wait()
     for copy in sends:
         copy.wait_send()
@@ -440,7 +560,7 @@
     columns = weights.shape[2]
     fuse = ways == 1 and prompt_total == PROMPT
     head3 = 3 * HEAD_DIM
-    cuts = [(0, head3), (head3, hidden), (head3 + hidden, HEAD_DIM)]
+    cuts = [(k * HEAD_DIM, HEAD_DIM) for k in range(3)] + [(head3, hidden), (head3 + hidden, HEAD_DIM)]
     cuts += [(head3 + hidden + HEAD_DIM + k * 256, 256) for k in range(hidden // 256)]
     blocks = (2, ways, HEADS, 2, rows, columns)
     group = runs * HEADS * STRIPE
@@ -451,11 +571,16 @@
 
     gathered = (runs, HEADS, STRIPE, width)
     tables = (3, runs, per_run, 128)
-    outs = [shape(gathered), shape(gathered), shape(blocks), shape(notes.shape[1:], F32), shape(tables, F32)]
+    chunks, wide = 4, width // 4
+    kept = head3 + hidden if fuse else columns
+    outs = [
+        shape((width, group) if fuse else gathered), shape((width, group) if fuse else gathered), shape(blocks[:-1] + (kept,)), shape(notes.shape[1:], F32),
+        shape((1, 1, 8, 128) if fuse else tables, F32),
+    ]
     if fuse:
         outs += [
-            shape((runs, per_run, HEAD_DIM)), shape((group, hidden)), shape((group, hidden)),
-            shape((runs, per_run, HEAD_DIM)), shape((runs, 4, per_run, 2 * HEAD_DIM)),
+            shape((group, HEAD_DIM + hidden)), shape((group, head3 + hidden)),
+            shape((EARLY, runs, 2, 2, STRIPE, wide)), shape((chunks - EARLY, runs, 2, 2, 2, STRIPE, wide)),
         ]
     extra = max(ways - 1, 1)
     count = len(cuts)
@@ -464,7 +589,7 @@
         pltpu.VMEM((HEADS,) + trig.shape, F32),
         pltpu.VMEM(notes.shape, F32), pltpu.VMEM(notes.shape, F32), pltpu.VMEM(notes.shape, F32),
         pltpu.VMEM((extra,) + notes.shape, F32), pltpu.VMEM(notes.shape, F32),
-        DMA((5,)), DMA((count + 10,)),
+        DMA((5,)), DMA((count + 14,)),
         DMA((7,)), DMA((HEADS,)), DMA((7,)), DMA((HEADS,)),
         DMA((count, ways * HEADS)), DMA((count, ways, HEADS)), DMA((count,)), DMA((count,)), DMA((count, 2)), DMA((count, 2)),
         DMA((HEADS,)), DMA((HEADS,)), DMA((1,)), DMA((1,)), DMA((1,)), DMA((1,)), DMA((extra,)), DMA((extra,)),
@@ -474,12 +599,15 @@
         scratch += [
             pltpu.VMEM((runs, per_run, HEAD_DIM), BF), pltpu.VMEM((runs, per_run, HEAD_DIM), BF),
             pltpu.VMEM((runs, 4, per_run, 2 * HEAD_DIM), BF), pltpu.VMEM((group, hidden), F32),
-            pltpu.VMEM((group, hidden), BF), pltpu.VMEM((group, hidden), BF),
-            pltpu.VMEM((runs, per_run, HEAD_DIM), BF), pltpu.VMEM((runs, per_run, HEAD_DIM), BF),
-            pltpu.VMEM((runs, 4, per_run, 2 * HEAD_DIM), BF),
+            pltpu.VMEM((group, HEAD_DIM + hidden), BF), pltpu.VMEM((group, head3 + hidden), BF),
+            pltpu.VMEM((group, HEAD_DIM), F32), pltpu.VMEM((group, 1), F32),
             pltpu.VMEM((per_run, (prompt_runs + 1) * 4 * per_run), F32),
             pltpu.VMEM((runs, 4 * per_run, 2 * HEAD_DIM), F32),
+            pltpu.VMEM((runs, 2, per_run, 2 * HEAD_DIM), BF), pltpu.VMEM((runs, per_run, 2 * HEAD_DIM), BF),
+            pltpu.VMEM((chunks, runs, 2, 2, 2, STRIPE, wide), BF), pltpu.VMEM((EARLY, runs, 2, 2, STRIPE, wide), BF),
+            pltpu.VMEM((2, 256, group), BF), DMA((2,)),
             DMA((4,)), DMA((4,)), DMA((2, 4)), DMA((2, 4)),
+            DMA((2,)), DMA((2,)), DMA((1,)), DMA((1,)), DMA((EARLY,)), DMA((EARLY,)),
         ]
     return fuse, pl.pallas_call(
         functools.partial(open_kernel, ways, tuple(cuts), fuse, prompt_runs, prompt_total),
@@ -560,12 +688,11 @@
     return jnp.concatenate([front * cosine + moved * sign, u[:, 128:]], 1)
 
 
-def finish_kernel(ways, att, act, dexp, dq, dkv, tables, w_all, n_all, g_all, note,
+def finish_kernel(ways, early, left, right, w_all, n_all, g_all, note, half_in, part_in,
                   out_sum, e_sum, own_a, own_b, note_all,
-                  v_left, v_right, v_w, v_turn, kv_own, kv_c, kv_x,
-                  o_p, o_y, o_1, o_2, e_p, e_y, e_1, e_2,
-                  raw, flat, ring, a_c, a_x, a_w, b_c, b_x, b_w, n_mine, n_c, n_x, n_w,
-                  load, load_raw, kv_load, kv_s, kv_r, kvx_s, kvx_r,
+                  v_left, v_right, v_w, o_own, o_y, o_1, o_2, e_p, e_y, e_1, e_2,
+                  raw, ring, a_c, a_x, a_w, b_c, b_x, b_w, n_mine, n_c, n_x, n_w,
+                  load, load_raw, load_o,
                   oy_s, oy_r, o1_s, o1_r, o2_s, o2_r, ey_s, ey_r, e1_s, e1_r, e2_s, e2_r,
                   ac_s, ac_r, ax_s, ax_r, aw_s, aw_r, ah_s, ah_r,
                   bc_s, bc_r, bx_s, bx_r, bw_s, bw_r, bh_s, bh_r, keep, n_s, n_r):
@@ -573,8 +700,8 @@
     x, w, h, c, hy, hz = place.x, place.w, place.h, place.c, place.hy, place.hz
     d0, d1 = hz % 2, hz // 2
     runs = v_left.shape[0]
-    chunks = o_p.shape[0]
-    wide = o_p.shape[-1]
+    chunks = e_p.shape[0]
+    wide = e_p.shape[-1]
     rows = own_a.shape[1]
     hp = 256 // (2 * rows)
     tiles = HEADS // hp
@@ -592,27 +719,11 @@
 
     greet(place.peers_h() + place.peers_w() + [place.peer_x(), place.peer_c()])
 
-    def fetch(src, dst, k):
-        copy = pltpu.make_async_copy(src, dst, load.at[k])
+    def fetch(src, dst, sem):
+        copy = pltpu.make_async_copy(src, dst, sem)
         copy.start()
         return copy
 
-    early = [
-        fetch(att, v_left.at[..., :HEAD_DIM], 0),
-        fetch(act, v_left.at[..., HEAD_DIM:], 1),
-        fetch(w_all.at[:, pl.ds(v_right.shape[-1], inner)], v_w.at[:, :inner], 2),
-    ]
-
-    kv_first, kv_mine = [], []
-    for k, xs in ((0, 1 - x), (1, x)):
-        kv_first.append(send(dkv.at[:, xs * 2 + 1 - c], kv_c.at[:, k], kv_s.at[k], kv_r.at[k], place.peer_c()))
-        kv_mine.append(pltpu.make_async_copy(dkv.at[:, xs * 2 + c], kv_own.at[:, k], kv_load.at[k]))
-        kv_mine[k].start()
-    late = [
-        fetch(dexp, v_right.at[..., head3:], 3),
-        fetch(dq, v_right.at[..., :HEAD_DIM], 4),
-        fetch(tables, v_turn, 5),
-    ]
 
     def partial(src, q, buf, depth):
         @pl.loop(0, wide // 256)
@@ -626,9 +737,10 @@
             )
             buf[q, :, :, :, :, :, pl.ds(at, 256)] = value.astype(BF).reshape(runs, 2, 2, 2, STRIPE, 256)
 
-    def sums(buf, y, one, two, s_y, r_y, s_1, r_1, s_2, r_2, total):
-        def start(q):
-            return send(buf.at[q, :, :, :, 1 - hy], y.at[q], s_y.at[q], r_y.at[q], place.peer_y())
+    def sums(mine, y, one, two, s_1, r_1, s_2, r_2, total):
+        def near(q):
+            target = place.device(h=(hz + 1 - 2 * d0) * 2 + hy)
+            return send(y.at[q, :, :, 1 - d0], one.at[q], s_1.at[q], r_1.at[q], target)
 
         def after_y(q, copy):
             copy.wait_recv()
@@ -636,11 +748,10 @@
             @pl.loop(0, runs)
             def _(run):
                 for t in range(LINE):
-                    value = y[q, run, t // 2, t % 2].astype(F32) + buf[q, run, t // 2, t % 2, hy].astype(F32)
+                    value = y[q, run, t // 2, t % 2].astype(F32) + mine(q, run, t).astype(F32)
                     y[q, run, t // 2, t % 2] = value.astype(BF)
 
-            target = place.device(h=(hz + 1 - 2 * d0) * 2 + hy)
-            return send(y.at[q, :, :, 1 - d0], one.at[q], s_1.at[q], r_1.at[q], target)
+            return near(q)
 
         def after_1(q, copy):
             copy.wait_recv()
@@ -661,40 +772,14 @@
             def _(run):
                 total[run, :, q * wide : (q + 1) * wide] = two[q, run].astype(F32) + one[q, run, d1].astype(F32)
 
-        return start, after_y, after_1, after_2
-
-    o_start, o_after_y, o_after_1, o_after_2 = sums(o_p, o_y, o_1, o_2, oy_s, oy_r, o1_s, o1_r, o2_s, o2_r, out_sum)
-    e_start, e_after_y, e_after_1, e_after_2 = sums(e_p, e_y, e_1, e_2, ey_s, ey_r, e1_s, e1_r, e2_s, e2_r, e_sum)
-
-    for copy in early:
-        copy.wait()
-    o_step = {}
-    for q in range(chunks):
-        partial(v_left, q, o_p, inner)
-        o_step[q] = o_start(q)
-    w_load = fetch(w_all.at[:, pl.ds(0, v_right.shape[-1])], v_w, 6)
-
-    def kv_add(k, final):
-        kv_mine[k].wait()
-        kv_first[k].wait_recv()
-
-        @pl.loop(0, runs)
-        def _(run):
-            value = kv_own[run, k].astype(F32) + kv_c[run, k].astype(F32)
-            if final:
-                value = value + kv_x[run].astype(F32)
-                back = turn(value[:, :HEAD_DIM].astype(BF).astype(F32), [v_turn[t, run] for t in range(3)], -1.0)
-                shape = (LINE, 2, STRIPE, HEAD_DIM)
-                v_right[run, :, :, :, HEAD_DIM : 2 * HEAD_DIM] = back.astype(BF).reshape(shape)
-                v_right[run, :, :, :, 2 * HEAD_DIM : head3] = value[:, HEAD_DIM:].astype(BF).reshape(shape)
-            else:
-                kv_c[run, k] = value.astype(BF)
-
-    kv_add(0, False)
-    kv_second = remote(kv_c.at[:, 0], kv_x, kvx_s.at[0], kvx_r.at[0], place.peer_x())
-    kv_second.start()
-    for copy in late:
-        copy.wait()
+        return near, after_y, after_1, after_2
+
+    o_near, o_after_y, o_after_1, o_after_2 = sums(
+        lambda q, run, t: o_own[q - (early or 0), run, t // 2, t % 2], o_y, o_1, o_2, o1_s, o1_r, o2_s, o2_r, out_sum
+    )
+    _, e_after_y, e_after_1, e_after_2 = sums(
+        lambda q, run, t: e_p[q, run, t // 2, t % 2, hy], e_y, e_1, e_2, e1_s, e1_r, e2_s, e2_r, e_sum
+    )
 
     order_t = [(k, dw, dt) for k in range(2) for dw in list(range(1, ways)) + [0] for dt in list(range(1, tiles)) + [0]]
     own_t = h // hp
@@ -702,42 +787,49 @@
     def where(k, dw, dt):
         return (1 - x if k == 0 else x), (w + dw) % ways, (own_t + dt) % tiles
 
-    def raw_copy(n, src, buf):
-        xs, ws, t = where(*order_t[n])
-        at = pl.multiple_of(((xs * ways + ws) * tiles + t) * 256, 256)
-        return pltpu.make_async_copy(src.at[:, pl.ds(at, 256)], raw.at[n % 2, buf], load_raw.at[n % 2, buf])
-
-    def product(n, buf, src, first, count, at):
-        flat[...] = raw[n % 2, buf].T
-
+    def product(m, buf, src, first, count, at):
         @pl.loop(0, count // 256)
         def _(k):
             col = pl.multiple_of(k * 256, 256)
             value = jnp.dot(
-                flat[...], src[..., pl.ds(first + col, 256)].reshape(group, 256), preferred_element_type=F32
+                raw[m % 2, buf], src[..., pl.ds(first + col, 256)].reshape(group, 256), preferred_element_type=F32
             )
-            ring[n % 3, :, :, :, pl.ds(at + col, 256)] = value.astype(BF).reshape(hp, 2, rows, 256)
-
-    def grads(cols, from_c, from_x, from_w, c_s, c_r, x_s, x_r, w_s, w_r, h_s, h_r, out, fill, need, flag):
-        first, second, third, last = {}, {}, {}, []
-
-        def begin(n):
-            for buf, src in need:
-                raw_copy(n, src, buf).start()
+            ring[m % 3, :, :, :, pl.ds(at + col, 256)] = value.astype(BF).reshape(hp, 2, rows, 256)
+
+    made, order_m = [], []
+
+    def raw_copies(m):
+        n, need = order_m[m]
+        xs, ws, t = where(*order_t[n])
+        at = pl.multiple_of(((xs * ways + ws) * tiles + t) * 256, 256)
+        return [
+            pltpu.make_async_copy(src.at[pl.ds(at, 256)], raw.at[m % 2, buf], load_raw.at[m % 2, buf])
+            for buf, src in need
+        ]
+
+    def begin(m):
+        if m < len(order_m):
+            for copy in raw_copies(m):
+                copy.start()
+
+    def grads(cols, from_c, from_x, from_w, c_s, c_r, x_s, x_r, w_s, w_r, h_s, h_r, out, fill, flag):
+        first, second, third, spot = {}, {}, {}, {}
 
         def make(n):
-            if n >= 3:
-                first[n - 3].wait_send()
-            for buf, src in need:
-                raw_copy(n, src, buf).wait()
-            fill(n)
-            if n + 1 < len(order_t):
-                begin(n + 1)
+            m = len(made)
+            if m >= 3:
+                made[m - 3].wait_send()
+            for copy in raw_copies(m):
+                copy.wait()
+            fill(m)
+            begin(m + 1)
             k, dw, dt = order_t[n]
             first[n] = remote(
-                ring.at[n % 3, :, 1 - c, :, pl.ds(0, cols)], from_c.at[k, dw, dt], c_s.at[n], c_r.at[n], place.peer_c()
+                ring.at[m % 3, :, 1 - c, :, pl.ds(0, cols)], from_c.at[k, dw, dt], c_s.at[n], c_r.at[n], place.peer_c()
             )
             first[n].start()
+            spot[n] = m % 3
+            made.append(first[n])
 
         def mine(n):
             k, dw, dt = order_t[n]
@@ -745,7 +837,7 @@
 
             @pl.loop(0, hp)
             def _(q):
-                value = from_c[k, dw, dt, q].astype(F32) + ring[n % 3, q, c, :, :cols].astype(F32)
+                value = from_c[k, dw, dt, q].astype(F32) + ring[spot[n], q, c, :, :cols].astype(F32)
                 from_c[k, dw, dt, q] = value.astype(BF)
 
         def cross(n):
@@ -784,10 +876,6 @@
                 def _():
                     pltpu.make_async_copy(from_c.at[1, 0, dt, q], out.at[h], keep.at[flag]).start()
 
-        def drain():
-            for n in range(max(len(order_t) - 3, 0), len(order_t)):
-                first[n].wait_send()
-
         def end():
             for n in range(len(order_t)):
                 k, dw, dt = order_t[n]
@@ -804,121 +892,143 @@
                 remote(out.at[hs], out.at[hs], h_s.at[0], h_r.at[hs], place.peer_x()).wait_recv()
             pltpu.make_async_copy(from_c.at[1, 0, 0, 0], out.at[h], keep.at[flag]).wait()
 
-        return begin, make, mine, cross, close, drain, end
-
-    def fill_a(n):
-        product(n, 1, v_left, 0, inner, 0)
-        product(n, 0, v_right, head3, a_cols - inner, inner)
-
-    def fill_b(n):
-        product(n, 0, v_right, 0, head3, 0)
-
-    a_begin, a_make, a_mine, a_cross, a_close, a_drain, a_end = grads(
-        a_cols, a_c, a_x, a_w, ac_s, ac_r, ax_s, ax_r, aw_s, aw_r, ah_s, ah_r, own_a, fill_a, ((0, n_all), (1, g_all)), 0
-    )
-    b_begin, b_make, b_mine, b_cross, b_close, b_drain, b_end = grads(
-        b_cols, b_c, b_x, b_w, bc_s, bc_r, bx_s, bx_r, bw_s, bw_r, bh_s, bh_r, own_b, fill_b, ((0, n_all),), 1
+        return make, mine, cross, close, end
+
+    def fill_a(m):
+        product(m, 1, v_left, 0, inner, 0)
+        product(m, 0, v_right, head3, a_cols - inner, inner)
+
+    def fill_b(m):
+        product(m, 0, v_right, 0, head3, 0)
+
+    a_make, a_mine, a_cross, a_close, a_end = grads(
+        a_cols, a_c, a_x, a_w, ac_s, ac_r, ax_s, ax_r, aw_s, aw_r, ah_s, ah_r, own_a, fill_a, 0
+    )
+    b_make, b_mine, b_cross, b_close, b_end = grads(
+        b_cols, b_c, b_x, b_w, bc_s, bc_r, bx_s, bx_r, bw_s, bw_r, bh_s, bh_r, own_b, fill_b, 1
     )
     count = len(order_t)
     half = count // 2
-    a_begin(0)
-    for n in range(half):
-        a_make(n)
-        a_mine(n)
-        if n == 0:
-            kv_second.wait_send()
-        a_cross(n)
-        if n == 1:
-            o_step[0] = o_after_y(0, o_step[0])
-    o_step[1] = o_after_y(1, o_step[1])
-    o_step[0] = o_after_1(0, o_step[0])
-
-    kv_second.wait_recv()
-    kv_add(1, True)
-    w_load.wait()
-    e_step = {}
-    for q in range(chunks):
+    order_m += [(n, ((0, n_all), (1, g_all))) for n in A_ORDER] + [(n, ((0, n_all),)) for n in A_ORDER]
+
+    plan = []
+
+    def step(time, body, *given):
+        plan.append((time, len(plan), body, given))
+
+    state = {}
+
+    def wait_all(copies):
+        for copy in copies:
+            copy.wait()
+
+    def e_part(q):
         partial(v_right, q, e_p, v_right.shape[-1])
-        e_step[q] = e_start(q)
-        if q == 1:
-            o_step[2] = o_after_y(2, o_step[2])
-            o_step[1] = o_after_1(1, o_step[1])
-    o_after_2(0, o_step[0])
-
-    def fold_columns(first, cols, row):
-        @pl.loop(0, cols // 128)
+        state["e", q] = send(e_p.at[q, :, :, :, 1 - hy], e_y.at[q], ey_s.at[q], ey_r.at[q], place.peer_y())
+
+    def o_start():
+        for q in range(early, chunks):
+            state["o", q] = send(part_in.at[q - early, :, :, :, 1 - hy], o_y.at[q], oy_s.at[q], oy_r.at[q], place.peer_y())
+        for q in range(chunks):
+            if q < early:
+                state["o_load", q] = fetch(half_in.at[q], o_y.at[q], load_o.at[q])
+            else:
+                state["o_load", q] = fetch(part_in.at[q - early, :, :, :, hy], o_own.at[q - early], load_o.at[q])
+
+    def o_first(q):
+        state["o_load", q].wait()
+        if q < early:
+            state["o", q] = o_near(q)
+        else:
+            state["o", q] = o_after_y(q, state["o", q])
+
+    def advance(key, body, q):
+        state[key, q] = body(q, state[key, q])
+
+    note_w = []
+    base = 1 + ways
+
+    def note_sums():
+        state["note_load"].wait()
+
+        @pl.loop(0, v_right.shape[-1] // 128)
         def _(k):
             at = pl.multiple_of(k * 128, 128)
-            value = v_right[..., pl.ds(first + at, 128)].reshape(group, 128).astype(F32)
-            n_mine[pl.ds(row + k, 1), :] = jnp.sum(value, 0, keepdims=True)
-
-    n_load = pltpu.make_async_copy(note, n_mine, keep.at[2])
-    n_load.start()
-    n_load.wait()
-    fold_columns(0, v_right.shape[-1], 0)
-    note_copy = send(n_mine, n_c, n_s.at[0], n_r.at[0], place.peer_c())
-
-    note_w = []
-    for n in range(half, count):
-        a_make(n)
-        a_mine(n)
-        if n == half:
-            note_copy.wait_recv()
-            n_c[...] = n_c[...] + n_mine[...]
-            note_copy = send(n_c, n_x, n_s.at[1], n_r.at[1], place.peer_x())
-        a_close(n)
-        if n == half + 1:
-            note_copy.wait_recv()
-            n_x[...] = n_x[...] + n_c[...]
-            for k, device in enumerate(place.peers_w()):
-                note_w.append(send(n_x, n_w.at[k], n_s.at[2 + k], n_r.at[2 + k], device))
-            o_step[3] = o_after_y(3, o_step[3])
-            o_step[2] = o_after_1(2, o_step[2])
-    o_after_2(1, o_step[1])
-    o_step[3] = o_after_1(3, o_step[3])
-    for k, copy in enumerate(note_w):
-        copy.wait()
-    total = n_x[...]
-    for k in range(ways - 1):
-        total = total + n_w[k]
-    n_x[...] = total
-    base = 1 + ways
-    for dh in range(1, HEADS):
-        send(n_x, note_all.at[h], n_s.at[base + dh], n_r.at[base + h], place.device(h=(h + dh) % HEADS))
-    n_keep = pltpu.make_async_copy(n_x, note_all.at[h], keep.at[3])
-    n_keep.start()
-
-    a_drain()
-    b_begin(0)
-    for n in range(half):
-        b_make(n)
-        b_mine(n)
-        b_cross(n)
-        if n == 0:
-            e_step[0] = e_after_y(0, e_step[0])
-        if n == 1:
-            o_after_2(2, o_step[2])
-    e_step[1] = e_after_y(1, e_step[1])
-    e_step[0] = e_after_1(0, e_step[0])
-    o_after_2(3, o_step[3])
-    for n in range(half, count):
-        b_make(n)
-        b_mine(n)
-    e_step[2] = e_after_y(2, e_step[2])
-    e_step[1] = e_after_1(1, e_step[1])
-    e_after_2(0, e_step[0])
-    for n in range(half, count):
-        b_close(n)
-    e_step[3] = e_after_y(3, e_step[3])
-    e_step[2] = e_after_1(2, e_step[2])
-    e_after_2(1, e_step[1])
-    e_step[3] = e_after_1(3, e_step[3])
-    e_after_2(2, e_step[2])
-    e_after_2(3, e_step[3])
+            value = v_right[..., pl.ds(at, 128)].reshape(group, 128).astype(F32)
+            n_mine[pl.ds(k, 1), :] = jnp.sum(value, 0, keepdims=True)
+
+        state["note"] = send(n_mine, n_c, n_s.at[0], n_r.at[0], place.peer_c())
+
+    def note_cross():
+        state["note"].wait_recv()
+        n_c[...] = n_c[...] + n_mine[...]
+        state["note"] = send(n_c, n_x, n_s.at[1], n_r.at[1], place.peer_x())
+
+    def note_ways():
+        state["note"].wait_recv()
+        n_x[...] = n_x[...] + n_c[...]
+        for k, device in enumerate(place.peers_w()):
+            note_w.append(send(n_x, n_w.at[k], n_s.at[2 + k], n_r.at[2 + k], device))
+
+    def note_out():
+        if ways > 1:
+            wait_all(note_w)
+            total = n_x[...]
+            for k in range(ways - 1):
+                total = total + n_w[k]
+            n_x[...] = total
+        for dh in range(1, HEADS):
+            send(n_x, note_all.at[h], n_s.at[base + dh], n_r.at[base + h], place.device(h=(h + dh) % HEADS))
+        state["note_keep"] = pltpu.make_async_copy(n_x, note_all.at[h], keep.at[3])
+        state["note_keep"].start()
+
+    if early is not None:
+        o_start()
+    state["note_load"] = fetch(note, n_mine, keep.at[2])
+    loads = [fetch(right, v_right, load.at[0]), fetch(left, v_left, load.at[1])]
+    begin(0)
+    w_load = fetch(w_all.at[:, pl.ds(0, v_right.shape[-1])], v_w, load.at[2])
+    if early is not None:
+        for q, times in enumerate(((0.5, 9, 19.5), (0.6, 14.5, 25), (14.2, 37, 49), (26, 48.2, 62))):
+            step(times[0], o_first, q)
+            step(times[1], advance, "o", o_after_1, q)
+            step(times[2], advance, "o", o_after_2, q)
+    step(1, wait_all, loads)
+    for i, (n, time) in enumerate(zip(A_ORDER, (2, 4.5, 10, 15, 19.6, 26.2, 31, 36), strict=True)):
+        step(time, a_make, n)
+        if i > 0:
+            step(time, a_mine, A_ORDER[i - 1])
+            if A_ORDER[i - 1] < half:
+                step(time, a_cross, A_ORDER[i - 1])
+    step(38, a_mine, A_ORDER[-1])
+    step(7.2, w_load.wait)
+    for q in range(chunks):
+        step((7.3, 13, 17.5, 22.5)[q], e_part, q)
+    step(25.5, note_sums)
+    step(36.5, note_cross)
+    step(60, note_ways)
+    step(60, note_out)
+    for i, (n, time) in enumerate(zip(A_ORDER, (39, 40, 41, 42, 44, 45, 46, 47), strict=True)):
+        step(time, b_make, n)
+        if i > 0:
+            step(time, b_mine, A_ORDER[i - 1])
+            if A_ORDER[i - 1] < half:
+                step(time, b_cross, A_ORDER[i - 1])
+    step(47.5, b_mine, A_ORDER[-1])
+    for n, times in zip(range(half, count), ((22, 74), (35.5, 79), (49.5, 84), (63, 88)), strict=True):
+        step(times[0], a_close, n)
+        step(times[1], b_close, n)
+    for q, times in enumerate(((48, 66, 80), (59, 77, 92), (71, 89, 104), (83, 101, 114))):
+        step(times[0], advance, "e", e_after_y, q)
+        step(times[1], advance, "e", e_after_1, q)
+        step(times[2], advance, "e", e_after_2, q)
+    for _, _, body, given in sorted(plan, key=lambda one: one[:2]):
+        body(*given)
+    for copy in made[-3:]:
+        copy.wait_send()
     a_end()
-    b_drain()
     b_end()
-    n_keep.wait()
+    state["note_keep"].wait()
     for dh in range(1, HEADS):
         hs = (h + dh) % HEADS
         remote(note_all.at[hs], note_all.at[hs], n_s.at[0], n_r.at[base + hs], place.peer_x()).wait_recv()
@@ -927,30 +1037,31 @@
             copy.wait_send()
 
 
-def finish(ways, rows, att, act, dexp, dq, dkv, tables, w_all, n_all, g_all, note):
+def finish(ways, rows, left, right, w_all, n_all, g_all, note, half, part):
     width = w_all.shape[0]
-    inner = att.shape[-1] + act.shape[-1]
-    right = w_all.shape[1] - inner
+    inner, right_cols = left.shape[1], right.shape[1]
     head3 = 3 * HEAD_DIM
-    a_cols, b_cols = inner + right - head3, head3
-    group = n_all.shape[0]
-    runs, _, per_run, pair = dkv.shape
+    a_cols, b_cols = inner + right_cols - head3, head3
+    group = n_all.shape[1]
+    runs = group // (HEADS * STRIPE)
     lines = (runs, LINE, 2, STRIPE)
     hp = 256 // (2 * rows)
     tiles = HEADS // hp
     chunks, wide = 4, width // 4
     extra = max(ways - 1, 1)
     count = 2 * ways * tiles
+    assert count == len(A_ORDER)
+    early = None if half is None else half.shape[0]
 
     def vm(shape, kind=BF):
         return pltpu.VMEM(shape, kind)
 
-    def row_buffers():
+    def row_buffers(first, used):
         return [
-            vm((chunks, runs, 2, 2, 2, STRIPE, wide)),
-            vm((chunks, runs, 2, 2, STRIPE, wide)),
-            vm((chunks, runs, 2, STRIPE, wide)),
-            vm((chunks, runs, STRIPE, wide)),
+            vm(first),
+            vm((chunks, runs, 2, 2, STRIPE, wide) if used else (1, 1, 1, 1, 16, 128)),
+            vm((chunks, runs, 2, STRIPE, wide) if used else (1, 1, 1, 16, 128)),
+            vm((chunks, runs, STRIPE, wide) if used else (1, 1, 16, 128)),
         ]
 
     def spare(shape):
@@ -971,14 +1082,14 @@
 
     scratch = (
         [
-            vm(lines + (inner,)), vm(lines + (right,)), vm((width, right)), vm(tables.shape, F32),
-            vm((runs, 2, per_run, pair)), vm((runs, 2, per_run, pair)), vm((runs, per_run, pair)),
+            vm(lines + (inner,)), vm(lines + (right_cols,)), vm((width, right_cols)),
         ]
-        + row_buffers() + row_buffers()
-        + [vm((2, 2, group, 256)), vm((256, group)), vm((3, hp, 2, rows, a_cols))]
+        + row_buffers((max(chunks - (early or 0), 1), runs, 2, 2, STRIPE, wide) if early is not None else (1, 1, 1, 1, 16, 128), early is not None)
+        + row_buffers((chunks, runs, 2, 2, 2, STRIPE, wide), True)
+        + [vm((2, 2, 256, group)), vm((3, hp, 2, rows, a_cols))]
         + gradient_buffers(a_cols) + gradient_buffers(b_cols)
         + [vm(note.shape, F32)] * 3 + [vm((extra,) + note.shape, F32)]
-        + [DMA((7,)), DMA((2, 2)), DMA((2,)), DMA((2,)), DMA((2,)), DMA((1,)), DMA((1,))]
+        + [DMA((3,)), DMA((2, 2)), DMA((chunks,))]
         + [DMA((chunks,))] * 12
         + gradient_sems() + gradient_sems()
         + [DMA((4,)), DMA((1 + ways + HEADS,)), DMA((1 + ways + HEADS,))]
@@ -990,12 +1101,13 @@
         jax.ShapeDtypeStruct((HEADS, rows, b_cols), BF),
         jax.ShapeDtypeStruct((HEADS,) + note.shape, F32),
     )
+    empty = jnp.zeros((1, 1, 1, 1, 16, 128), BF)
     ins = (
-        att.reshape(lines + (HEAD_DIM,)), act.reshape(lines + (inner - HEAD_DIM,)), dexp.reshape(lines + (right - head3,)),
-        dq.reshape(lines + (HEAD_DIM,)), dkv, tables, w_all, n_all, g_all, note,
+        left.reshape(lines + (inner,)), right.reshape(lines + (right_cols,)), w_all, n_all, g_all, note,
+        empty if half is None else half, empty if part is None else part,
     )
     return pl.pallas_call(
-        functools.partial(finish_kernel, ways),
+        functools.partial(finish_kernel, ways, early),
         out_shape=shapes,
         in_specs=[ANY] * len(ins),
         out_specs=(VMEM, VMEM, ANY, ANY, ANY),
@@ -1004,47 +1116,53 @@
     )(*ins)
 
 
-def attention_step(i, prompt_runs, mask, q_ref, do_ref, key, value_of, turn_ref, o_ref, dq_ref, s_ref, sum_ref):
-    m = q_ref.shape[1]
-    keys = sum_ref.shape[1]
-    by_rows = (((1,), (1,)), ((), ()))
-    by_tokens = (((0,), (0,)), ((), ()))
-
-    def dot(a, b, dims=(((1,), (0,)), ((), ()))):
-        return lax.dot_general(a, b, dims, preferred_element_type=F32)
-
-    pieces = list(range(min(i + 1, prompt_runs))) + ([i] if i >= prompt_runs else [])
+def pieces_of(i, prompt_runs):
+    return list(range(min(i + 1, prompt_runs))) + ([i] if i >= prompt_runs else [])
+
+
+def attention_forward(i, prompt_runs, mask, q_ref, key, value_of, s_ref):
     q = q_ref[i]
-    peak = None
-    for at, k in enumerate(pieces):
-        s = dot(q, key(k), by_rows)
+    peak, scores = None, []
+    for at, k in enumerate(pieces_of(i, prompt_runs)):
+        keys = key(k)
+        s = lax.dot_general(q, keys, (((1,), (1,)), ((), ())), preferred_element_type=F32)
         keep = mask(i, k)
         if keep is not None:
             s = jnp.where(keep, s, -1e30)
-        s_ref[:, at * keys : (at + 1) * keys] = s
+        here = slice(at * keys.shape[0], (at + 1) * keys.shape[0])
+        s_ref[:, here] = s
         top = jnp.max(s, -1, keepdims=True)
         peak = top if peak is None else jnp.maximum(peak, top)
-    total = jnp.zeros((m, 1), F32)
-    out = jnp.zeros((m, HEAD_DIM), F32)
-    for at, k in enumerate(pieces):
-        p = jnp.exp(s_ref[:, at * keys : (at + 1) * keys] - peak)
+        scores.append((k, here))
+    total, out = 0.0, 0.0
+    for k, here in scores:
+        p = jnp.exp(s_ref[:, here] - peak)
         keep = mask(i, k)
         if keep is not None:
             p = jnp.where(keep, p, 0.0)
-        s_ref[:, at * keys : (at + 1) * keys] = p
         total = total + jnp.sum(p, -1, keepdims=True)
-        out = out + dot(p.astype(BF), value_of(k))
-    inverse = 1.0 / total
-    out = out * inverse
-    o_ref[i] = out.astype(BF)
-    do = do_ref[i]
+        out = out + jnp.dot(p.astype(BF), value_of(k), preferred_element_type=F32)
+    return out / total, peak + jnp.log(total)
+
+
+def attention_backward(i, prompt_runs, mask, q_ref, do_ref, key, value_of, out, lse, turn_ref, sum_ref):
+    by_rows = (((1,), (1,)), ((), ()))
+    by_tokens = (((0,), (0,)), ((), ()))
+
+    def dot(a, b, dims=(((1,), (0,)), ((), ()))):
+        return lax.dot_general(a, b, dims, preferred_element_type=F32)
+
+    q, do = q_ref[i], do_ref[i]
     delta = jnp.sum(out * do.astype(F32), -1, keepdims=True)
-    dq = jnp.zeros((m, HEAD_DIM), F32)
-    for at, k in enumerate(pieces):
-        p = s_ref[:, at * keys : (at + 1) * keys] * inverse
-        dp = dot(do, value_of(k), by_rows)
-        ds = (p * (dp - delta)).astype(BF)
-        dq = dq + dot(ds, key(k))
+    dq = 0.0
+    for k in pieces_of(i, prompt_runs):
+        keys = key(k)
+        p = jnp.exp(dot(q, keys, by_rows) - lse)
+        keep = mask(i, k)
+        if keep is not None:
+            p = jnp.where(keep, p, 0.0)
+        ds = (p * (dot(do, value_of(k), by_rows) - delta)).astype(BF)
+        dq = dq + dot(ds, keys)
         dk = dot(ds, q, by_tokens)
         dv = dot(p.astype(BF), do, by_tokens)
         if i == k:
@@ -1054,7 +1172,7 @@
             sum_ref[k, :, :HEAD_DIM] = sum_ref[k, :, :HEAD_DIM] + dk
             sum_ref[k, :, HEAD_DIM:] = sum_ref[k, :, HEAD_DIM:] + dv
     dq = (dq * (1.0 / math.sqrt(HEAD_DIM))).astype(BF).astype(F32)
-    dq_ref[i] = turn(dq, [turn_ref[t, i] for t in range(3)], -1.0).astype(BF)
+    return turn(dq, [turn_ref[t, i] for t in range(3)], -1.0)
 
 
 def attention_kernel(prompt_runs, one_prompt, q_ref, do_ref, kv_ref, row_ref, col_ref, turn_ref,
@@ -1067,11 +1185,19 @@
             return None
         return rows[:, 2:3] == cols[2:3, :]
 
+    def key(k):
+        return kv_ref[k, :, :HEAD_DIM]
+
+    def value_of(k):
+        return kv_ref[k, :, HEAD_DIM:]
+
     for i in range(q_ref.shape[0]):
-        attention_step(
-            i, prompt_runs, mask, q_ref, do_ref, lambda k: kv_ref[k, :, :HEAD_DIM], lambda k: kv_ref[k, :, HEAD_DIM:],
-            turn_ref, o_ref, dq_ref, s_ref, sum_ref,
+        out, lse = attention_forward(i, prompt_runs, mask, q_ref, key, value_of, s_ref)
+        o_ref[i] = out.astype(BF)
+        back = attention_backward(
+            i, prompt_runs, mask, q_ref, do_ref, key, value_of, out, lse, turn_ref, sum_ref
         )
+        dq_ref[i] = back.astype(BF)
     dkv_ref[...] = sum_ref[...].astype(BF)
 
 
@@ -1233,15 +1359,13 @@
         trig_of(base_position), trig_of(within), row_tokens[:, :, None], col_tokens[:, None, :],
     )
     n_all, g_all, w_all, note, tables = opened[:5]
-    n_all = n_all.reshape(group_rows, width)
-    g_all = g_all.reshape(group_rows, width)
-    w_all = w_all.reshape(width, block_columns + HEAD_DIM + hidden)
+    w_all = w_all.reshape(width, w_all.shape[-1])
     bias_block = note[:note_rows].reshape(block_columns)
     out_bias = note[note_rows : note_rows + slice_rows].reshape(width)
     if fuse:
-        attended, activated, d_expanded, d_queries, d_pairs = opened[5:]
-        attended = attended.reshape(group_rows, HEAD_DIM)
+        left, right, half, part = opened[5:]
     else:
+        n_all, g_all = n_all.reshape(group_rows, width), g_all.reshape(group_rows, width)
         flat = tables.reshape(3, group_rows, lanes)
         cosine, sine = flat[0, :, : ROT // 2], flat[2, :, ROT // 2 : ROT]
         w_in, w_out = w_all[:, :block_columns], w_all[:, block_columns:]
@@ -1273,21 +1397,33 @@
         )
         attended = attended.reshape(group_rows, HEAD_DIM)
 
-    d_pairs = d_pairs.reshape(runs, ways, 4, rows_run, 2 * HEAD_DIM)
-    if ways > 1:
-        alike = [[w2 * 2 * HEADS + k for w2 in range(ways)] for k in range(2 * HEADS)]
-        d_pairs = lax.psum_scatter(
-            d_pairs.astype(F32), "blk", scatter_dimension=1, axis_index_groups=alike, tiled=True
-        ).astype(BF)
-    d_pairs = d_pairs[:, 0]
+        left = jnp.concatenate([attended, activated], 1)
+        part = lax.dot_general(left, w_out, (((1,), (1,)), ((), ())), preferred_element_type=F32)
+        part = part.reshape(runs, HEADS, STRIPE, width)
+        others = [[w2 * 2 * HEADS + h2 * 2 + c2 for h2 in range(HEADS)] for w2 in range(ways) for c2 in range(2)]
+        out_rows = lax.psum_scatter(part, "blk", scatter_dimension=1, axis_index_groups=others, tiled=True)[:, 0]
+        half = part = None
+        n_all, g_all = n_all.T, g_all.T
+        d_pairs = d_pairs.astype(F32).reshape(runs, ways, 2, 2, rows_run, 2 * HEAD_DIM).transpose(1, 3, 2, 0, 4, 5)
+        d_pairs = d_pairs.reshape(2 * ways, 2, runs, rows_run, 2 * HEAD_DIM)
+        alike = [[w2 * 2 * HEADS + h2 * 2 + c2 for w2 in range(ways) for c2 in range(2)] for h2 in range(HEADS)]
+        d_pairs = lax.psum_scatter(d_pairs, "blk", scatter_dimension=0, axis_index_groups=alike, tiled=True)[0]
+        d_pairs = lax.psum_scatter(d_pairs, "head", scatter_dimension=0, tiled=True)
+        d_pairs = d_pairs.reshape(group_rows, 2 * HEAD_DIM)
+        d_keys = rotate(d_pairs[:, :HEAD_DIM].astype(BF).astype(F32), cosine, -sine).astype(BF)
+        right = jnp.concatenate(
+            [d_queries.reshape(group_rows, HEAD_DIM), d_keys, d_pairs[:, HEAD_DIM:].astype(BF), d_expanded], 1
+        )
+
     own_sums = jnp.sum(grad_out, 0).reshape(width // lanes, lanes)
     sum_note = jnp.concatenate(
         [jnp.zeros((note_rows, lanes), F32), own_sums, jnp.zeros((-(note_rows + width // lanes) % 8, lanes), F32)]
     )
     out_sum, e_sum, owned_a, owned_b, owned_notes = finish(
-        ways, rows, attended, activated, d_expanded, d_queries, d_pairs,
-        tables, w_all, n_all, g_all, sum_note,
-    )
+        ways, rows, left, right, w_all, n_all, g_all, sum_note, half, part
+    )
+    if not fuse:
+        out_sum = out_rows
     output = restored((states + out_sum.reshape(tok_dev, width) + out_bias).astype(BF))
     e_sum = e_sum.reshape(tok_dev, width)
     dx = inverse_spread * (

time: 430 us -> 395 us (0.919)
  the two profiles are of different devices: /device:TPU:0 before, /device:TPU:8 now
where the time goes in v4:
time: 395 us; the launch traced here: 389 us
  Pallas kernels  343 us (87%)
  other arithmetic  25.3 us (6%)
  local copies, waits for them, and re-layouts  15.7 us (4%)
    pallas_call x1, Pallas kernels, open_all(): pl.pallas_call(functools.partial(open_kernel, ways, tuple(cuts), fuse, pr...  198 us
    pallas_call x1, Pallas kernels, finish(): pl.pallas_call(functools.partial(finish_kernel, ways, early), out_shape=s...  146 us

profile of v4, /device:TPU:8, one launch (start us, length us, event | category | flops | bytes accessed | tf_op | source)
XLA Modules:
  0.0 389.4 jit_solution(18299842692225456271)
XLA Ops:
  0.7 0.8 fusion.29
  1.5 0.7 and_select_fusion
  2.2 0.8 select_reduce_fusion.1
  3.0 0.7 convert_element_type.97
  3.6 0.7 convert_element_type.102
  4.3 0.7 convert_element_type.100
  5.0 0.7 convert_element_type.104
  6.6 0.8 add_dynamic-update-slice_fusion.2
  8.2 0.7 add_select_fusion
  8.9 1.3 select_reduce_fusion
  11.4 1.0 copy.100
  12.7 0.9 broadcast_add_fusion.refs_6_
  13.6 1.1 convert_reduce_fusion
  14.7 0.7 maximum_maximum_fusion.1.note
  16.5 1.7 reshape.299
  18.9 1.0 fusion.15
  20.6 0.7 maximum_maximum_fusion.refs_3_
  21.3 1.5 bitcast_bitcast_fusion
  22.8 1.9 pad_maximum_fusion.refs_2_
  24.7 197.7 %shard_map.271 = (bf16[2048,1024]{1,0:T(8,128)(2,1)}, bf16[2048,1024]{1,0:T(8,128)(2,1)}, bf16[2,1,8,2,64,1792]{5,4,3,2,1,0:T(8,128)(2,1)}, f32[32,128]{1,0:T(8,...) custom-call(bf16[8,16,2048]{2,1,0:T(8,128)(2,1)} %bitcast.138, ...), custom_call_target="tpu_custom_call" | custom-call | tf_op jit(solution)/shard_map/pallas_call | solution.py:612
  222.4 145.6 %shard_map.272 = (f32[8,16,2048]{2,1,0:T(8,128)}, f32[8,16,2048]{2,1,0:T(8,128)}, bf16[8,64,2304]{2,1,0:T(8,128)(2,1)}, bf16[8,64,768]{2,1,0:T(8,128)(2,1)}, f32[8,32,128]{2,1,0:T(8,128)}) custom-call(bf16[8,4,2,16,1280]{4,3,2,1,0:T(8,128)(2,1)} %bitcast.136, bf16[8,4,2,16,1792]{4,3,2,1,0:T(8,128)(2,1)} %bitcast.133, bf16[2048,1792]{1,0:T(8,128)(2,1)} %bitcast.127, ...), custom_call_target="tpu_custom_call" | custom-call | tf_op jit(solution)/shard_map/pallas_call | solution.py:1109
  368.1 1.6 fusion.12
  370.1 1.9 fusion.9
  372.0 1.1 convolution_convert_fusion
  373.1 1.1 convolution_convert_fusion.1
  376.1 1.1 reshape.325
  377.2 0.9 copy.79
  379.3 2.2 fusion.8
  382.6 1.5 copy.88
  384.1 0.8 copy.87
  385.1 1.1 copy-done.5
  386.2 2.5 fusion.4
  (99 shorter events, 10.8 us)
Async XLA Ops:
  0.6 13.0 %copy-start = (bf16[128,2048]{1,0:T(8,128)(2,1)S(1)}, bf16[128,2048]{1,0:T(8,128)(2,1)}, u32[]{:S(2)}) copy-start(bf16[128,2048]{1,0:T(8,128)(2,1)} %param.32) | copy-start | bytes 1572868
  0.7 14.7 %copy-start.7 = (bf16[64,6144]{1,0:T(8,128)(2,1)S(1)}, bf16[64,6144]{1,0:T(8,128)(2,1)}, u32[]{:S(2)}) copy-start(bf16[64,6144]{1,0:T(8,128)(2,1)} %param.22) | copy-start | bytes 2359300
  12.4 3.3 copy-start.14
  16.1 2.1 copy-start.11
  18.2 1.6 copy-start.4
  18.9 1.4 copy-start.15
  21.3 1.5 copy-start.6
  368.0 1.7 copy-start.2
  368.0 1.9 copy-start.12
  368.0 2.0 copy-start.13
  368.1 2.0 copy-start.3
  370.1 18.6 %copy-start.16 = (f32[64]{0:T(128)}, f32[64]{0:T(128)S(1)}, u32[]{:S(2)}) copy-start(f32[64]{0:T(128)S(1)} %dynamic_slice.34) | copy-start | bytes 772
  372.0 4.1 %copy-start.10 = (bf16[8,64,768]{2,1,0:T(8,128)(2,1)S(1)}, bf16[8,64,768]{2,1,0:T(8,128)(2,1)}, u32[]{:S(2)}) copy-start(bf16[8,64,768]{2,1,0:T(8,128)(2,1)} %get-tuple-element.38) | copy-start | bytes 2359300
  378.2 1.1 copy-start.8
  378.7 2.8 copy-start.9
  384.9 1.2 copy-start.5
  385.1 4.1 %copy-start.1 = (bf16[128,2048]{1,0:T(8,128)(2,1)S(1)}, bf16[128,2048]{1,0:T(8,128)(2,1)}, u32[]{:S(2)}) copy-start(bf16[128,2048]{1,0:T(8,128)(2,1)} %param.32) | copy-start | bytes 1572868

commit v5 on v4

--- a/solution.py
+++ b/solution.py
@@ -3,6 +3,7 @@
 
 import jax
 import jax.numpy as jnp
+import numpy as np
 from jax import lax
 from jax.experimental import pallas as pl
 from jax.experimental.pallas import tpu as pltpu
@@ -142,18 +143,21 @@
 
 
 def open_kernel(ways, cuts, fuse, prompt_runs, prompt_total, *refs):
-    names = ["n_in", "g_in", "w_in", "note_in", "trig_in", "step_in", "row_tok", "col_tok", "n_out", "g_out", "w_out", "note_out", "turn_out"]
+    names = ["x_in", "g_in", "tokens", "places", "gain_one", "shift_one", "gain_two", "shift_two", "qkv_bias", "expand_bias", "dense_bias", "shrink_bias", "freq_in", "step_in"]
+    names += ["qkv_in", "expand_in", "dense_in", "shrink_in", "n_out", "g_out", "w_out", "note_out", "turn_out", "sums_out"]
     if fuse:
         names += ["left_out", "right_out", "half_out", "part_out"]
     names += ["v_n", "v_g", "v_w", "v_turn", "trig", "note", "note_c", "note_x", "note_w", "note_h", "own", "put"]
+    names += ["v_qkv", "v_expand", "trig_own", "placed", "sums"]
     names += ["ns", "nr", "gs", "gr", "wa", "wr", "xs", "xr", "cs", "cr", "t_s", "t_r", "nc_s", "nc_r", "nx_s", "nx_r", "nw_s", "nw_r", "nh_s", "nh_r"]
     if fuse:
-        names += ["v_q", "v_do", "v_kv", "v_slope", "v_left", "v_right", "v_out", "lse", "s_ref", "sum_ref", "kv_c", "kv_x", "o_p", "o_y", "flat", "flat_sem"]
+        names += ["v_q", "v_do", "v_kv", "v_slope", "v_left", "v_right", "v_out", "lse", "s_ref", "sum_ref", "kv_c", "kv_x", "o_p", "o_y", "flat", "flat_sem", "row_tok", "col_tok"]
         names += ["kx_s", "kx_r", "kc_s", "kc_r", "fc_s", "fc_r", "fx_s", "fx_r", "oy_s", "oy_r"]
     at = dict(zip(names, refs, strict=True))
-    (n_in, g_in, w_in, note_in, trig_in, step_in, n_out, g_out, w_out, turn_out, v_n, v_g, v_w, v_turn) = (
-        at[k] for k in ["n_in", "g_in", "w_in", "note_in", "trig_in", "step_in", "n_out", "g_out", "w_out", "turn_out", "v_n", "v_g", "v_w", "v_turn"]
-    )
+    (step_in, n_out, g_out, w_out, turn_out, v_n, v_g, v_w, v_turn) = (
+        at[k] for k in ["step_in", "n_out", "g_out", "w_out", "turn_out", "v_n", "v_g", "v_w", "v_turn"]
+    )
+    v_qkv, v_expand, trig_own, placed, sums = (at[k] for k in ["v_qkv", "v_expand", "trig_own", "placed", "sums"])
     trig, note, note_c, note_x, note_w, note_h, own, put = (
         at[k] for k in ["trig", "note", "note_c", "note_x", "note_w", "note_h", "own", "put"]
     )
@@ -163,10 +167,6 @@
     width = v_n.shape[-1]
     per_run = HEADS * STRIPE
     stage_a = [(dw, dh) for dw in range(ways) for dh in range(HEADS) if (dw, dh) != (0, 0)]
-    greet(
-        [place.device(w=(w + dw) % ways, h=(h + dh) % HEADS) for dw, dh in stage_a]
-        + [place.peer_x(), place.peer_c()]
-    )
     sends, puts = [], []
 
     def send(src, dst, s, r, device):
@@ -180,15 +180,113 @@
         copy.start()
         puts.append(copy)
 
-    mine = [
-        pltpu.make_async_copy(w_in.at[h], v_w.at[x, w, h, c], own.at[0]),
-        pltpu.make_async_copy(n_in, v_n.at[:, h], own.at[1]),
-        pltpu.make_async_copy(g_in, v_g.at[:, h], own.at[2]),
-        pltpu.make_async_copy(trig_in, trig.at[h], own.at[3]),
-        pltpu.make_async_copy(note_in, note, own.at[4]),
+    devices, rows = at["tokens"].shape[0], v_qkv.shape[0]
+    hidden = v_expand.shape[1] // HEADS
+    run_size = devices * STRIPE
+    me = x * (2 * HEADS * ways) + w * (2 * HEADS) + h * 2 + c
+    raw = [
+        pltpu.make_async_copy(at["qkv_in"], v_qkv, own.at[0]),
+        pltpu.make_async_copy(at["expand_in"], v_expand, own.at[1]),
     ]
-    for copy in (mine[4], mine[0], mine[3], mine[1], mine[2]):
+    for copy in raw:
         copy.start()
+    mine = at["tokens"][pl.ds(me, 1), :]
+    mine_run = mine // run_size
+    tok_dev = mine.shape[1]
+    pick = lax.broadcasted_iota(jnp.int32, (tok_dev, tok_dev), 0) == mine_run * STRIPE + mine % STRIPE
+    pick = jnp.where(pick, 1.0, 0.0).astype(BF)
+
+    def ordered(ref):
+        return jnp.dot(pick, ref[...], preferred_element_type=F32)
+
+    states = ordered(at["x_in"])
+    centered = states - jnp.mean(states, -1, keepdims=True)
+    normed = centered * lax.rsqrt(jnp.mean(centered * centered, -1, keepdims=True) + 1e-05)
+    v_n[:, pl.ds(h, 1)] = normed.astype(BF).reshape(runs, 1, STRIPE, width)
+    grads = ordered(at["g_in"])
+    v_g[:, pl.ds(h, 1)] = grads.astype(BF).reshape(runs, 1, STRIPE, width)
+    sums[...] = jnp.zeros_like(sums)
+    g_sum = jnp.sum(grads, 0, keepdims=True)
+    first_sum = (3 * HEAD_DIM + hidden) // 128
+    for k in range(width // 128):
+        sums[first_sum + k : first_sum + k + 1, :] = g_sum[:, k * 128 : (k + 1) * 128]
+    far_off = jnp.int32(2**30)
+    for k in range(runs):
+        start = jnp.min(jnp.where(mine_run == k, at["places"][...], far_off), 1, keepdims=True)
+        angle = start.astype(F32) * at["freq_in"][...]
+        turned = lax.broadcasted_iota(jnp.int32, angle.shape, 1) < ROT
+        trig_own[0, k : k + 1] = jnp.where(turned, jnp.cos(angle), 1.0)
+        trig_own[1, k : k + 1] = jnp.where(turned, jnp.sin(angle), 0.0)
+
+    def share_of(name):
+        return at[name][...].astype(F32).reshape(1, at[name].shape[0])
+
+    def place_share(value, first):
+        count = value.shape[1]
+        span = -(-count // 128) * 128 + 128
+        value = jnp.concatenate([value, jnp.zeros((1, span - count), F32)], 1)
+        value = pltpu.roll(value, (me * count) % 128, 1)
+        for k in range(span // 128):
+            placed[pl.ds(first + me * count // 128 + k, 1), :] = value[:, k * 128 : (k + 1) * 128]
+
+    placed[...] = jnp.zeros_like(placed)
+    q_rows, e_rows, o_rows = 3 * width // 128, HEADS * hidden // 128, width // 128
+    place_share(share_of("qkv_bias"), 0)
+    place_share(share_of("expand_bias"), q_rows + 1)
+    place_share(share_of("dense_bias") + share_of("shrink_bias"), q_rows + e_rows + 2)
+    square = lax.broadcasted_iota(jnp.int32, (rows, rows), 0) == lax.broadcasted_iota(jnp.int32, (rows, rows), 1)
+    note[...] = jnp.zeros_like(note)
+
+    def spread(weight, gain, shift, step, put_rows):
+        diagonal = jnp.where(square, gain, 0.0).astype(BF)
+        for at_col in range(0, weight.shape[1], step):
+            value = weight[:, at_col : at_col + step]
+            through = jnp.dot(jnp.broadcast_to(shift, (16, rows)).astype(BF), value, preferred_element_type=F32)
+            weight[:, at_col : at_col + step] = jnp.dot(diagonal, value, preferred_element_type=F32).astype(BF)
+            for k in range(step // 128):
+                put_rows(at_col // 128 + k, through[:1, k * 128 : (k + 1) * 128])
+
+    def qkv_row(k, value):
+        third, rest = k // (q_rows // 3), k % (q_rows // 3)
+        hh, kk = rest // (HEAD_DIM // 128), rest % (HEAD_DIM // 128)
+        to = third * (HEAD_DIM // 128) + kk
+        note[hh, to : to + 1] = value + placed[k : k + 1, :]
+
+    def expand_row(k, value):
+        hh, kk = k // (hidden // 128), k % (hidden // 128)
+        to = 3 * HEAD_DIM // 128 + kk
+        note[hh, to : to + 1] = value + placed[q_rows + 1 + k : q_rows + 2 + k, :]
+
+    raw[0].wait()
+    spread(v_qkv, share_of("gain_one"), share_of("shift_one"), 1024, qkv_row)
+    raw[1].wait()
+    spread(v_expand, share_of("gain_two"), share_of("shift_two"), 1024, expand_row)
+    to = (3 * HEAD_DIM + hidden) // 128
+    first = q_rows + e_rows + 2
+    note[:, to : to + o_rows] = jnp.broadcast_to(placed[first : first + o_rows][None], (HEADS, o_rows, 128))
+    greet(
+        [place.device(w=(w + dw) % ways, h=(h + dh) % HEADS) for dw, dh in stage_a]
+        + [place.peer_x(), place.peer_c()]
+    )
+
+    def share(g, hs):
+        first, count = cuts[g]
+        if g < 3:
+            return v_qkv.at[:, pl.ds(pl.multiple_of(g * width + hs * HEAD_DIM, 256), count)]
+        if g == 3:
+            return v_expand.at[:, pl.ds(pl.multiple_of(hs * hidden, 256), count)]
+        if g == 4:
+            return at["dense_in"].at[:, pl.ds(pl.multiple_of(hs * HEAD_DIM, 256), count)]
+        return at["shrink_in"].at[:, pl.ds(pl.multiple_of(hs * hidden + (g - 5) * count, 256), count)]
+
+    kept = [
+        pltpu.make_async_copy(share(g, h), v_w.at[x, w, h, c, :, pl.ds(*cuts[g])], own.at[2 + g]) for g in range(len(cuts))
+    ]
+    trig_kept = pltpu.make_async_copy(trig_own, trig.at[h], own.at[2 + len(cuts)])
+    for copy in kept + [trig_kept]:
+        copy.start()
+    n_in, g_in = v_n.at[:, h], v_g.at[:, h]
+    save(sums, at["sums_out"])
     n_first_z, n_first_y, n_far, n_near, n_last, n_side, n_sent = relay_rows(place, n_in, v_n, at["ns"], at["nr"])
     g_first_z, g_first_y, g_far, g_near, g_last, g_side, g_sent = relay_rows(place, g_in, v_g, at["gs"], at["gr"])
     wa, wr, xs, xr, cs, cr = (at[k] for k in ["wa", "wr", "xs", "xr", "cs", "cr"])
@@ -201,7 +299,7 @@
             if dh % 2 != odd:
                 continue
             h2 = (h + dh) % HEADS
-            send(w_in.at[h2, :, columns(g)], v_w.at[x, w, h, c, :, columns(g)], wa.at[g, k], wr.at[g, w, h],
+            send(share(g, h2), v_w.at[x, w, h, c, :, columns(g)], wa.at[g, k], wr.at[g, w, h],
                  place.device(w=(w + dw) % ways, h=h2))
 
     def w_across(g):
@@ -209,6 +307,7 @@
             ws, hs = (w - dw) % ways, (h - dh) % HEADS
             spot = v_w.at[x, ws, hs, c, :, columns(g)]
             remote(spot, spot, wa.at[g, 0], wr.at[g, ws, hs], place.peer_x()).wait_recv()
+        kept[g].wait()
         block = v_w.at[x, :, :, c, :, columns(g)]
         send(block, block, xs.at[g], xr.at[g], place.peer_x())
         send(block, block, cs.at[g, 0], cr.at[g, 0], place.peer_c())
@@ -234,10 +333,9 @@
 
     def trig_send():
         for k in range(1, HEADS):
-            send(trig_in, trig.at[h], at["t_s"].at[k], at["t_r"].at[h], place.device(h=(h + k) % HEADS))
+            send(trig_own, trig.at[h], at["t_s"].at[k], at["t_r"].at[h], place.device(h=(h + k) % HEADS))
 
     def note_first():
-        mine[4].wait()
         state["note"] = send(note, note_c, at["nc_s"].at[0], at["nc_r"].at[0], place.peer_c())
 
     def note_cross():
@@ -278,7 +376,7 @@
         save(note_h.at[h], at["note_out"])
 
     def turn_tables():
-        mine[3].wait()
+        trig_kept.wait()
         for k in range(1, HEADS):
             hs = (h - k) % HEADS
             remote(trig.at[hs], trig.at[hs], at["t_s"].at[k], at["t_r"].at[hs], place.peer_x()).wait_recv()
@@ -295,8 +393,7 @@
         if not fuse:
             save(v_turn, turn_out)
 
-    def rows_done(copy, side, src, dst):
-        copy.wait()
+    def rows_done(side, src, dst):
         side()
         if not fuse:
             save(src, dst)
@@ -321,7 +418,6 @@
         step(0.02, w_first, k, 1)
         step(0.02, w_first, k, 0)
     step(0.2, note_first)
-    step(2, mine[0].wait)
     step(3, note_cross)
     step(6, note_out)
     for k in range(3):
@@ -339,7 +435,7 @@
     step(52.5, g_first_y)
     step(55, turn_tables)
     step(57, note_sum)
-    step(65, rows_done, mine[1], n_side, v_n, n_out)
+    step(65, rows_done, n_side, v_n, n_out)
     step(75.5, w_across, expand_at)
     step(86, w_across, dense_at)
     step(86.1, g_near)
@@ -349,12 +445,12 @@
         step(98.2, w_first, g, 0)
     step(112, w_beside, expand_at)
     step(113, w_ready, expand_at)
-    step(117, g_last)
+    step(117.7, g_last)
     step(121.5, w_beside, dense_at)
-    step(134, rows_done, mine[2], g_side, v_g, g_out)
+    step(134, rows_done, g_side, v_g, g_out)
     step(134.1, w_ready, dense_at)
     for k, g in enumerate(shrink):
-        step((125, 130, 135, 140)[k], w_across, g)
+        step((117.6, 117.72, 117.83, 117.95)[k], w_across, g)
         step((135.6, 142, 147, 152)[k], w_beside, g)
         step(156, w_ready, g)
     if fuse:
@@ -422,13 +518,41 @@
 
         row_tok, col_tok = at["row_tok"], at["col_tok"]
 
+        def token_tables():
+            tokens = at["tokens"][...]
+            starts = [
+                jnp.min(jnp.where(tokens // run_size == k, tokens, far_off), 1, keepdims=True) for k in range(runs)
+            ]
+            base = jnp.concatenate(starts, 1)
+            parts_of = [(base // 64).astype(F32).astype(BF), (base % 64).astype(F32).astype(BF)]
+            row = lax.broadcasted_iota(jnp.int32, (per_run, devices), 0)
+            owner = x * (2 * HEADS) + row // STRIPE * 2 + c
+            pick_row = owner == lax.broadcasted_iota(jnp.int32, (per_run, devices), 1)
+            pick_row = jnp.where(pick_row, 1.0, 0.0).astype(BF)
+            lane = lax.broadcasted_iota(jnp.int32, (devices, 4 * per_run), 1)
+            group = lane // per_run
+            owner = group // 2 * (2 * HEADS) + lane % per_run // STRIPE * 2 + group % 2
+            pick_col = owner == lax.broadcasted_iota(jnp.int32, (devices, 4 * per_run), 0)
+            pick_col = jnp.where(pick_col, 1.0, 0.0).astype(BF)
+            high, low = (jnp.dot(pick_row, part, preferred_element_type=F32) for part in parts_of)
+            within = lax.broadcasted_iota(jnp.int32, (per_run, runs), 0) % STRIPE
+            row_tok[...] = (high * 64 + low).astype(jnp.int32) + within
+            turn_over = (((0,), (0,)), ((), ()))
+            high, low = (
+                lax.dot_general(part, pick_col, turn_over, preferred_element_type=F32) for part in parts_of
+            )
+            within = lax.broadcasted_iota(jnp.int32, (runs, 4 * per_run), 1) % STRIPE
+            col_tok[...] = (high * 64 + low).astype(jnp.int32) + within
+
+        step(74, token_tables)
+
         def segment(tokens):
             return jnp.where(tokens < prompt_total, -1 - tokens // PROMPT, (tokens - prompt_total) // CONT)
 
         def mask(i, k):
             if i != k:
                 return None
-            rows, cols = row_tok[i], col_tok[k]
+            rows, cols = row_tok[:, i : i + 1], col_tok[i : i + 1, :]
             return (segment(rows) == segment(cols)) & (cols <= rows)
 
         def attended_back():
@@ -446,13 +570,13 @@
         def attend(i):
             here = slice(i * per_run, (i + 1) * per_run)
             out, total = attention_forward(i, prompt_runs, mask, v_q, key, value_of, s_ref)
-            v_out[here], lse[here] = out, total
+            v_out[here], lse[:, i : i + 1] = out, total
             v_left[here, :HEAD_DIM] = out.astype(BF)
 
         def attend_back(i):
             here = slice(i * per_run, (i + 1) * per_run)
             back = attention_backward(
-                i, prompt_runs, mask, v_q, v_do, key, value_of, v_out[here], lse[here], v_turn, sum_ref
+                i, prompt_runs, mask, v_q, v_do, key, value_of, v_out[here], lse[:, i : i + 1], v_turn, sum_ref
             )
             v_right[here, :HEAD_DIM] = back.astype(BF)
 
@@ -533,7 +657,7 @@
         count = v_slope.shape[1] // tile
         for t in range(count):
             for m in range(2):
-                step(117.5 + 0.1 * t + 0.05 * m, expand, m, t)
+                step(117.51 + 0.1 * t + 0.05 * m, expand, m, t)
                 step(161 + 0.1 * t, shrink_back, m, t)
         step(134.5, attended_back)
         step(151.5, fold_first)
@@ -555,9 +679,21 @@
     g_sent()
 
 
-def open_all(ways, rows, hidden, prompt_runs, prompt_total, normed, grads, weights, notes, trig, steps, row_tok, col_tok):
-    runs, _, width = normed.shape
-    columns = weights.shape[2]
+def open_all(ways, prompt_runs, prompt_total, inputs, cotangent, tokens, positions, scales, biases, qkv, expand, dense, shrink):
+    tok_dev, width = inputs.shape
+    rows, hidden = qkv.shape[0], expand.shape[1] // HEADS
+    runs = tok_dev // STRIPE
+    columns = 3 * HEAD_DIM + hidden + HEAD_DIM + hidden
+    note_rows = -(-((3 * HEAD_DIM + hidden) // 128 + width // 128) // 8) * 8
+    notes = jax.ShapeDtypeStruct((HEADS, note_rows, 128), F32)
+    trig = jax.ShapeDtypeStruct((2, runs, 128), F32)
+
+    frequency = np.float32(10000.0) ** (-np.arange(0, ROT, 2, dtype=np.float32) / np.float32(ROT))
+    lanes_of = np.pad(np.concatenate([frequency, frequency]), (0, 128 - ROT))[None].astype(np.float32)
+    step_angles = np.arange(STRIPE, dtype=np.float32)[:, None] * lanes_of
+    turned = np.arange(128)[None] < ROT
+    steps = np.stack([np.where(turned, np.cos(step_angles), 1.0), np.where(turned, np.sin(step_angles), 0.0)])
+    lanes_of, steps = jnp.asarray(lanes_of), jnp.asarray(steps.astype(np.float32))
     fuse = ways == 1 and prompt_total == PROMPT
     head3 = 3 * HEAD_DIM
     cuts = [(k * HEAD_DIM, HEAD_DIM) for k in range(3)] + [(head3, hidden), (head3 + hidden, HEAD_DIM)]
@@ -575,7 +711,7 @@
     kept = head3 + hidden if fuse else columns
     outs = [
         shape((width, group) if fuse else gathered), shape((width, group) if fuse else gathered), shape(blocks[:-1] + (kept,)), shape(notes.shape[1:], F32),
-        shape((1, 1, 8, 128) if fuse else tables, F32),
+        shape((1, 1, 8, 128) if fuse else tables, F32), shape(notes.shape[1:], F32),
     ]
     if fuse:
         outs += [
@@ -588,8 +724,10 @@
         pltpu.VMEM(gathered, BF), pltpu.VMEM(gathered, BF), pltpu.VMEM(blocks, BF), pltpu.VMEM(tables, F32),
         pltpu.VMEM((HEADS,) + trig.shape, F32),
         pltpu.VMEM(notes.shape, F32), pltpu.VMEM(notes.shape, F32), pltpu.VMEM(notes.shape, F32),
-        pltpu.VMEM((extra,) + notes.shape, F32), pltpu.VMEM(notes.shape, F32),
-        DMA((5,)), DMA((count + 14,)),
+        pltpu.VMEM((extra,) + notes.shape if ways > 1 else (1, 1, 8, 128), F32), pltpu.VMEM(notes.shape, F32),
+        DMA((3 + count,)), DMA((count + 15,)),
+        pltpu.VMEM(qkv.shape, BF), pltpu.VMEM(expand.shape, BF), pltpu.VMEM(trig.shape, F32),
+        pltpu.VMEM(((3 * width + HEADS * hidden + width) // 128 + 8, 128), F32), pltpu.VMEM(notes.shape[1:], F32),
         DMA((7,)), DMA((HEADS,)), DMA((7,)), DMA((HEADS,)),
         DMA((count, ways * HEADS)), DMA((count, ways, HEADS)), DMA((count,)), DMA((count,)), DMA((count, 2)), DMA((count, 2)),
         DMA((HEADS,)), DMA((HEADS,)), DMA((1,)), DMA((1,)), DMA((1,)), DMA((1,)), DMA((extra,)), DMA((extra,)),
@@ -600,23 +738,26 @@
             pltpu.VMEM((runs, per_run, HEAD_DIM), BF), pltpu.VMEM((runs, per_run, HEAD_DIM), BF),
             pltpu.VMEM((runs, 4, per_run, 2 * HEAD_DIM), BF), pltpu.VMEM((group, hidden), F32),
             pltpu.VMEM((group, HEAD_DIM + hidden), BF), pltpu.VMEM((group, head3 + hidden), BF),
-            pltpu.VMEM((group, HEAD_DIM), F32), pltpu.VMEM((group, 1), F32),
+            pltpu.VMEM((group, HEAD_DIM), F32), pltpu.VMEM((per_run, runs), F32),
             pltpu.VMEM((per_run, (prompt_runs + 1) * 4 * per_run), F32),
             pltpu.VMEM((runs, 4 * per_run, 2 * HEAD_DIM), F32),
             pltpu.VMEM((runs, 2, per_run, 2 * HEAD_DIM), BF), pltpu.VMEM((runs, per_run, 2 * HEAD_DIM), BF),
             pltpu.VMEM((chunks, runs, 2, 2, 2, STRIPE, wide), BF), pltpu.VMEM((EARLY, runs, 2, 2, STRIPE, wide), BF),
             pltpu.VMEM((2, 256, group), BF), DMA((2,)),
+            pltpu.VMEM((per_run, runs), jnp.int32), pltpu.VMEM((runs, 4 * per_run), jnp.int32),
             DMA((4,)), DMA((4,)), DMA((2, 4)), DMA((2, 4)),
             DMA((2,)), DMA((2,)), DMA((1,)), DMA((1,)), DMA((EARLY,)), DMA((EARLY,)),
         ]
     return fuse, pl.pallas_call(
         functools.partial(open_kernel, ways, tuple(cuts), fuse, prompt_runs, prompt_total),
         out_shape=tuple(outs),
-        in_specs=[ANY] * 5 + [VMEM] * 3,
+        in_specs=[VMEM] * 14 + [ANY] * 4,
         out_specs=(ANY,) * len(outs),
         scratch_shapes=scratch,
         compiler_params=pltpu.CompilerParams(collective_id=0, has_side_effects=True, vmem_limit_bytes=62 * 2**20),
-    )(normed, grads, weights, notes, trig, steps, row_tok, col_tok)
+    )(
+        inputs, cotangent, tokens, positions, *scales, *biases, lanes_of, steps, qkv, expand, dense, shrink
+    )
 
 
 def exchange_kernel(ways, own, full, local, to_w, to_x, to_c, recv):
@@ -1116,6 +1257,150 @@
     )(*ins)
 
 
+def close_kernel(tokens, note, notes, gain_one, shift_one, gain_two, shift_two, *refs):
+    sources, rest = refs[:8], refs[8:]
+    (output, input_grad, gain_one_grad, shift_one_grad, gain_two_grad, shift_two_grad, qkv_out, qk_bias, v_bias, dense_out,
+     dense_bias, expand_out, expand_bias, shrink_out, shrink_bias) = rest[:15]
+    x_in, g_in, out_sum, e_sum, qkv_in, expand_in, own_a, own_b = kept = rest[15:23]
+    qkv_grad, dense_grad, expand_grad, shrink_grad, load, put = rest[23:]
+    loads = [pltpu.make_async_copy(src, dst, load.at[k]) for k, (src, dst) in enumerate(zip(sources, kept, strict=True))]
+    for k in (6, 7, 4, 5, 0, 2, 1, 3):
+        loads[k].start()
+    saves = []
+
+    def save(src, dst):
+        copy = pltpu.make_async_copy(src, dst, put.at[len(saves)])
+        copy.start()
+        saves.append(copy)
+
+    x, b = lax.axis_index("head"), lax.axis_index("blk")
+    devices, rows = tokens.shape[0], qkv_in.shape[0]
+    me = x * (devices // 2) + b
+    width = x_in.shape[1]
+    hidden = expand_in.shape[1] // HEADS
+    head_rows, block_rows = HEAD_DIM // 128, (3 * HEAD_DIM + hidden) // 128
+
+    square = lax.broadcasted_iota(jnp.int32, (rows, rows), 0) == lax.broadcasted_iota(jnp.int32, (rows, rows), 1)
+
+    def down(ref):
+        return jnp.sum(jnp.where(square, ref[...].astype(F32).reshape(1, rows), 0.0), 1, keepdims=True)
+
+    def across(column):
+        return jnp.sum(jnp.where(square, column, 0.0), 0, keepdims=True)
+
+    def sums_of(h, first, count):
+        return jnp.concatenate([notes[h, first + k : first + k + 1] for k in range(count)], 1)
+
+    def one_norm(gain, shift, weight, grad, pieces):
+        by_gain, by_shift = 0.0, 0.0
+        for first, value, column_sums in pieces:
+            count = value.shape[1]
+            here = slice(first, first + count)
+            kept = weight[:, here].astype(F32)
+            grad[:, here] = gain * value + shift * column_sums
+            by_gain = by_gain + jnp.sum(kept * value, 1, keepdims=True)
+            by_shift = by_shift + jnp.sum(kept * column_sums, 1, keepdims=True)
+        return across(by_gain), across(by_shift)
+
+    qkv_pieces = (
+        (t * width + h * HEAD_DIM, own_b[h, :, t * HEAD_DIM : (t + 1) * HEAD_DIM].astype(F32),
+         sums_of(h, t * head_rows, head_rows))
+        for h in range(HEADS) for t in range(3)
+    )
+    expand_pieces = (
+        (h * hidden, own_a[h, :, HEAD_DIM + hidden :].astype(F32), sums_of(h, 3 * head_rows, hidden // 128))
+        for h in range(HEADS)
+    )
+    loads[6].wait()
+    for h in range(HEADS):
+        shrink_grad[:, h * hidden : (h + 1) * hidden] = own_a[h, :, HEAD_DIM : HEAD_DIM + hidden].astype(F32)
+    save(shrink_grad, shrink_out)
+    for h in range(HEADS):
+        dense_grad[:, h * HEAD_DIM : (h + 1) * HEAD_DIM] = own_a[h, :, :HEAD_DIM].astype(F32)
+    save(dense_grad, dense_out)
+    loads[5].wait()
+    gain_two_grad[...], shift_two_grad[...] = one_norm(
+        down(gain_two), down(shift_two), expand_in, expand_grad, expand_pieces
+    )
+    save(expand_grad, expand_out)
+    loads[7].wait()
+    loads[4].wait()
+    gain_one_grad[...], shift_one_grad[...] = one_norm(down(gain_one), down(shift_one), qkv_in, qkv_grad, qkv_pieces)
+    save(qkv_grad, qkv_out)
+    for k in range(4):
+        loads[k].wait()
+
+    def share(row, count):
+        return jnp.where(me % (128 // count) == 0, row[:, :count], row[:, 128 - count :])
+
+    in_head = HEADS * head_rows
+    third, rest = me // in_head, me % in_head
+    qk_bias[...] = notes[pl.ds(rest // head_rows, 1), pl.ds(third * head_rows + rest % head_rows, 1)][0]
+    half = me // 2
+    v_bias[...] = share(notes[pl.ds(half // head_rows, 1), pl.ds(2 * head_rows + half % head_rows, 1)][0], rows)
+    per_head = hidden // 128
+    for k in range(2):
+        row = me * 2 + k
+        expand_bias[:, k * 128 : (k + 1) * 128] = notes[
+            pl.ds(row // per_head, 1), pl.ds(3 * head_rows + row % per_head, 1)
+        ][0]
+    total = 0.0
+    for h in range(HEADS):
+        total = total + notes[pl.ds(h, 1), pl.ds(block_rows + half, 1)][0]
+    dense_bias[...] = share(total, rows)
+    shrink_bias[...] = share(total, rows)
+
+    mine = tokens[pl.ds(me, 1), :]
+    tok_dev = mine.shape[1]
+    pick = lax.broadcasted_iota(jnp.int32, (tok_dev, tok_dev), 0) == mine // (devices * STRIPE) * STRIPE + mine % STRIPE
+    pick = jnp.where(pick, 1.0, 0.0).astype(BF)
+
+    def restored(value):
+        value = value.astype(BF)
+        return lax.dot_general(pick, value, (((0,), (0,)), ((), ())), preferred_element_type=F32).astype(BF)
+
+    states = jnp.dot(pick, x_in[...], preferred_element_type=F32)
+    bias = jnp.concatenate([note[block_rows + k : block_rows + k + 1] for k in range(width // 128)], 1)
+    output[...] = restored(states + out_sum[...].reshape(tok_dev, width) + bias)
+    centered = states - jnp.mean(states, -1, keepdims=True)
+    inverse_spread = lax.rsqrt(jnp.mean(centered * centered, -1, keepdims=True) + 1e-05)
+    normed = centered * inverse_spread
+    e = e_sum[...].reshape(tok_dev, width)
+    dx = inverse_spread * (e - jnp.mean(e, -1, keepdims=True) - normed * jnp.mean(e * normed, -1, keepdims=True))
+    input_grad[...] = restored(jnp.dot(pick, g_in[...], preferred_element_type=F32) + dx)
+    for copy in saves:
+        copy.wait()
+
+
+def close(tokens, inputs, cotangent, out_sum, e_sum, note, notes, scales, qkv, expand, own_a, own_b):
+    rows, hidden_all = expand.shape
+    width = inputs.shape[1]
+    devices = tokens.shape[0]
+
+    def shape(*dims):
+        return jax.ShapeDtypeStruct(dims, F32)
+
+    low = jax.ShapeDtypeStruct(inputs.shape, BF)
+    sources = (inputs, cotangent, out_sum, e_sum, qkv, expand, own_a, own_b)
+    outs = (
+        low, low, shape(1, rows), shape(1, rows), shape(1, rows), shape(1, rows), shape(rows, 3 * width),
+        shape(1, 2 * width // devices), shape(1, rows), shape(rows, width), shape(1, rows), shape(rows, hidden_all),
+        shape(1, hidden_all // devices), shape(rows, hidden_all), shape(1, rows),
+    )
+    large = (6, 9, 11, 13)
+    results = pl.pallas_call(
+        close_kernel,
+        out_shape=outs,
+        in_specs=[VMEM] * 7 + [ANY] * len(sources),
+        out_specs=tuple(ANY if k in large else VMEM for k in range(len(outs))),
+        scratch_shapes=[pltpu.VMEM(one.shape, one.dtype) for one in sources]
+        + [pltpu.VMEM(outs[k].shape, F32) for k in large]
+        + [DMA((len(sources),)), DMA((4,))],
+        compiler_params=pltpu.CompilerParams(vmem_limit_bytes=62 * 2**20),
+    )(tokens, note, notes, *scales, *sources)
+    return tuple(one[0] if one.shape[0] == 1 else one for one in results)
+
+
 def pieces_of(i, prompt_runs):
     return list(range(min(i + 1, prompt_runs))) + ([i] if i >= prompt_runs else [])
 
@@ -1216,11 +1501,6 @@
         scratch_shapes=[pltpu.VMEM((m, (prompt_runs + 1) * count), F32), pltpu.VMEM(pairs.shape, F32)],
         compiler_params=pltpu.CompilerParams(vmem_limit_bytes=60 * 2**20),
     )(queries, d_out, pairs, row_meta, col_meta, tables)
-
-
-def angles_of(positions):
-    frequency = 10000.0 ** (-jnp.arange(0, ROT, 2, dtype=F32) / ROT)
-    return positions.astype(F32)[:, None] * frequency[None, :]
 
 
 def rotate(values, cosine, sine):
@@ -1258,16 +1538,9 @@
     block_columns = head3 + hidden
 
     by_device = token_of_row.reshape(devices, tok_dev)
-    run_of = by_device // run_size
-    big = jnp.int32(2**30)
-    each_run = jnp.arange(runs, dtype=jnp.int32)
-    base = jnp.min(jnp.where(run_of[:, :, None] == each_run, by_device[:, :, None], big), 1)
     mine = lax.dynamic_index_in_dim(by_device, me, 0, False)
     sorted_at = mine // run_size * STRIPE + mine % STRIPE
     pick = (sorted_at[None, :] == jnp.arange(tok_dev, dtype=jnp.int32)[:, None]).astype(BF)
-    base_position = jnp.min(
-        jnp.where((mine // run_size)[:, None] == each_run, position_ids[:, None], big), 0
-    )
 
     def ordered(rows_in):
         return jnp.dot(pick, rows_in, preferred_element_type=F32).astype(BF)
@@ -1275,97 +1548,43 @@
     def restored(rows_in):
         return lax.dot_general(pick, rows_in, (((0,), (0,)), ((), ())), preferred_element_type=F32).astype(BF)
 
+    scales = (attn_norm_gain, attn_norm_bias, mlp_norm_gain, mlp_norm_bias)
+    fuse, opened = open_all(
+        ways, prompt_runs, prompt_total, inputs, cotangent, by_device, position_ids[None],
+        scales, (qkv_bias, expand_bias, dense_bias, shrink_bias),
+        qkv_weight, expand_weight, dense_weight, shrink_weight,
+    )
+    lanes = 128
+    note_rows = block_columns // lanes
+    slice_rows = width // lanes
+    rows_run = group_rows // runs
+    n_all, g_all, w_all, note, tables, sum_note = opened[:6]
+    w_all = w_all.reshape(width, w_all.shape[-1])
+    out_bias = note[note_rows : note_rows + slice_rows].reshape(width)
+    gain_one, shift_one = attn_norm_gain.astype(F32), attn_norm_bias.astype(F32)
+    gain_two, shift_two = mlp_norm_gain.astype(F32), mlp_norm_bias.astype(F32)
+    qkv_wide, expand_wide = qkv_weight.astype(F32), expand_weight.astype(F32)
     states = ordered(inputs).astype(F32)
-    grad_low = ordered(cotangent)
-    grad_out = grad_low.astype(F32)
+    grad_out = ordered(cotangent).astype(F32)
     average = jnp.mean(states, -1, keepdims=True)
     centered = states - average
     inverse_spread = lax.rsqrt(jnp.mean(centered * centered, -1, keepdims=True) + 1e-05)
     normed = centered * inverse_spread
-    normed_low = normed.astype(BF)
-
-    gain_one, shift_one = attn_norm_gain.astype(F32), attn_norm_bias.astype(F32)
-    gain_two, shift_two = mlp_norm_gain.astype(F32), mlp_norm_bias.astype(F32)
-    qkv_wide, expand_wide = qkv_weight.astype(F32), expand_weight.astype(F32)
-
-    def split_qkv(values):
-        return values.reshape(-1, 3, HEADS, HEAD_DIM).transpose(2, 0, 1, 3).reshape(HEADS, -1, head3)
-
-    def split(values):
-        return values.reshape(values.shape[0], HEADS, -1).transpose(1, 0, 2)
-
-    weights = jnp.concatenate(
-        [
-            split_qkv((qkv_wide * gain_one[:, None]).astype(BF)),
-            split((expand_wide * gain_two[:, None]).astype(BF)),
-            split(dense_weight),
-            split(shrink_weight),
-        ],
-        -1,
-    )
-    own_qkv_bias = lax.dynamic_update_slice_in_dim(
-        jnp.zeros((3 * width,), F32), qkv_bias.astype(F32), me * qkv_bias.shape[0], 0
-    )
-    own_expand_bias = lax.dynamic_update_slice_in_dim(
-        jnp.zeros((HEADS * hidden,), F32), expand_bias.astype(F32), me * expand_bias.shape[0], 0
-    )
-    bias_parts = jnp.concatenate(
-        [
-            split_qkv((jnp.sum(qkv_wide * shift_one[:, None], 0) + own_qkv_bias)[None])[:, 0],
-            split((jnp.sum(expand_wide * shift_two[:, None], 0) + own_expand_bias)[None])[:, 0],
-        ],
-        -1,
-    )
-    lanes = 128
-    note_rows = block_columns // lanes
-
-    slice_rows = width // lanes
-    own_out_bias = lax.dynamic_update_slice_in_dim(
-        jnp.zeros((width,), F32), dense_bias.astype(F32) + shrink_bias.astype(F32), me * rows, 0
-    )
-    notes = jnp.concatenate(
-        [
-            bias_parts.reshape(HEADS, note_rows, lanes),
-            jnp.broadcast_to(own_out_bias.reshape(1, slice_rows, lanes), (HEADS, slice_rows, lanes)),
-            jnp.zeros((HEADS, -(note_rows + slice_rows) % 8, lanes), F32),
-        ],
-        1,
-    )
-
-    def trig_of(positions):
-        angles = angles_of(positions)
-        cosine, sine = jnp.cos(angles), jnp.sin(angles)
-        rest = ((0, 0), (0, lanes - ROT))
-        return jnp.stack(
-            [
-                jnp.pad(jnp.concatenate([cosine, cosine], 1), rest, constant_values=1.0),
-                jnp.pad(jnp.concatenate([sine, sine], 1), rest),
-            ]
-        )
-
-    within = jnp.arange(STRIPE, dtype=jnp.int32)
-    rows_run = group_rows // runs
-
-    bases = base.reshape(2, ways, HEADS, 2, runs)
-    own_base = lax.dynamic_index_in_dim(bases, x, 0, False)
-    own_base = lax.dynamic_index_in_dim(own_base, w, 0, False)
-    own_base = lax.dynamic_index_in_dim(own_base, c, 1, False)
-    row_tokens = (own_base.T[:, :, None] + within).reshape(runs, rows_run)
-    col_tokens = (bases.transpose(4, 1, 0, 3, 2)[..., None] + within).reshape(runs, run_size)
-
-    fuse, opened = open_all(
-        ways, rows, hidden, prompt_runs, prompt_total,
-        normed_low.reshape(runs, STRIPE, width), grad_low.reshape(runs, STRIPE, width), weights, notes,
-        trig_of(base_position), trig_of(within), row_tokens[:, :, None], col_tokens[:, None, :],
-    )
-    n_all, g_all, w_all, note, tables = opened[:5]
-    w_all = w_all.reshape(width, w_all.shape[-1])
-    bias_block = note[:note_rows].reshape(block_columns)
-    out_bias = note[note_rows : note_rows + slice_rows].reshape(width)
     if fuse:
-        left, right, half, part = opened[5:]
+        left, right, half, part = opened[6:]
     else:
         n_all, g_all = n_all.reshape(group_rows, width), g_all.reshape(group_rows, width)
+        bias_block = note[:note_rows].reshape(block_columns)
+        run_of = by_device // run_size
+        each_run = jnp.arange(runs, dtype=jnp.int32)
+        base = jnp.min(jnp.where(run_of[:, :, None] == each_run, by_device[:, :, None], 2**30), 1)
+        within = jnp.arange(STRIPE, dtype=jnp.int32)
+        bases = base.reshape(2, ways, HEADS, 2, runs)
+        own_base = lax.dynamic_index_in_dim(bases, x, 0, False)
+        own_base = lax.dynamic_index_in_dim(own_base, w, 0, False)
+        own_base = lax.dynamic_index_in_dim(own_base, c, 1, False)
+        row_tokens = (own_base.T[:, :, None] + within).reshape(runs, rows_run)
+        col_tokens = (bases.transpose(4, 1, 0, 3, 2)[..., None] + within).reshape(runs, run_size)
         flat = tables.reshape(3, group_rows, lanes)
         cosine, sine = flat[0, :, : ROT // 2], flat[2, :, ROT // 2 : ROT]
         w_in, w_out = w_all[:, :block_columns], w_all[:, block_columns:]
@@ -1415,15 +1634,15 @@
             [d_queries.reshape(group_rows, HEAD_DIM), d_keys, d_pairs[:, HEAD_DIM:].astype(BF), d_expanded], 1
         )
 
-    own_sums = jnp.sum(grad_out, 0).reshape(width // lanes, lanes)
-    sum_note = jnp.concatenate(
-        [jnp.zeros((note_rows, lanes), F32), own_sums, jnp.zeros((-(note_rows + width // lanes) % 8, lanes), F32)]
-    )
     out_sum, e_sum, owned_a, owned_b, owned_notes = finish(
         ways, rows, left, right, w_all, n_all, g_all, sum_note, half, part
     )
-    if not fuse:
-        out_sum = out_rows
+    if fuse:
+        return close(
+            by_device, inputs, cotangent, out_sum, e_sum, note, owned_notes, scales, qkv_weight, expand_weight, owned_a,
+            owned_b,
+        )
+    out_sum = out_rows
     output = restored((states + out_sum.reshape(tok_dev, width) + out_bias).astype(BF))
     e_sum = e_sum.reshape(tok_dev, width)
     dx = inverse_spread * (

time: 395 us -> 358 us (0.906)
  other arithmetic: 25.3 us -> 0 us
  local copies, waits for them, and re-layouts: 15.7 us -> 0 us
  Pallas kernels: 343 us -> 354 us
    pallas_call x0 -> x1, Pallas kernels: none -> 8.17 us  [close(): pl.pallas_call(close_kernel, out_shape=outs, in_specs=[VMEM] * 7 + [ANY]...]
    reshape x10 -> x0, local copies, waits for them, and re-layouts: 7.57 us -> none  [the longest x3 2.45 us: join(): return values.transpose(1, 0, 2).reshape(values.shape[1], -1)]
    reduce_sum x8 -> x0, other arithmetic: 7.53 us -> none  [the longest x1 2.5 us: per_device(): jnp.sum(expand_wide * expand_sum, 1)]
    convert_element_type x9 -> x0, other arithmetic: 5.9 us -> none  [the longest x1 1.88 us: per_device(): input_grad = restored((grad_out + dx).astype(BF))]
    pallas_call x1, Pallas kernels: 198 us -> 202 us  [open_all(): pl.pallas_call(functools.partial(open_kernel, ways, tuple(cuts), fuse, pr...]
where the time goes in v5:
time: 358 us; the launch traced here: 355 us
  Pallas kernels  354 us (99%)
    pallas_call x1, Pallas kernels, open_all(): pl.pallas_call(functools.partial(open_kernel, ways, tuple(cuts), fuse, pr...  202 us
    pallas_call x1, Pallas kernels, finish(): pl.pallas_call(functools.partial(finish_kernel, ways, early), out_shape=s...  143 us
    pallas_call x1, Pallas kernels, close(): pl.pallas_call(close_kernel, out_shape=outs, in_specs=[VMEM] * 7 + [ANY]...  8.17 us

profile of v5, /device:TPU:8, one launch (start us, length us, event | category | flops | bytes accessed | tf_op | source)
XLA Modules:
  0.0 355.0 jit_solution(14141430978846187455)
XLA Ops:
  0.6 202.5 %shard_map.289 = (bf16[2048,1024]{1,0:T(8,128)(2,1)}, bf16[2048,1024]{1,0:T(8,128)(2,1)}, bf16[2,1,8,2,64,1792]{5,4,3,2,1,0:T(8,128)(2,1)}, f32[32,128]{1,0:T(8,...) custom-call(bf16[128,2048]{1,0:T(8,128)(2,1)} %refs_0_.3, ...), custom_call_target="tpu_custom_call" | custom-call | tf_op jit(solution)/shard_map/pallas_call | solution.py:751
  203.1 143.4 %shard_map.290 = (f32[8,16,2048]{2,1,0:T(8,128)}, f32[8,16,2048]{2,1,0:T(8,128)}, bf16[8,64,2304]{2,1,0:T(8,128)(2,1)}, bf16[8,64,768]{2,1,0:T(8,128)(2,1)}, f32[8,32,128]{2,1,0:T(8,128)}) custom-call(bf16[8,4,2,16,1280]{4,3,2,1,0:T(8,128)(2,1)} %bitcast.16, bf16[8,4,2,16,1792]{4,3,2,1,0:T(8,128)(2,1)} %bitcast.15, bf16[2048,1792]{1,0:T(8,128)(2,1)} %bitcast.14, ...), custom_call_target="tpu_custom_call" | custom-call | tf_op jit(solution)/shard_map/pallas_call | solution.py:1250
  346.5 8.2 %shard_map.291 = (bf16[128,2048]{1,0:T(8,128)(2,1)}, bf16[128,2048]{1,0:T(8,128)(2,1)}, f32[1,64]{1,0:T(1,128)}, f32[1,64]{1,0:T(1,128)}, f32[1,64]{1,0:T(1,128)...) custom-call(s32[32,128]{1,0:T(8,128)} %bitcast.18, ...), custom_call_target="tpu_custom_call" | custom-call | tf_op jit(solution)/shard_map/pallas_call | solution.py:1391

commit v6 on v5

--- a/solution.py
+++ b/solution.py
@@ -143,24 +143,26 @@
 
 
 def open_kernel(ways, cuts, fuse, prompt_runs, prompt_total, *refs):
-    names = ["x_in", "g_in", "tokens", "places", "gain_one", "shift_one", "gain_two", "shift_two", "qkv_bias", "expand_bias", "dense_bias", "shrink_bias", "freq_in", "step_in"]
-    names += ["qkv_in", "expand_in", "dense_in", "shrink_in", "n_out", "g_out", "w_out", "note_out", "turn_out", "sums_out"]
+    refs = list(refs)
+
+    def take(count):
+        taken = refs[:count]
+        del refs[:count]
+        return taken
+
+    (x_in, grad_in, token_ref, places, gain_one, shift_one, gain_two, shift_two, qkv_bias, expand_bias, dense_bias,
+     shrink_bias, freq_in, step_in, qkv_in, expand_in, dense_in, shrink_in) = take(18)
+    n_out, g_out, w_out, note_ref, turn_out, sums_out = take(6)
+    left_out, right_out, half_out, part_out = take(4) if fuse else [None] * 4
+    v_n, v_g, v_w, v_turn, trig, note, note_c, note_x, note_w, note_h, own, put = take(12)
+    v_qkv, v_expand, trig_own, placed, sums = take(5)
+    ns, nr, gs, gr, wa, wr, xs, xr, cs, cr = take(10)
+    t_s, t_r, nc_s, nc_r, nx_s, nx_r, nw_s, nw_r, nh_s, nh_r = take(10)
     if fuse:
-        names += ["left_out", "right_out", "half_out", "part_out"]
-    names += ["v_n", "v_g", "v_w", "v_turn", "trig", "note", "note_c", "note_x", "note_w", "note_h", "own", "put"]
-    names += ["v_qkv", "v_expand", "trig_own", "placed", "sums"]
-    names += ["ns", "nr", "gs", "gr", "wa", "wr", "xs", "xr", "cs", "cr", "t_s", "t_r", "nc_s", "nc_r", "nx_s", "nx_r", "nw_s", "nw_r", "nh_s", "nh_r"]
-    if fuse:
-        names += ["v_q", "v_do", "v_kv", "v_slope", "v_left", "v_right", "v_out", "lse", "s_ref", "sum_ref", "kv_c", "kv_x", "o_p", "o_y", "flat", "flat_sem", "row_tok", "col_tok"]
-        names += ["kx_s", "kx_r", "kc_s", "kc_r", "fc_s", "fc_r", "fx_s", "fx_r", "oy_s", "oy_r"]
-    at = dict(zip(names, refs, strict=True))
-    (step_in, n_out, g_out, w_out, turn_out, v_n, v_g, v_w, v_turn) = (
-        at[k] for k in ["step_in", "n_out", "g_out", "w_out", "turn_out", "v_n", "v_g", "v_w", "v_turn"]
-    )
-    v_qkv, v_expand, trig_own, placed, sums = (at[k] for k in ["v_qkv", "v_expand", "trig_own", "placed", "sums"])
-    trig, note, note_c, note_x, note_w, note_h, own, put = (
-        at[k] for k in ["trig", "note", "note_c", "note_x", "note_w", "note_h", "own", "put"]
-    )
+        (v_q, v_do, v_kv, v_slope, v_left, v_right, v_out, lse, s_ref, sum_ref, kv_c, kv_x, o_p, o_y, flat, flat_sem,
+         row_tok, col_tok) = take(18)
+        kx_s, kx_r, kc_s, kc_r, fc_s, fc_r, fx_s, fx_r, oy_s, oy_r = take(10)
+    assert not refs
     place = Place(ways)
     x, w, h, c = place.x, place.w, place.h, place.c
     runs = v_n.shape[0]
@@ -180,17 +182,17 @@
         copy.start()
         puts.append(copy)
 
-    devices, rows = at["tokens"].shape[0], v_qkv.shape[0]
+    devices, rows = token_ref.shape[0], v_qkv.shape[0]
     hidden = v_expand.shape[1] // HEADS
     run_size = devices * STRIPE
     me = x * (2 * HEADS * ways) + w * (2 * HEADS) + h * 2 + c
     raw = [
-        pltpu.make_async_copy(at["qkv_in"], v_qkv, own.at[0]),
-        pltpu.make_async_copy(at["expand_in"], v_expand, own.at[1]),
+        pltpu.make_async_copy(qkv_in, v_qkv, own.at[0]),
+        pltpu.make_async_copy(expand_in, v_expand, own.at[1]),
     ]
     for copy in raw:
         copy.start()
-    mine = at["tokens"][pl.ds(me, 1), :]
+    mine = token_ref[pl.ds(me, 1), :]
     mine_run = mine // run_size
     tok_dev = mine.shape[1]
     pick = lax.broadcasted_iota(jnp.int32, (tok_dev, tok_dev), 0) == mine_run * STRIPE + mine % STRIPE
@@ -199,11 +201,11 @@
     def ordered(ref):
         return jnp.dot(pick, ref[...], preferred_element_type=F32)
 
-    states = ordered(at["x_in"])
+    states = ordered(x_in)
     centered = states - jnp.mean(states, -1, keepdims=True)
     normed = centered * lax.rsqrt(jnp.mean(centered * centered, -1, keepdims=True) + 1e-05)
     v_n[:, pl.ds(h, 1)] = normed.astype(BF).reshape(runs, 1, STRIPE, width)
-    grads = ordered(at["g_in"])
+    grads = ordered(grad_in)
     v_g[:, pl.ds(h, 1)] = grads.astype(BF).reshape(runs, 1, STRIPE, width)
     sums[...] = jnp.zeros_like(sums)
     g_sum = jnp.sum(grads, 0, keepdims=True)
@@ -212,14 +214,14 @@
         sums[first_sum + k : first_sum + k + 1, :] = g_sum[:, k * 128 : (k + 1) * 128]
     far_off = jnp.int32(2**30)
     for k in range(runs):
-        start = jnp.min(jnp.where(mine_run == k, at["places"][...], far_off), 1, keepdims=True)
-        angle = start.astype(F32) * at["freq_in"][...]
+        start = jnp.min(jnp.where(mine_run == k, places[...], far_off), 1, keepdims=True)
+        angle = start.astype(F32) * freq_in[...]
         turned = lax.broadcasted_iota(jnp.int32, angle.shape, 1) < ROT
         trig_own[0, k : k + 1] = jnp.where(turned, jnp.cos(angle), 1.0)
         trig_own[1, k : k + 1] = jnp.where(turned, jnp.sin(angle), 0.0)
 
-    def share_of(name):
-        return at[name][...].astype(F32).reshape(1, at[name].shape[0])
+    def share_of(ref):
+        return ref[...].astype(F32).reshape(1, ref.shape[0])
 
     def place_share(value, first):
         count = value.shape[1]
@@ -231,9 +233,9 @@
 
     placed[...] = jnp.zeros_like(placed)
     q_rows, e_rows, o_rows = 3 * width // 128, HEADS * hidden // 128, width // 128
-    place_share(share_of("qkv_bias"), 0)
-    place_share(share_of("expand_bias"), q_rows + 1)
-    place_share(share_of("dense_bias") + share_of("shrink_bias"), q_rows + e_rows + 2)
+    place_share(share_of(qkv_bias), 0)
+    place_share(share_of(expand_bias), q_rows + 1)
+    place_share(share_of(dense_bias) + share_of(shrink_bias), q_rows + e_rows + 2)
     square = lax.broadcasted_iota(jnp.int32, (rows, rows), 0) == lax.broadcasted_iota(jnp.int32, (rows, rows), 1)
     note[...] = jnp.zeros_like(note)
 
@@ -258,9 +260,9 @@
         note[hh, to : to + 1] = value + placed[q_rows + 1 + k : q_rows + 2 + k, :]
 
     raw[0].wait()
-    spread(v_qkv, share_of("gain_one"), share_of("shift_one"), 1024, qkv_row)
+    spread(v_qkv, share_of(gain_one), share_of(shift_one), 1024, qkv_row)
     raw[1].wait()
-    spread(v_expand, share_of("gain_two"), share_of("shift_two"), 1024, expand_row)
+    spread(v_expand, share_of(gain_two), share_of(shift_two), 1024, expand_row)
     to = (3 * HEAD_DIM + hidden) // 128
     first = q_rows + e_rows + 2
     note[:, to : to + o_rows] = jnp.broadcast_to(placed[first : first + o_rows][None], (HEADS, o_rows, 128))
@@ -276,8 +278,8 @@
         if g == 3:
             return v_expand.at[:, pl.ds(pl.multiple_of(hs * hidden, 256), count)]
         if g == 4:
-            return at["dense_in"].at[:, pl.ds(pl.multiple_of(hs * HEAD_DIM, 256), count)]
-        return at["shrink_in"].at[:, pl.ds(pl.multiple_of(hs * hidden + (g - 5) * count, 256), count)]
+            return dense_in.at[:, pl.ds(pl.multiple_of(hs * HEAD_DIM, 256), count)]
+        return shrink_in.at[:, pl.ds(pl.multiple_of(hs * hidden + (g - 5) * count, 256), count)]
 
     kept = [
         pltpu.make_async_copy(share(g, h), v_w.at[x, w, h, c, :, pl.ds(*cuts[g])], own.at[2 + g]) for g in range(len(cuts))
@@ -286,10 +288,9 @@
     for copy in kept + [trig_kept]:
         copy.start()
     n_in, g_in = v_n.at[:, h], v_g.at[:, h]
-    save(sums, at["sums_out"])
-    n_first_z, n_first_y, n_far, n_near, n_last, n_side, n_sent = relay_rows(place, n_in, v_n, at["ns"], at["nr"])
-    g_first_z, g_first_y, g_far, g_near, g_last, g_side, g_sent = relay_rows(place, g_in, v_g, at["gs"], at["gr"])
-    wa, wr, xs, xr, cs, cr = (at[k] for k in ["wa", "wr", "xs", "xr", "cs", "cr"])
+    save(sums, sums_out)
+    n_first_z, n_first_y, n_far, n_near, n_last, n_side, n_sent = relay_rows(place, n_in, v_n, ns, nr)
+    g_first_z, g_first_y, g_far, g_near, g_last, g_side, g_sent = relay_rows(place, g_in, v_g, gs, gr)
 
     def columns(g):
         return pl.ds(cuts[g][0], cuts[g][1])
@@ -333,15 +334,15 @@
 
     def trig_send():
         for k in range(1, HEADS):
-            send(trig_own, trig.at[h], at["t_s"].at[k], at["t_r"].at[h], place.device(h=(h + k) % HEADS))
+            send(trig_own, trig.at[h], t_s.at[k], t_r.at[h], place.device(h=(h + k) % HEADS))
 
     def note_first():
-        state["note"] = send(note, note_c, at["nc_s"].at[0], at["nc_r"].at[0], place.peer_c())
+        state["note"] = send(note, note_c, nc_s.at[0], nc_r.at[0], place.peer_c())
 
     def note_cross():
         state["note"].wait_recv()
         note_c[...] = note_c[...] + note[...]
-        state["note"] = send(note_c, note_x, at["nx_s"].at[0], at["nx_r"].at[0], place.peer_x())
+        state["note"] = send(note_c, note_x, nx_s.at[0], nx_r.at[0], place.peer_x())
 
     def note_out():
         state["note"].wait_recv()
@@ -349,7 +350,7 @@
         summed = note_x
         if ways > 1:
             crossed = [
-                send(note_x, note_w.at[k], at["nw_s"].at[k], at["nw_r"].at[k], device)
+                send(note_x, note_w.at[k], nw_s.at[k], nw_r.at[k], device)
                 for k, device in enumerate(place.peers_w())
             ]
             for copy in crossed:
@@ -363,23 +364,23 @@
             summed = note_c
         for k in range(1, HEADS):
             h2 = (h + k) % HEADS
-            send(summed.at[h2], note_h.at[h], at["nh_s"].at[k], at["nh_r"].at[h], place.device(h=h2))
+            send(summed.at[h2], note_h.at[h], nh_s.at[k], nh_r.at[h], place.device(h=h2))
         state["summed"] = summed
 
     def note_sum():
         bias = state["summed"][h]
         for k in range(1, HEADS):
             hs = (h - k) % HEADS
-            remote(note_h.at[hs], note_h.at[hs], at["nh_s"].at[k], at["nh_r"].at[hs], place.peer_x()).wait_recv()
+            remote(note_h.at[hs], note_h.at[hs], nh_s.at[k], nh_r.at[hs], place.peer_x()).wait_recv()
             bias = bias + note_h[hs]
         note_h[h] = bias
-        save(note_h.at[h], at["note_out"])
+        save(note_h.at[h], note_ref)
 
     def turn_tables():
         trig_kept.wait()
         for k in range(1, HEADS):
             hs = (h - k) % HEADS
-            remote(trig.at[hs], trig.at[hs], at["t_s"].at[k], at["t_r"].at[hs], place.peer_x()).wait_recv()
+            remote(trig.at[hs], trig.at[hs], t_s.at[k], t_r.at[hs], place.peer_x()).wait_recv()
         lane = lax.broadcasted_iota(jnp.int32, (STRIPE, 128), 1)
         for hh in range(HEADS):
             @pl.loop(0, runs)
@@ -401,11 +402,11 @@
     flipped = []
 
     def flip(src, dst, t):
-        spot = at["flat"].at[len(flipped) % 2]
+        spot = flat.at[len(flipped) % 2]
         if len(flipped) >= 2:
             flipped[-2].wait()
         spot[...] = src[..., t * 256 : (t + 1) * 256].reshape(runs * per_run, 256).T
-        copy = pltpu.make_async_copy(spot, dst.at[t * 256 : (t + 1) * 256], at["flat_sem"].at[len(flipped) % 2])
+        copy = pltpu.make_async_copy(spot, dst.at[t * 256 : (t + 1) * 256], flat_sem.at[len(flipped) % 2])
         copy.start()
         flipped.append(copy)
 
@@ -428,7 +429,7 @@
     step(27, n_far)
     step(36.1, w_first, expand_at, 0)
     step(52, n_last)
-    step(52.1, w_first, expand_at, 1)
+    step(41, w_first, expand_at, 1)
     step(52.2, w_first, dense_at, 1)
     step(52.3, w_first, dense_at, 0)
     step(52.4, g_first_z)
@@ -436,28 +437,24 @@
     step(55, turn_tables)
     step(57, note_sum)
     step(65, rows_done, n_side, v_n, n_out)
-    step(75.5, w_across, expand_at)
+    step(64.9, w_across, expand_at)
     step(86, w_across, dense_at)
     step(86.1, g_near)
-    step(98, g_far)
+    step(95, g_far)
     for g in shrink:
-        step(98.1, w_first, g, 1)
-        step(98.2, w_first, g, 0)
-    step(112, w_beside, expand_at)
-    step(113, w_ready, expand_at)
-    step(117.7, g_last)
-    step(121.5, w_beside, dense_at)
+        step(95.1, w_first, g, 1)
+        step(95.2, w_first, g, 0)
+    step(96, w_beside, expand_at)
+    step(97, w_ready, expand_at)
+    step(118.5, g_last)
+    step(127.5, w_beside, dense_at)
     step(134, rows_done, g_side, v_g, g_out)
     step(134.1, w_ready, dense_at)
     for k, g in enumerate(shrink):
-        step((117.6, 117.72, 117.83, 117.95)[k], w_across, g)
-        step((135.6, 142, 147, 152)[k], w_beside, g)
+        step((128, 130, 132, 138.5)[k], w_across, g)
+        step((141, 145, 149, 152)[k], w_beside, g)
         step(156, w_ready, g)
     if fuse:
-        v_q, v_do, v_kv, v_slope, v_left, v_right, v_out, lse, s_ref, sum_ref, kv_c, kv_x, o_p, o_y = (
-            at[k] for k in ["v_q", "v_do", "v_kv", "v_slope", "v_left", "v_right", "v_out", "lse", "s_ref", "sum_ref", "kv_c", "kv_x", "o_p", "o_y"]
-        )
-        kx_s, kx_r, kc_s, kc_r = (at[k] for k in ["kx_s", "kx_r", "kc_s", "kc_r"])
         kv_sends = []
         tile = 256
 
@@ -516,10 +513,9 @@
             first = 3 * HEAD_DIM + t * tile
             v_right[m * half : (m + 1) * half, first : first + tile] = value.astype(BF)
 
-        row_tok, col_tok = at["row_tok"], at["col_tok"]
 
         def token_tables():
-            tokens = at["tokens"][...]
+            tokens = token_ref[...]
             starts = [
                 jnp.min(jnp.where(tokens // run_size == k, tokens, far_off), 1, keepdims=True) for k in range(runs)
             ]
@@ -587,7 +583,7 @@
             v_kv[...] = sum_ref[...].astype(BF).reshape(v_kv.shape)
             for k, xx in ((0, 1 - x), (1, x)):
                 state["fold", k] = send(
-                    v_kv.at[:, xx * 2 + 1 - c], kv_c.at[:, k], at["fc_s"].at[k], at["fc_r"].at[k], place.peer_c()
+                    v_kv.at[:, xx * 2 + 1 - c], kv_c.at[:, k], fc_s.at[k], fc_r.at[k], place.peer_c()
                 )
 
         def fold_add(k, final):
@@ -608,12 +604,12 @@
 
         def fold_cross():
             fold_add(0, False)
-            state["fold_x"] = send(kv_c.at[:, 0], kv_x, at["fx_s"].at[0], at["fx_r"].at[0], place.peer_x())
+            state["fold_x"] = send(kv_c.at[:, 0], kv_x, fx_s.at[0], fx_r.at[0], place.peer_x())
 
         def fold_close():
             state["fold_x"].wait_recv()
             fold_add(1, True)
-            save(v_right.at[:, pl.ds(0, 3 * HEAD_DIM)], at["right_out"].at[:, pl.ds(0, 3 * HEAD_DIM)])
+            save(v_right.at[:, pl.ds(0, 3 * HEAD_DIM)], right_out.at[:, pl.ds(0, 3 * HEAD_DIM)])
 
         chunks, early, wide = o_p.shape[0], o_y.shape[0], o_p.shape[-1]
 
@@ -629,10 +625,10 @@
                 o_p[q, :, :, :, :, :, k * tile : (k + 1) * tile] = value.astype(BF).reshape(runs, 2, 2, 2, STRIPE, tile)
             if q < early:
                 state["out", q] = send(
-                    o_p.at[q, :, :, :, 1 - place.hy], o_y.at[q], at["oy_s"].at[q], at["oy_r"].at[q], place.peer_y()
+                    o_p.at[q, :, :, :, 1 - place.hy], o_y.at[q], oy_s.at[q], oy_r.at[q], place.peer_y()
                 )
             else:
-                save(o_p.at[q], at["part_out"].at[q - early])
+                save(o_p.at[q], part_out.at[q - early])
 
         def out_side(q):
             state["out", q].wait_recv()
@@ -643,21 +639,21 @@
                     value = o_y[q, run, t // 2, t % 2].astype(F32) + o_p[q, run, t // 2, t % 2, place.hy].astype(F32)
                     o_y[q, run, t // 2, t % 2] = value.astype(BF)
 
-            save(o_y.at[q], at["half_out"].at[q])
+            save(o_y.at[q], half_out.at[q])
 
         for p in range(parts):
             step(67 + 2 * p, project, p)
-            step(80.5 + 6 * p, kv_beside, p)
-            step(101, kv_ready, p)
+            step(108.5 + 2 * p, kv_beside, p)
+            step(118, kv_ready, p)
         for i in range(runs):
-            step(105.5 + 1.2 * i, attend, i)
+            step(119 + i, attend, i)
             step(135 + 2 * i, attend_back, i)
             step(75, flip, v_n, n_out, i)
             step(163, flip, v_g, g_out, i)
         count = v_slope.shape[1] // tile
         for t in range(count):
             for m in range(2):
-                step(117.51 + 0.1 * t + 0.05 * m, expand, m, t)
+                step(97.51 + 0.1 * t + 0.05 * m, expand, m, t)
                 step(161 + 0.1 * t, shrink_back, m, t)
         step(134.5, attended_back)
         step(151.5, fold_first)
@@ -666,8 +662,8 @@
             step(156.5 + 0.1 * q if q < early else 162, out_part, q)
         for q in range(early):
             step(172 + 12 * q, out_side, q)
-        step(157, save, v_left, at["left_out"])
-        step(161.9, save, v_right.at[:, pl.ds(3 * HEAD_DIM, v_slope.shape[1])], at["right_out"].at[:, pl.ds(3 * HEAD_DIM, v_slope.shape[1])])
+        step(157, save, v_left, left_out)
+        step(161.9, save, v_right.at[:, pl.ds(3 * HEAD_DIM, v_slope.shape[1])], right_out.at[:, pl.ds(3 * HEAD_DIM, v_slope.shape[1])])
         step(183, fold_close)
     for _, _, body, given in sorted(plan, key=lambda one: one[:2]):
         body(*given)
@@ -1156,10 +1152,10 @@
             if A_ORDER[i - 1] < half:
                 step(time, b_cross, A_ORDER[i - 1])
     step(47.5, b_mine, A_ORDER[-1])
-    for n, times in zip(range(half, count), ((22, 74), (35.5, 79), (49.5, 84), (63, 88)), strict=True):
+    for n, times in zip(range(half, count), ((22, 77.5), (35.5, 79), (60, 84), (67, 88)), strict=True):
         step(times[0], a_close, n)
         step(times[1], b_close, n)
-    for q, times in enumerate(((48, 66, 80), (59, 77, 92), (71, 89, 104), (83, 101, 114))):
+    for q, times in enumerate(((48, 66, 80), (49.2, 78, 92), (62, 89, 104), (76, 101, 114))):
         step(times[0], advance, "e", e_after_y, q)
         step(times[1], advance, "e", e_after_1, q)
         step(times[2], advance, "e", e_after_2, q)

time: 358 us -> 353 us (0.986)
  Pallas kernels: 354 us -> 346 us
    pallas_call x1, Pallas kernels: 202 us -> 197 us  [open_all(): pl.pallas_call(functools.partial(open_kernel, ways, tuple(cuts), fuse, pr...]
where the time goes in v6:
time: 353 us; the launch traced here: 347 us
  Pallas kernels  346 us (98%)
    pallas_call x1, Pallas kernels, open_all(): pl.pallas_call(functools.partial(open_kernel, ways, tuple(cuts), fuse, pr...  197 us
    pallas_call x1, Pallas kernels, finish(): pl.pallas_call(functools.partial(finish_kernel, ways, early), out_shape=s...  140 us
    pallas_call x1, Pallas kernels, close(): pl.pallas_call(close_kernel, out_shape=outs, in_specs=[VMEM] * 7 + [ANY]...  8.17 us

profile of v6, /device:TPU:8, one launch (start us, length us, event | category | flops | bytes accessed | tf_op | source)
XLA Modules:
  0.0 346.8 jit_solution(12546902418011745265)
XLA Ops:
  0.6 197.3 %shard_map.289 = (bf16[2048,1024]{1,0:T(8,128)(2,1)}, bf16[2048,1024]{1,0:T(8,128)(2,1)}, bf16[2,1,8,2,64,1792]{5,4,3,2,1,0:T(8,128)(2,1)}, f32[32,128]{1,0:T(8,...) custom-call(bf16[128,2048]{1,0:T(8,128)(2,1)} %refs_0_.3, ...), custom_call_target="tpu_custom_call" | custom-call | tf_op jit(solution)/shard_map/pallas_call | solution.py:747
  197.9 140.5 %shard_map.290 = (f32[8,16,2048]{2,1,0:T(8,128)}, f32[8,16,2048]{2,1,0:T(8,128)}, bf16[8,64,2304]{2,1,0:T(8,128)(2,1)}, bf16[8,64,768]{2,1,0:T(8,128)(2,1)}, f32[8,32,128]{2,1,0:T(8,128)}) custom-call(bf16[8,4,2,16,1280]{4,3,2,1,0:T(8,128)(2,1)} %bitcast.16, bf16[8,4,2,16,1792]{4,3,2,1,0:T(8,128)(2,1)} %bitcast.15, bf16[2048,1792]{1,0:T(8,128)(2,1)} %bitcast.14, ...), custom_call_target="tpu_custom_call" | custom-call | tf_op jit(solution)/shard_map/pallas_call | solution.py:1246
  338.4 8.2 %shard_map.291 = (bf16[128,2048]{1,0:T(8,128)(2,1)}, bf16[128,2048]{1,0:T(8,128)(2,1)}, f32[1,64]{1,0:T(1,128)}, f32[1,64]{1,0:T(1,128)}, f32[1,64]{1,0:T(1,128)...) custom-call(s32[32,128]{1,0:T(8,128)} %bitcast.18, ...), custom_call_target="tpu_custom_call" | custom-call | tf_op jit(solution)/shard_map/pallas_call | solution.py:1387
